TPU v7x, 256 devices: a whole 4x4x8 slice. The times are simulated.
256 devices in a mesh: dp: 16 (over z, core), expert: 16 (over y, x).
Axes of the slice: x: 4, y: 4, z: 8, core: 2. Of those that a mesh axis runs over, the one named last changes fastest.
Arguments:
- tokens: bfloat16 [32768, 2048], P(('dp', 'expert')), may hold values from -24 to 24
- out_grad: bfloat16 [32768, 2048], P(('dp', 'expert')), may hold values from -6 to 6
- gates: bfloat16 [32768, 4], P(('dp', 'expert')), may hold values from 0.099609375 to 1
- expert_ids: int32 [32768, 4], P(('dp', 'expert')), may hold values from 0 to 15, all different within a row; in each aligned block of 128 rows (0 to 127, 128 to 255, ...) at most 40 rows name the same one
- w_gate: bfloat16 [16, 2048, 768], P('expert'), may hold values from -0.125 to 0.125
- w_up: bfloat16 [16, 2048, 768], P('expert'), may hold values from -0.125 to 0.125
- w_down: bfloat16 [16, 768, 2048], P('expert'), may hold values from -0.21875 to 0.21875
Outputs:
- token_grad: bfloat16 [32768, 2048], P(('dp', 'expert'))
- gate_grad: bfloat16 [32768, 4], P(('dp', 'expert'))
- grad_gate: bfloat16 [16, 2048, 768], P('expert', 'dp')
- grad_up: bfloat16 [16, 2048, 768], P('expert', 'dp')
- grad_down: bfloat16 [16, 768, 2048], P('expert', 'dp')
Inputs may be any that keep to these rules, and one draw needn't show every extreme that they name: `expert_ids`: in each aligned block of 128 rows (one device's tokens) no expert is named by more than 40 rows, a bound that some block reaches; a row names 4 different experts.
All inputs are finite; a program needn't handle non-finite values.
Results may differ from a plain program's by a relative error of at most 0.023.
Values may be sent and summed in bfloat16 or wider, within the bound.
No kernel may reach another device: no remote copies, remote signals or barrier semaphores. Data moves between devices by JAX's collectives and lax.ppermute only.
A program may use at most 128 MiB of HBM per device.

v0:
```python
import jax
import jax.numpy as jnp
from jax import lax
from jax.experimental import pallas as pl
from jax.experimental.pallas import tpu as pltpu
from jax.sharding import PartitionSpec as P

F32 = jnp.float32
BF16 = jnp.bfloat16
N_TOK = 128
D = 2048
FF = 768
CAP = 40
N_EXP = 16
ROWS = N_EXP * CAP
N_Z = 8
EXTRA = 128
CHUNK = 160
FULL = 64
MID = 26
H = D // 2
Q = D // 4


def params(mib=FULL):
    return pltpu.CompilerParams(vmem_limit_bytes=mib * 1024 * 1024)


def cost(flops, nbytes):
    return pl.CostEstimate(flops=int(flops), bytes_accessed=int(nbytes), transcendentals=0)


def dot(a, b, ca=1, cb=0):
    return lax.dot_general(a, b, (((ca,), (cb,)), ((), ())), preferred_element_type=F32)


def slot_matrix(ids_t, gates_t=None):
    expert = lax.broadcasted_iota(jnp.int32, (N_EXP, N_TOK), 0)
    member = jnp.zeros((N_EXP, N_TOK), F32)
    weight = jnp.zeros((N_EXP, N_TOK), F32)
    for k in range(4):
        hit = ids_t[k : k + 1, :] == expert
        member = jnp.where(hit, 1.0, member)
        if gates_t is not None:
            weight = jnp.where(hit, gates_t[k : k + 1, :].astype(F32), weight)
    row = lax.broadcasted_iota(jnp.int32, (N_TOK, N_TOK), 0)
    col = lax.broadcasted_iota(jnp.int32, (N_TOK, N_TOK), 1)
    before = jnp.where(row < col, 1.0, 0.0).astype(BF16)
    position = dot(member.astype(BF16), before)
    code = jnp.where(member > 0.0, position, -1.0)
    slot = lax.broadcasted_iota(jnp.int32, (CAP, N_TOK), 0).astype(F32)
    pieces = []
    for e in range(N_EXP):
        value = 1.0 if gates_t is None else weight[e : e + 1, :]
        pieces.append(jnp.where(code[e : e + 1, :] == slot, value, 0.0))
    return jnp.concatenate(pieces, axis=0).astype(BF16)


ANY = pl.BlockSpec(memory_space=pl.ANY)
SMEM = pl.BlockSpec(memory_space=pltpu.SMEM)


def shape(*dims):
    return jax.ShapeDtypeStruct(dims, BF16)


def vmem(*dims, dtype=BF16):
    return pltpu.VMEM(dims, dtype)


def start(sems, at, source, target):
    copy = pltpu.make_async_copy(source, target, sems.at[at])
    copy.start()
    return copy


def wait(copies):
    for copy in copies:
        copy.wait()


def dispatch_kernel(core_ref, ids_hbm, gates_hbm, x_hbm, out_hbm, ids, gates, x, slots, out, sems, out_sems):
    few = [start(sems, 0, ids_hbm, ids)]
    if gates_hbm is None:
        loads = [start(sems, 2, x_hbm, x)]
    else:
        few.append(start(sems, 1, gates_hbm, gates))
        core = core_ref[0]
        own = pl.ds(pl.multiple_of(core * H, H), H)
        other = pl.ds(pl.multiple_of((1 - core) * H, H), H)
        loads = [
            start(sems, 2, x_hbm.at[:, own], x.at[:, pl.ds(0, H)]),
            start(sems, 3, x_hbm.at[:, other], x.at[:, pl.ds(H, H)]),
        ]
    wait(few)
    slots[...] = slot_matrix(ids[...], None if gates_hbm is None else gates[...])
    wait(loads)
    stores = []
    for i in range(ROWS // CHUNK):
        part = slice(i * CHUNK, (i + 1) * CHUNK)
        out[part, :] = dot(slots[part, :], x[...]).astype(BF16)
        stores.append(start(out_sems, i, out.at[part, :], out_hbm.at[part, :]))
    wait(stores)


def plain_kernel(core_ref, ids_hbm, x_hbm, *refs):
    dispatch_kernel(core_ref, ids_hbm, None, x_hbm, *refs)


def dispatch(core, ids_t, gates_t, x):
    plain = gates_t is None
    args = [core, ids_t] + ([] if plain else [gates_t]) + [x]
    return pl.pallas_call(
        plain_kernel if plain else dispatch_kernel,
        in_specs=[SMEM] + [ANY] * (len(args) - 1),
        out_specs=ANY,
        out_shape=shape(ROWS, D),
        scratch_shapes=[
            vmem(4, N_TOK, dtype=jnp.int32),
            vmem(4, N_TOK),
            vmem(N_TOK, D),
            vmem(ROWS, N_TOK),
            vmem(ROWS, D),
            pltpu.SemaphoreType.DMA((4,)),
            pltpu.SemaphoreType.DMA((ROWS // CHUNK,)),
        ],
        compiler_params=params(),
        cost_estimate=cost(2 * ROWS * N_TOK * D, 2 * ROWS * D),
    )(*args)


def down_turn_kernel(core_ref, w_ref, out_ref):
    out_ref[0] = w_ref[0].T


def turn_down(core, w):
    return pl.pallas_call(
        down_turn_kernel,
        grid_spec=pltpu.PrefetchScalarGridSpec(
            num_scalar_prefetch=1,
            grid=(3, 2),
            in_specs=[pl.BlockSpec((1, 256, H), lambda n, i, c: (0, n, i + c[0] - 2 * i * c[0]))],
            out_specs=pl.BlockSpec((1, H, 256), lambda n, i, c: (n, i, 0)),
        ),
        out_shape=shape(3, D, 256),
        compiler_params=params(),
        cost_estimate=cost(0, 4 * D * FF),
    )(core, w)


def up_turn_kernel(g_ref, u_ref, gt_ref, ut_ref):
    gt_ref[0] = g_ref[0].T
    ut_ref[0] = u_ref[0].T


def turn_up(wg, wu):
    weight = pl.BlockSpec((1, Q, FF), lambda n: (0, n, 0))
    out = pl.BlockSpec((1, FF, Q), lambda n: (n, 0, 0))
    turned = jax.ShapeDtypeStruct((4, FF, Q), BF16)
    return pl.pallas_call(
        up_turn_kernel,
        grid=(4,),
        in_specs=[weight, weight],
        out_specs=[out, out],
        out_shape=[turned, turned],
        compiler_params=params(),
        cost_estimate=cost(0, 8 * D * FF),
    )(wg, wu)


def forward_kernel(x_ref, wg_ref, wu_ref, ht_ref, h_ref, f_ref, a_ref):
    x = x_ref[...]
    g = dot(x, wg_ref[0])
    u = dot(x, wu_ref[0])
    s = jax.nn.sigmoid(g)
    a = g * s
    h = (a * u).astype(BF16)
    h_ref[0] = h
    ht_ref[...] = h.T
    a_ref[0] = a.astype(BF16)
    f_ref[0] = (u * s * (1.0 + g * (1.0 - s))).astype(BF16)


def forward(x, wg, wu):
    weight = pl.BlockSpec((1, D, 256), lambda n: (0, 0, n))
    out = pl.BlockSpec((1, ROWS, 256), lambda n: (n, 0, 0))
    return pl.pallas_call(
        forward_kernel,
        grid=(3,),
        in_specs=[pl.BlockSpec((ROWS, D), lambda n: (0, 0)), weight, weight],
        out_specs=[pl.BlockSpec((256, ROWS), lambda n: (n, 0)), out, out, out],
        out_shape=[shape(FF, ROWS)] + [shape(3, ROWS, 256)] * 3,
        compiler_params=params(MID),
        cost_estimate=cost(4 * ROWS * D * FF, 13_000_000),
    )(x, wg, wu)


def split_kernel(core_ref, mine_ref, theirs_ref, own_ref, other_ref):
    own_ref[...] = mine_ref[...].T
    other_ref[...] = theirs_ref[...].T


def split_transposed(core, first):
    out = pl.BlockSpec((128, ROWS), lambda n, c: (n, 0))
    return pl.pallas_call(
        split_kernel,
        grid_spec=pltpu.PrefetchScalarGridSpec(
            num_scalar_prefetch=1,
            grid=(N_Z,),
            in_specs=[
                pl.BlockSpec((ROWS, 128), lambda n, c: (0, 2 * n + c[0])),
                pl.BlockSpec((ROWS, 128), lambda n, c: (0, 2 * n + 1 - c[0])),
            ],
            out_specs=[out, out],
        ),
        out_shape=[shape(H, ROWS), shape(H, ROWS)],
        compiler_params=params(MID),
        cost_estimate=cost(0, 4 * ROWS * D),
    )(core, first, first)


def backward_kernel(me_ref, dy_ref, wd_ref, h_ref, f_ref, a_ref, dg_ref, du_ref, gg_ref, total):
    n = pl.program_id(0)
    b = dot(dy_ref[...], wd_ref[0])
    dg_ref[...] = (b * f_ref[0].astype(F32)).astype(BF16)
    du_ref[...] = (b * a_ref[0].astype(F32)).astype(BF16)
    part = jnp.sum(b * h_ref[0].astype(F32), axis=1, keepdims=True)
    part = jnp.broadcast_to(part, (ROWS, EXTRA))

    @pl.when(n == 0)
    def _():
        total[...] = part

    @pl.when(n > 0)
    def _():
        total[...] += part

    @pl.when(n == pl.num_programs(0) - 1)
    def _():
        value = total[...]
        high = value.astype(BF16).astype(F32)
        col = lax.broadcasted_iota(jnp.int32, (ROWS, EXTRA), 1)
        me = me_ref[0]
        low = jnp.where(col == me + N_EXP, value - high, 0.0)
        gg_ref[...] = jnp.where(col == me, high, low).astype(BF16)


def backward(me, dy, wd_t, h, f, a):
    block = pl.BlockSpec((1, ROWS, 256), lambda n: (n, 0, 0))
    part = pl.BlockSpec((ROWS, 256), lambda n: (0, n))
    return pl.pallas_call(
        backward_kernel,
        grid=(3,),
        in_specs=[
            SMEM,
            pl.BlockSpec((ROWS, D), lambda n: (0, 0)),
            pl.BlockSpec((1, D, 256), lambda n: (n, 0, 0)),
            block,
            block,
            block,
        ],
        out_specs=[part, part, pl.BlockSpec((ROWS, EXTRA), lambda n: (0, 0))],
        out_shape=[shape(ROWS, FF), shape(ROWS, FF), shape(ROWS, EXTRA)],
        scratch_shapes=[vmem(ROWS, EXTRA, dtype=F32)],
        compiler_params=params(),
        cost_estimate=cost(2 * ROWS * D * FF, 11_000_000),
    )(me, dy, wd_t, h, f, a)


def pair_kernel(*refs):
    dg_ref, du_ref, wg_ref, wu_ref, gg_ref, _, _, _, _, out_ref, flag_ref = refs
    n = pl.program_id(0)
    value = dot(dg_ref[...], wg_ref[0]) + dot(du_ref[...], wu_ref[0])
    out_ref[:, pl.ds(pl.multiple_of(n * Q, Q), Q)] = value.astype(BF16)
    flag_ref[...] = jnp.zeros_like(flag_ref)

    @pl.when(n == 0)
    def _():
        out_ref[:, D:] = gg_ref[...]


def pair_grads(half, dg, du, wg_t, wu_t, gg, pairs, after):
    size = ROWS // 2
    part = pl.BlockSpec((size, FF), lambda n: (half, 0))
    weight = pl.BlockSpec((1, FF, Q), lambda n: (n, 0, 0))
    return pl.pallas_call(
        pair_kernel,
        grid=(4,),
        in_specs=[part, part, weight, weight, pl.BlockSpec((size, EXTRA), lambda n: (half, 0))] + [ANY] * 4,
        out_specs=[
            pl.BlockSpec((size, D + EXTRA), lambda n: (half, 0)),
            pl.BlockSpec((16, 128), lambda n: (0, 0)),
        ],
        out_shape=[shape(ROWS, D + EXTRA), shape(16, 128)],
        input_output_aliases={5: 0} if half else {},
        compiler_params=params(MID),
        cost_estimate=cost(2 * ROWS * D * FF, 9_000_000),
    )(dg, du, wg_t, wu_t, gg, pairs, *after)


def outer_kernel(at_ref, bt_ref, a_ref, b_ref, after_ref, out_ref, flag_ref):
    value = dot(at_ref[...], a_ref[...]) + dot(bt_ref[...], b_ref[...])
    out_ref[...] = value.astype(BF16)
    flag_ref[...] = jnp.zeros_like(flag_ref)


def outer_sum(own_t, other_t, own, other, other_at, n, after):
    m, width = own_t.shape[0], 256
    left = pl.BlockSpec((m, ROWS), lambda j: (0, 0))
    return pl.pallas_call(
        outer_kernel,
        grid=(n // width,),
        in_specs=[
            left,
            left,
            pl.BlockSpec((ROWS, width), lambda j: (0, j)),
            pl.BlockSpec((ROWS, width), lambda j: (0, j + other_at // width)),
            ANY,
        ],
        out_specs=[
            pl.BlockSpec((m, width), lambda j: (0, j)),
            pl.BlockSpec((16, 128), lambda j: (0, 0)),
        ],
        out_shape=[shape(m, n), shape(16, 128)],
        compiler_params=params(MID),
        cost_estimate=cost(4 * ROWS * m * n, 2 * (m * n + 2 * ROWS * (m + n))),
    )(own_t, other_t, own, other, after)


def combine_kernel(ids_hbm, gates_hbm, rows_hbm, tok_hbm, gate_hbm, ids, gates, rows, extra, tok, gate, sems, out_sems):
    few = [start(sems, 0, ids_hbm, ids), start(sems, 1, gates_hbm, gates)]
    extra_load = start(sems, 2, rows_hbm.at[:, pl.ds(D, EXTRA)], extra)
    loads = [start(sems, 3 + n, rows_hbm.at[:, pl.ds(n * Q, Q)], rows.at[n]) for n in range(4)]
    wait(few)
    slots = slot_matrix(ids[...])
    stores = []
    for n in range(4):
        loads[n].wait()
        tok[:, n * Q : (n + 1) * Q] = dot(slots, rows[n], 0, 0).astype(BF16)
    stores.append(start(out_sems, 0, tok, tok_hbm))
    extra_load.wait()
    by_expert = dot(extra[...], slots, 0, 0)
    value = by_expert[:N_EXP] + by_expert[N_EXP : 2 * N_EXP]
    expert_at = lax.broadcasted_iota(jnp.int32, (N_EXP, N_TOK), 0)
    choice = lax.broadcasted_iota(jnp.int32, (4, N_TOK), 0)
    grads = jnp.zeros((4, N_TOK), F32)
    for k in range(4):
        mine = jnp.where(ids[k : k + 1, :] == expert_at, value, 0.0)
        grads = jnp.where(choice == k, jnp.sum(mine, axis=0, keepdims=True), grads)
    gate[...] = (grads / gates[...].astype(F32)).astype(BF16)
    stores.append(start(out_sems, 1, gate, gate_hbm))
    wait(stores)


def combine(ids_t, gates_t, rows):
    return pl.pallas_call(
        combine_kernel,
        in_specs=[ANY] * 3,
        out_specs=[ANY] * 2,
        out_shape=[shape(N_TOK, D), shape(4, N_TOK)],
        scratch_shapes=[
            vmem(4, N_TOK, dtype=jnp.int32),
            vmem(4, N_TOK),
            vmem(4, ROWS, Q),
            vmem(ROWS, EXTRA),
            vmem(N_TOK, D),
            vmem(4, N_TOK),
            pltpu.SemaphoreType.DMA((7,)),
            pltpu.SemaphoreType.DMA((2,)),
        ],
        compiler_params=params(16),
        cost_estimate=cost(2 * ROWS * N_TOK * D, 2 * ROWS * D),
    )(ids_t, gates_t, rows)


def exchange_experts(rows):
    width = rows.shape[1]
    moved = lax.all_to_all(
        rows.reshape(N_EXP, CAP, width), "expert", split_axis=0, concat_axis=0, tiled=True
    )
    return moved.reshape(ROWS, width)


def hold_kernel(*refs):
    pass


def hold(a, *after, mib=1):
    place = pl.BlockSpec(memory_space=pl.ANY)
    return pl.pallas_call(
        hold_kernel,
        in_specs=[place] * (1 + len(after)),
        out_specs=place,
        out_shape=jax.ShapeDtypeStruct(a.shape, a.dtype),
        input_output_aliases={0: 0},
        compiler_params=params(mib),
    )(a, *after)


def swap_cores(a):
    return lax.ppermute(a, "dp", [(i, i ^ 1) for i in range(2 * N_Z)])


def pick(a, index):
    return lax.dynamic_index_in_dim(a, index, 0, keepdims=False)


ROUTE = tuple((2 * i, 2 * ((i + 1) % N_Z)) for i in range(N_Z)) + tuple(
    (2 * i + 1, 2 * ((i - 1) % N_Z) + 1) for i in range(N_Z)
)


def ring_step(g, held, z, sign, step, after=None):
    if step == 1:
        held = pick(g, (z - sign) & (N_Z - 1))
    came = lax.ppermute(held, "dp", ROUTE)
    if after is not None:
        came = hold(came, after)
    block = pick(g, (z - (step + 1) * sign) & (N_Z - 1))
    return (came.astype(F32) + block.astype(F32)).astype(BF16)


def body(tokens, out_grad, gates, expert_ids, w_gate, w_up, w_down):
    dp = lax.axis_index("dp").astype(jnp.int32)
    z, core = dp >> 1, dp & 1
    sign = 1 - 2 * core
    core_arg = core.reshape(1)
    me = lax.axis_index("expert").astype(jnp.int32).reshape(1)
    ids_t, gates_t = expert_ids.T, gates.T

    down_t = turn_down(core_arg, w_down)
    gate_t, up_t = turn_up(w_gate, w_up)
    x = exchange_experts(dispatch(core_arg, ids_t, None, tokens))
    dy_rows = hold(dispatch(core_arg, ids_t, gates_t, out_grad), x, down_t, up_t, mib=FULL)
    dy = exchange_experts(dy_rows)

    hidden_t, hidden, factor, active = forward(x, w_gate, w_up)
    hidden_other_t = swap_cores(hidden_t)
    x_own, x_theirs = split_transposed(core_arg, x)
    x_other = swap_cores(x_theirs)

    dy = hold(dy, x_other, hidden_other_t, mib=FULL)
    dy_other = swap_cores(dy)
    d_gate, d_up, prob = backward(me, dy, down_t, hidden, factor, active)
    d_gate_other, d_up_other = swap_cores(d_gate), swap_cores(d_up)
    part_down, flag = outer_sum(hidden_t, hidden_other_t, dy, dy_other, H, H, prob)
    part_gate, flag = outer_sum(x_own, x_other, d_gate, d_gate_other, 0, FF, flag)
    part_up, flag = outer_sum(x_own, x_other, d_up, d_up_other, 0, FF, flag)

    part_down = part_down.reshape(N_Z, FF // N_Z, H)
    part_gate = part_gate.reshape(N_Z, D // (2 * N_Z), FF)
    part_up = part_up.reshape(N_Z, D // (2 * N_Z), FF)
    sum_down = ring_step(part_down, None, z, sign, 1)
    sum_gate = ring_step(part_gate, None, z, sign, 1)
    sum_up = ring_step(part_up, None, z, sign, 1)

    pairs, first_flag = pair_grads(0, d_gate, d_up, gate_t, up_t, prob, flag, (flag, flag, flag))
    pairs, flag = pair_grads(1, d_gate, d_up, gate_t, up_t, prob, pairs, (sum_down, sum_gate, sum_up))
    back_rows = exchange_experts(pairs)
    token_grad, gate_grad_t = combine(ids_t, gates_t, back_rows)

    sum_down = hold(sum_down, first_flag)
    for step in range(2, N_Z):
        sum_down = ring_step(part_down, sum_down, z, sign, step)
        sum_gate = ring_step(part_gate, sum_gate, z, sign, step)
        sum_up = ring_step(part_up, sum_up, z, sign, step, gate_grad_t if step == 6 else None)

    halves = sum_down.reshape(2, FF // (2 * N_Z), H)
    mine = pick(halves, core)
    theirs = swap_cores(pick(halves, 1 - core))
    left = jnp.where(core == 0, mine, theirs)
    right = jnp.where(core == 0, theirs, mine)
    grad_down = jnp.concatenate([left, right], axis=1)
    return token_grad, gate_grad_t.T, sum_gate[None], sum_up[None], grad_down[None]


def solution(mesh):
    both = P(("dp", "expert"), None)
    weight = P("expert", None, None)
    grad = P("expert", "dp", None)
    return jax.shard_map(
        body,
        mesh=mesh,
        in_specs=(both, both, both, both, weight, weight, weight),
        out_specs=(both, both, grad, grad, grad),
        check_vma=False,
    )
```

profile of v0, /device:TPU:2, one launch (start us, length us, event | category | flops | bytes accessed | tf_op | source)
XLA Modules:
  0.0 201.5 jit_solution(8242803395070406427)
XLA Ops:
  0.6 2.9 %shard_map.111 = bf16[640,2048]{1,0:T(8,128)(2,1)} custom-call(s32[1]{0:T(128)} %bitcast.3.core_ref, s32[4,128]{1,0:T(4,128)} %bitcast.120, bf16[128,2048]{1,0:T(8,128)(2,1)} %x_hbm.3), custom_call_target="tpu_custom_call" | custom-call | flops 335544320 | bytes 2621440 | tf_op jit(solution)/shard_map/pallas_call | solution.py:113
  3.6 7.5 %all-to-all-start = ((bf16[16,40,2048]{2,1,0:T(8,128)(2,1)}), bf16[16,40,2048]{2,1,0:T(8,128)(2,1)}, u32[]{:S(2)}, u32[]{:S(2)}) async-start(bf16[16,40,2048]{2,1,0:T(8,128)(2,1)} %bitcast.127), calls=%async_computation | async-start | bytes 5242880 | tf_op jit(solution)/shard_map/all_to_all | solution.py:378
  11.1 5.8 %shard_map.112.refs_2_.wd_ref = bf16[3,2048,256]{2,1,0:T(8,128)(2,1)} custom-call(s32[1]{0:T(128)} %bitcast.3.core_ref, bf16[1,768,2048]{2,1,0:T(8,128)(2,1)} %w_ref.1), custom_call_target="tpu_custom_call" | custom-call | bytes 6291456 | tf_op jit(solution)/shard_map/pallas_call | solution.py:137
  16.8 6.1 %shard_map.113 = (bf16[4,768,512]{2,1,0:T(8,128)(2,1)}, bf16[4,768,512]{2,1,0:T(8,128)(2,1)}) custom-call(bf16[1,2048,768]{2,1,0:T(8,128)(2,1)} %wg_ref.1, bf16[1,2048,768]{2,1,0:T(8,128)(2,1)} %wu_ref.1), custom_call_target="tpu_custom_call" | custom-call | bytes 12582912 | tf_op jit(solution)/shard_map/pallas_call | solution.py:160
  22.9 2.9 %shard_map.110.refs_0_ = bf16[640,2048]{1,0:T(8,128)(2,1)} custom-call(s32[1]{0:T(128)} %bitcast.3.core_ref, s32[4,128]{1,0:T(4,128)} %bitcast.121, bf16[4,128]{1,0:T(4,128)(2,1)} %bitcast.123, bf16[128,2048]{1,0:T(8,128)(2,1)} %x_hbm.2), custom_call_target="tpu_custom_call" | custom-call | flops 335544320 | bytes 2621440 | tf_op jit(solution)/shard_map/pallas_call | solution.py:113
  25.9 20.0 %all-to-all-done = bf16[16,40,2048]{2,1,0:T(8,128)(2,1)} async-done(((bf16[16,40,2048]{2,1,0:T(8,128)(2,1)}), bf16[16,40,2048]{2,1,0:T(8,128)(2,1)}, u32[]{:S(2)}, u32[]{:S(2)}) %all-to-all-start) | async-done | bytes 2621472 | tf_op jit(solution)/shard_map/all_to_all | solution.py:378
  45.9 9.6 %all-to-all-start.1 = ((bf16[16,40,2048]{2,1,0:T(8,128)(2,1)}), bf16[16,40,2048]{2,1,0:T(8,128)(2,1)}, u32[]{:S(2)}, u32[]{:S(2)}) async-start(bf16[16,40,2048]{2,1,0:T(8,128)(2,1)} %bitcast.126), calls=%async_computation.1 | async-start | bytes 5242880 | tf_op jit(solution)/shard_map/all_to_all | solution.py:378
  55.5 5.0 %shard_map.115 = (bf16[1024,640]{1,0:T(8,128)(2,1)S(1)}, bf16[1024,640]{1,0:T(8,128)(2,1)S(1)}) custom-call(s32[1]{0:T(128)} %bitcast.3.core_ref, bf16[640,2048]{1,0:T(8,128)(2,1)} %bitcast.5.refs_1_.mine_ref.theirs_ref.x_ref, bf16[640,2048]{1,0:T(8,128)(2,1)} %bitcast.5.refs_1_.mine_ref.theirs_ref.x_ref), custom_call_target="tpu_custom_call" | custom-call | bytes 5242880 | tf_op jit(solution)/shard_map/pallas_call | solution.py:205
  61.6 7.1 %shard_map.116 = (bf16[768,640]{1,0:T(8,128)(2,1)S(1)}, bf16[3,640,256]{2,1,0:T(8,128)(2,1)S(1)}, bf16[3,640,256]{2,1,0:T(8,128)(2,1)S(1)}, bf16[3,640,256]{2,1,0:T(8,128)(2,1)S(1)}) custom-call(bf16[640,2048]{1,0:T(8,128)(2,1)} %bitcast.5.refs_1_.mine_ref.theirs_ref.x_ref, bf16[1,2048,768]{2,1,0:T(8,128)(2,1)S(1)} %copy-done.4, ...), custom_call_target="tpu_custom_call" | custom-call | flops 4026531840 | bytes 13000000 | tf_op jit(solution)/shard_map/pallas_call | solution.py:187
  74.5 13.1 %all-to-all-done.1 = bf16[16,40,2048]{2,1,0:T(8,128)(2,1)} async-done(((bf16[16,40,2048]{2,1,0:T(8,128)(2,1)}), bf16[16,40,2048]{2,1,0:T(8,128)(2,1)}, u32[]{:S(2)}, u32[]{:S(2)}) %all-to-all-start.1) | async-done | bytes 2621472 | tf_op jit(solution)/shard_map/all_to_all | solution.py:378
  87.6 7.1 %shard_map.118 = (bf16[640,768]{1,0:T(8,128)(2,1)}, bf16[640,768]{1,0:T(8,128)(2,1)}, bf16[640,128]{1,0:T(8,128)(2,1)}) custom-call(s32[1]{0:T(128)} %bitcast.2.me_ref, bf16[640,2048]{1,0:T(8,128)(2,1)} %shard_map.117.dy_ref.a_ref, bf16[3,2048,256]{2,1,0:T(8,128)(2,1)} %shard_map.112.refs_2_.wd_ref, bf16[3,640,256]{2,1,0:T(8,128)(2,1)} %copy-done.11, ...), custom_call_target="tpu_custom_call" | custom-call | flops 2013265920 | bytes 11000000 | tf_op jit(solution)/shard_map/pallas_call | solution.py:251
  97.5 5.2 %shard_map.119 = (bf16[768,1024]{1,0:T(8,128)(2,1)S(1)}, bf16[16,128]{1,0:T(8,128)(2,1)S(1)}) custom-call(bf16[768,640]{1,0:T(8,128)(2,1)S(1)} %copy-done.22, bf16[768,640]{1,0:T(8,128)(2,1)} %collective-permute-done.1.refs_2_.bt_ref, bf16[640,2048]{1,0:T(8,128)(2,1)} %shard_map.117.dy_ref.a_ref, bf16[640,2048]{1,0:T(8,128)(2,1)} %collective-permute-done.4.b_ref, ...), custom_call_target="tpu_custom_call" | custom-call | flops 2013265920 | bytes 6160384 | tf_op jit(solution)/shard_map/pallas_call | solution.py:310
  102.7 5.1 %shard_map.120 = (bf16[1024,768]{1,0:T(8,128)(2,1)S(1)}, bf16[16,128]{1,0:T(8,128)(2,1)S(1)}) custom-call(bf16[1024,640]{1,0:T(8,128)(2,1)S(1)} %copy-done.20, bf16[1024,640]{1,0:T(8,128)(2,1)} %collective-permute-done.refs_1_.bt_ref, bf16[640,768]{1,0:T(8,128)(2,1)S(1)} %copy-done.2, bf16[640,768]{1,0:T(8,128)(2,1)S(1)} %collective-permute-done.3.b_ref, ...), custom_call_target="tpu_custom_call" | custom-call | flops 2013265920 | bytes 6160384 | tf_op jit(solution)/shard_map/pallas_call | solution.py:310
  107.9 5.1 %shard_map.121 = (bf16[1024,768]{1,0:T(8,128)(2,1)S(1)}, bf16[16,128]{1,0:T(8,128)(2,1)S(1)}) custom-call(bf16[1024,640]{1,0:T(8,128)(2,1)S(1)} %copy-done.20, bf16[1024,640]{1,0:T(8,128)(2,1)} %collective-permute-done.refs_1_.bt_ref, bf16[640,768]{1,0:T(8,128)(2,1)S(1)} %copy-done.3, bf16[640,768]{1,0:T(8,128)(2,1)S(1)} %collective-permute-done.2.b_ref, ...), custom_call_target="tpu_custom_call" | custom-call | flops 2013265920 | bytes 6160384 | tf_op jit(solution)/shard_map/pallas_call | solution.py:310
  119.2 3.9 %shard_map.122 = (bf16[640,2176]{1,0:T(8,128)(2,1)}, bf16[16,128]{1,0:T(8,128)(2,1)S(1)}) custom-call(bf16[640,768]{1,0:T(8,128)(2,1)S(1)} %copy-done.2, bf16[640,768]{1,0:T(8,128)(2,1)S(1)} %copy-done.3, bf16[4,768,512]{2,1,0:T(8,128)(2,1)S(1)} %copy-done.1, bf16[4,768,512]{2,1,0:T(8,128)(2,1)S(1)} %copy-done, bf16[640,128]{1,0:T(8,128)(2,1)S(1)} %copy-done.15, ...), custom_call_target="tpu_custom_call" | custom-call | flops 2013265920 | bytes 9000000 | tf_op jit(solution)/shard_map/pallas_call | solution.py:286
  126.9 3.9 %shard_map.123 = (bf16[640,2176]{1,0:T(8,128)(2,1)}, bf16[16,128]{1,0:T(8,128)(2,1)}) custom-call(bf16[640,768]{1,0:T(8,128)(2,1)S(1)} %copy-done.2, bf16[640,768]{1,0:T(8,128)(2,1)S(1)} %copy-done.3, bf16[4,768,512]{2,1,0:T(8,128)(2,1)S(1)} %copy-done.1, bf16[4,768,512]{2,1,0:T(8,128)(2,1)S(1)} %copy-done, ...), custom_call_target="tpu_custom_call", output_to_operand_aliasing={{0}: (5, {})} | custom-call | flops 2013265920 | bytes 9000000 | tf_op jit(solution)/shard_map/pallas_call | solution.py:286
  134.0 8.7 %all-to-all-start.2 = ((bf16[16,40,2176]{2,1,0:T(8,128)(2,1)}), bf16[16,40,2176]{2,1,0:T(8,128)(2,1)S(1)}, u32[]{:S(2)}, u32[]{:S(2)}) async-start(bf16[16,40,2176]{2,1,0:T(8,128)(2,1)} %bitcast.17), calls=%async_computation.2 | async-start | bytes 5570560 | tf_op jit(solution)/shard_map/all_to_all | solution.py:378
  143.9 3.1 %collective-permute-start.21 = (bf16[96,1024]{1,0:T(8,128)(2,1)S(1)}, bf16[96,1024]{1,0:T(8,128)(2,1)S(1)}, u32[]{:S(2)}, u32[]{:S(2)}) collective-permute-start(bf16[96,1024]{1,0:T(8,128)(2,1)S(1)} %fusion.5), channel_id=1, source_target_pairs={{0,32},{32,64},{64,96},{96,128},{128,160},{160,192},{192,224},{224... | collective-permute-start | bytes 589832 | tf_op jit(solution)/shard_map/ppermute | solution.py:416
  159.6 3.4 %collective-permute-done.16 = bf16[128,768]{1,0:T(8,128)(2,1)S(1)} collective-permute-done((bf16[128,768]{1,0:T(8,128)(2,1)S(1)}, bf16[128,768]{1,0:T(8,128)(2,1)S(1)}, u32[]{:S(2)}, u32[]{:S(2)}) %collective-permute-start.16) | collective-permute-done | bytes 196640 | tf_op jit(solution)/shard_map/ppermute | solution.py:416
  167.6 3.4 %collective-permute-done.17 = bf16[128,768]{1,0:T(8,128)(2,1)S(1)} collective-permute-done((bf16[128,768]{1,0:T(8,128)(2,1)S(1)}, bf16[128,768]{1,0:T(8,128)(2,1)S(1)}, u32[]{:S(2)}, u32[]{:S(2)}) %collective-permute-start.17) | collective-permute-done | bytes 196640 | tf_op jit(solution)/shard_map/ppermute | solution.py:416
  175.4 5.7 %collective-permute-done.12 = bf16[128,768]{1,0:T(8,128)(2,1)S(1)} collective-permute-done((bf16[128,768]{1,0:T(8,128)(2,1)S(1)}, bf16[128,768]{1,0:T(8,128)(2,1)S(1)}, u32[]{:S(2)}, u32[]{:S(2)}) %collective-permute-start.12) | collective-permute-done | bytes 196640 | tf_op jit(solution)/shard_map/ppermute | solution.py:416
  183.3 4.7 %collective-permute-done.13 = bf16[128,768]{1,0:T(8,128)(2,1)S(1)} collective-permute-done((bf16[128,768]{1,0:T(8,128)(2,1)S(1)}, bf16[128,768]{1,0:T(8,128)(2,1)S(1)}, u32[]{:S(2)}, u32[]{:S(2)}) %collective-permute-start.13) | collective-permute-done | bytes 196640 | tf_op jit(solution)/shard_map/ppermute | solution.py:416
  188.9 2.4 %shard_map.124 = (bf16[128,2048]{1,0:T(8,128)(2,1)}, bf16[4,128]{1,0:T(4,128)(2,1)}) custom-call(s32[4,128]{1,0:T(4,128)S(1)} %bitcast.122, bf16[4,128]{1,0:T(4,128)(2,1)S(1)} %bitcast.124, bf16[640,2176]{1,0:T(8,128)(2,1)S(1)} %bitcast.95), custom_call_target="tpu_custom_call" | custom-call | flops 335544320 | bytes 2621440 | tf_op jit(solution)/shard_map/pallas_call | solution.py:356
  193.7 6.2 %collective-permute-done.19 = bf16[128,768]{1,0:T(8,128)(2,1)S(1)} collective-permute-done((bf16[128,768]{1,0:T(8,128)(2,1)S(1)}, bf16[128,768]{1,0:T(8,128)(2,1)S(1)}, u32[]{:S(2)}, u32[]{:S(2)}) %collective-permute-start.19) | collective-permute-done | bytes 196640 | tf_op jit(solution)/shard_map/ppermute | solution.py:416
  (126 shorter events, 52.5 us)
Async XLA Ops:
  3.6 42.3 %all-to-all-start = ((bf16[16,40,2048]{2,1,0:T(8,128)(2,1)}), bf16[16,40,2048]{2,1,0:T(8,128)(2,1)}, u32[]{:S(2)}, u32[]{:S(2)}) async-start(bf16[16,40,2048]{2,1,0:T(8,128)(2,1)} %bitcast.127), calls=%async_computation | async-start | bytes 5242880 | tf_op jit(solution)/shard_map/all_to_all | solution.py:378
  45.9 41.7 %all-to-all-start.1 = ((bf16[16,40,2048]{2,1,0:T(8,128)(2,1)}), bf16[16,40,2048]{2,1,0:T(8,128)(2,1)}, u32[]{:S(2)}, u32[]{:S(2)}) async-start(bf16[16,40,2048]{2,1,0:T(8,128)(2,1)} %bitcast.126), calls=%async_computation.1 | async-start | bytes 5242880 | tf_op jit(solution)/shard_map/all_to_all | solution.py:378
  61.6 12.8 %collective-permute-start = (bf16[1024,640]{1,0:T(8,128)(2,1)S(1)}, bf16[1024,640]{1,0:T(8,128)(2,1)}, u32[]{:S(2)}, u32[]{:S(2)}) collective-permute-start(bf16[1024,640]{1,0:T(8,128)(2,1)S(1)} %get-tuple-element.28), channel_id=1, source_target_pairs={{0,16},{16,0},{32,48},{48,32},{64,80},{80,64},{96,112},{112,96},{1... | collective-permute-start | bytes 3932168 | tf_op jit(solution)/shard_map/ppermute | solution.py:401
  87.6 7.8 %collective-permute-start.4 = (bf16[640,2048]{1,0:T(8,128)(2,1)}, bf16[640,2048]{1,0:T(8,128)(2,1)}, u32[]{:S(2)}, u32[]{:S(2)}) collective-permute-start(bf16[640,2048]{1,0:T(8,128)(2,1)} %shard_map.117.dy_ref.a_ref), channel_id=1, source_target_pairs={{0,16},{16,0},{32,48},{48,32},{64,80},{80,64},{96,112},{112,96},{1... | collective-permute-start | bytes 7864328 | tf_op jit(solution)/shard_map/ppermute | solution.py:401
  94.7 8.0 %collective-permute-start.3 = (bf16[640,768]{1,0:T(8,128)(2,1)}, bf16[640,768]{1,0:T(8,128)(2,1)S(1)}, u32[]{:S(2)}, u32[]{:S(2)}) collective-permute-start(bf16[640,768]{1,0:T(8,128)(2,1)} %get-tuple-element.33.a_ref.refs_0_), channel_id=1, source_target_pairs={{0,16},{16,0},{32,48},{48,32},{64,80},{80,64},{96,112},{112,96},{1... | collective-permute-start | bytes 2949128 | tf_op jit(solution)/shard_map/ppermute | solution.py:401
  95.3 12.5 %collective-permute-start.2 = (bf16[640,768]{1,0:T(8,128)(2,1)}, bf16[640,768]{1,0:T(8,128)(2,1)S(1)}, u32[]{:S(2)}, u32[]{:S(2)}) collective-permute-start(bf16[640,768]{1,0:T(8,128)(2,1)} %get-tuple-element.34.a_ref.refs_1_), channel_id=1, source_target_pairs={{0,16},{16,0},{32,48},{48,32},{64,80},{80,64},{96,112},{112,96},{1... | collective-permute-start | bytes 2949128 | tf_op jit(solution)/shard_map/ppermute | solution.py:401
  113.1 10.0 %collective-permute-start.7 = (bf16[128,768]{1,0:T(8,128)(2,1)S(1)}, bf16[128,768]{1,0:T(8,128)(2,1)S(1)}, u32[]{:S(2)}, u32[]{:S(2)}) collective-permute-start(bf16[128,768]{1,0:T(8,128)(2,1)S(1)} %dynamic-slice_bitcast_fusion), channel_id=1, source_target_pairs={{0,32},{32,64},{64,96},{96,128},{128,160},{160,192},{192,224},{224... | collective-permute-start | bytes 589832 | tf_op jit(solution)/shard_map/ppermute | solution.py:416
  115.0 9.7 %collective-permute-start.6 = (bf16[128,768]{1,0:T(8,128)(2,1)S(1)}, bf16[128,768]{1,0:T(8,128)(2,1)S(1)}, u32[]{:S(2)}, u32[]{:S(2)}) collective-permute-start(bf16[128,768]{1,0:T(8,128)(2,1)S(1)} %dynamic-slice_bitcast_fusion.1), channel_id=1, source_target_pairs={{0,32},{32,64},{64,96},{96,128},{128,160},{160,192},{192,224},{224... | collective-permute-start | bytes 589832 | tf_op jit(solution)/shard_map/ppermute | solution.py:416
  117.2 9.6 %collective-permute-start.5 = (bf16[96,1024]{1,0:T(8,128)(2,1)S(1)}, bf16[96,1024]{1,0:T(8,128)(2,1)S(1)}, u32[]{:S(2)}, u32[]{:S(2)}) collective-permute-start(bf16[96,1024]{1,0:T(8,128)(2,1)S(1)} %dynamic-slice_bitcast_fusion.2), channel_id=1, source_target_pairs={{0,32},{32,64},{64,96},{96,128},{128,160},{160,192},{192,224},{224... | collective-permute-start | bytes 589832 | tf_op jit(solution)/shard_map/ppermute | solution.py:416
  130.8 11.9 %collective-permute-start.20 = (bf16[96,1024]{1,0:T(8,128)(2,1)S(1)}, bf16[96,1024]{1,0:T(8,128)(2,1)}, u32[]{:S(2)}, u32[]{:S(2)}) collective-permute-start(bf16[96,1024]{1,0:T(8,128)(2,1)S(1)} %shard_map.126), channel_id=1, source_target_pairs={{0,32},{32,64},{64,96},{96,128},{128,160},{160,192},{192,224},{224... | collective-permute-start | bytes 589832 | tf_op jit(solution)/shard_map/ppermute | solution.py:416
  130.8 16.3 %collective-permute-start.14 = (bf16[128,768]{1,0:T(8,128)(2,1)S(1)}, bf16[128,768]{1,0:T(8,128)(2,1)}, u32[]{:S(2)}, u32[]{:S(2)}) collective-permute-start(bf16[128,768]{1,0:T(8,128)(2,1)S(1)} %fusion.18.refs_8_), channel_id=1, source_target_pairs={{0,32},{32,64},{64,96},{96,128},{128,160},{160,192},{192,224},{224... | collective-permute-start | bytes 589832 | tf_op jit(solution)/shard_map/ppermute | solution.py:416
  132.0 16.4 %collective-permute-start.8 = (bf16[128,768]{1,0:T(8,128)(2,1)S(1)}, bf16[128,768]{1,0:T(8,128)(2,1)}, u32[]{:S(2)}, u32[]{:S(2)}) collective-permute-start(bf16[128,768]{1,0:T(8,128)(2,1)S(1)} %fusion.19.refs_7_), channel_id=1, source_target_pairs={{0,32},{32,64},{64,96},{96,128},{128,160},{160,192},{192,224},{224... | collective-permute-start | bytes 589832 | tf_op jit(solution)/shard_map/ppermute | solution.py:416
  134.0 54.9 %all-to-all-start.2 = ((bf16[16,40,2176]{2,1,0:T(8,128)(2,1)}), bf16[16,40,2176]{2,1,0:T(8,128)(2,1)S(1)}, u32[]{:S(2)}, u32[]{:S(2)}) async-start(bf16[16,40,2176]{2,1,0:T(8,128)(2,1)} %bitcast.17), calls=%async_computation.2 | async-start | bytes 5570560 | tf_op jit(solution)/shard_map/all_to_all | solution.py:378
  143.9 7.0 %collective-permute-start.21 = (bf16[96,1024]{1,0:T(8,128)(2,1)S(1)}, bf16[96,1024]{1,0:T(8,128)(2,1)S(1)}, u32[]{:S(2)}, u32[]{:S(2)}) collective-permute-start(bf16[96,1024]{1,0:T(8,128)(2,1)S(1)} %fusion.5), channel_id=1, source_target_pairs={{0,32},{32,64},{64,96},{96,128},{128,160},{160,192},{192,224},{224... | collective-permute-start | bytes 589832 | tf_op jit(solution)/shard_map/ppermute | solution.py:416
  148.1 7.0 %collective-permute-start.15 = (bf16[128,768]{1,0:T(8,128)(2,1)S(1)}, bf16[128,768]{1,0:T(8,128)(2,1)S(1)}, u32[]{:S(2)}, u32[]{:S(2)}) collective-permute-start(bf16[128,768]{1,0:T(8,128)(2,1)S(1)} %fusion.11), channel_id=1, source_target_pairs={{0,32},{32,64},{64,96},{96,128},{128,160},{160,192},{192,224},{224... | collective-permute-start | bytes 589832 | tf_op jit(solution)/shard_map/ppermute | solution.py:416
  149.4 7.8 %collective-permute-start.9 = (bf16[128,768]{1,0:T(8,128)(2,1)S(1)}, bf16[128,768]{1,0:T(8,128)(2,1)S(1)}, u32[]{:S(2)}, u32[]{:S(2)}) collective-permute-start(bf16[128,768]{1,0:T(8,128)(2,1)S(1)} %fusion.17), channel_id=1, source_target_pairs={{0,32},{32,64},{64,96},{96,128},{128,160},{160,192},{192,224},{224... | collective-permute-start | bytes 589832 | tf_op jit(solution)/shard_map/ppermute | solution.py:416
  151.9 7.4 %collective-permute-start.22 = (bf16[96,1024]{1,0:T(8,128)(2,1)S(1)}, bf16[96,1024]{1,0:T(8,128)(2,1)S(1)}, u32[]{:S(2)}, u32[]{:S(2)}) collective-permute-start(bf16[96,1024]{1,0:T(8,128)(2,1)S(1)} %fusion.4), channel_id=1, source_target_pairs={{0,32},{32,64},{64,96},{96,128},{128,160},{160,192},{192,224},{224... | collective-permute-start | bytes 589832 | tf_op jit(solution)/shard_map/ppermute | solution.py:416
  157.3 7.9 %collective-permute-start.10 = (bf16[128,768]{1,0:T(8,128)(2,1)S(1)}, bf16[128,768]{1,0:T(8,128)(2,1)S(1)}, u32[]{:S(2)}, u32[]{:S(2)}) collective-permute-start(bf16[128,768]{1,0:T(8,128)(2,1)S(1)} %fusion.16), channel_id=1, source_target_pairs={{0,32},{32,64},{64,96},{96,128},{128,160},{160,192},{192,224},{224... | collective-permute-start | bytes 589832 | tf_op jit(solution)/shard_map/ppermute | solution.py:416
  159.4 7.9 %collective-permute-start.23 = (bf16[96,1024]{1,0:T(8,128)(2,1)S(1)}, bf16[96,1024]{1,0:T(8,128)(2,1)S(1)}, u32[]{:S(2)}, u32[]{:S(2)}) collective-permute-start(bf16[96,1024]{1,0:T(8,128)(2,1)S(1)} %fusion.3), channel_id=1, source_target_pairs={{0,32},{32,64},{64,96},{96,128},{128,160},{160,192},{192,224},{224... | collective-permute-start | bytes 589832 | tf_op jit(solution)/shard_map/ppermute | solution.py:416
  165.2 7.9 %collective-permute-start.11 = (bf16[128,768]{1,0:T(8,128)(2,1)S(1)}, bf16[128,768]{1,0:T(8,128)(2,1)S(1)}, u32[]{:S(2)}, u32[]{:S(2)}) collective-permute-start(bf16[128,768]{1,0:T(8,128)(2,1)S(1)} %fusion.15), channel_id=1, source_target_pairs={{0,32},{32,64},{64,96},{96,128},{128,160},{160,192},{192,224},{224... | collective-permute-start | bytes 589832 | tf_op jit(solution)/shard_map/ppermute | solution.py:416
  167.3 7.9 %collective-permute-start.24 = (bf16[96,1024]{1,0:T(8,128)(2,1)S(1)}, bf16[96,1024]{1,0:T(8,128)(2,1)S(1)}, u32[]{:S(2)}, u32[]{:S(2)}) collective-permute-start(bf16[96,1024]{1,0:T(8,128)(2,1)S(1)} %fusion.2), channel_id=1, source_target_pairs={{0,32},{32,64},{64,96},{96,128},{128,160},{160,192},{192,224},{224... | collective-permute-start | bytes 589832 | tf_op jit(solution)/shard_map/ppermute | solution.py:416
  172.0 19.3 %collective-permute-start.18 = (bf16[128,768]{1,0:T(8,128)(2,1)S(1)}, bf16[128,768]{1,0:T(8,128)(2,1)S(1)}, u32[]{:S(2)}, u32[]{:S(2)}) collective-permute-start(bf16[128,768]{1,0:T(8,128)(2,1)S(1)} %fusion.8), channel_id=1, source_target_pairs={{0,32},{32,64},{64,96},{96,128},{128,160},{160,192},{192,224},{224... | collective-permute-start | bytes 589832 | tf_op jit(solution)/shard_map/ppermute | solution.py:416
  173.2 7.9 %collective-permute-start.12 = (bf16[128,768]{1,0:T(8,128)(2,1)S(1)}, bf16[128,768]{1,0:T(8,128)(2,1)S(1)}, u32[]{:S(2)}, u32[]{:S(2)}) collective-permute-start(bf16[128,768]{1,0:T(8,128)(2,1)S(1)} %fusion.14), channel_id=1, source_target_pairs={{0,32},{32,64},{64,96},{96,128},{128,160},{160,192},{192,224},{224... | collective-permute-start | bytes 589832 | tf_op jit(solution)/shard_map/ppermute | solution.py:416
  175.3 7.9 %collective-permute-start.25 = (bf16[96,1024]{1,0:T(8,128)(2,1)S(1)}, bf16[96,1024]{1,0:T(8,128)(2,1)S(1)}, u32[]{:S(2)}, u32[]{:S(2)}) collective-permute-start(bf16[96,1024]{1,0:T(8,128)(2,1)S(1)} %fusion.1), channel_id=1, source_target_pairs={{0,32},{32,64},{64,96},{96,128},{128,160},{160,192},{192,224},{224... | collective-permute-start | bytes 589832 | tf_op jit(solution)/shard_map/ppermute | solution.py:416
  (29 other events, 227.8 us)
where the time goes:
time: 203 us; the launch traced here: 202 us
  waiting for transfers between devices  74.4 us (37%)
  Pallas kernels  62.4 us (31%)
  starting transfers between devices  43.7 us (22%)
  other arithmetic  11.9 us (6%)
  local copies, waits for them, and re-layouts  7.89 us (4%)
    ppermute x21, waiting for transfers between devices, ring_step(): came = lax.ppermute(held, 'dp', ROUTE)  39.9 us
    all_to_all x3, waiting for transfers between devices, exchange_experts(): lax.all_to_all(rows.reshape(N_EXP, CAP, width), 'expert', split_axis=0, c...  33.2 us
    all_to_all x3, starting transfers between devices, exchange_experts(): lax.all_to_all(rows.reshape(N_EXP, CAP, width), 'expert', split_axis=0, c...  25.8 us
    ppermute x21, starting transfers between devices, ring_step(): came = lax.ppermute(held, 'dp', ROUTE)  16.6 us
    pallas_call x3, Pallas kernels, outer_sum(): pl.pallas_call(outer_kernel, grid=(n // width,), in_specs=[left, left, pl...  15.3 us
    convert_element_type x19, other arithmetic, ring_step(): return (came.astype(F32) + block.astype(F32)).astype(BF16)  8.82 us
    unnamed x46, local copies, waits for them, and re-layouts  7.82 us
    pallas_call x2, Pallas kernels, pair_grads(): pl.pallas_call(pair_kernel, grid=(4,), in_specs=[part, part, weight, weig...  7.72 us
  transfers between devices with their start and end apart: 30, of which 19 were waited for; matrix products, arithmetic and copies ran while one was open for 5% of the time, Pallas kernels for 25%

commit v1 on v0

--- a/solution.py
+++ b/solution.py
@@ -3,6 +3,7 @@
 from jax import lax
 from jax.experimental import pallas as pl
 from jax.experimental.pallas import tpu as pltpu
+from jax.sharding import Mesh
 from jax.sharding import PartitionSpec as P
 
 F32 = jnp.float32
@@ -267,35 +268,28 @@
     )(me, dy, wd_t, h, f, a)
 
 
-def pair_kernel(*refs):
-    dg_ref, du_ref, wg_ref, wu_ref, gg_ref, _, _, _, _, out_ref, flag_ref = refs
+def pair_kernel(dg_ref, du_ref, wg_ref, wu_ref, gg_ref, after_ref, out_ref):
     n = pl.program_id(0)
     value = dot(dg_ref[...], wg_ref[0]) + dot(du_ref[...], wu_ref[0])
     out_ref[:, pl.ds(pl.multiple_of(n * Q, Q), Q)] = value.astype(BF16)
-    flag_ref[...] = jnp.zeros_like(flag_ref)
 
     @pl.when(n == 0)
     def _():
         out_ref[:, D:] = gg_ref[...]
 
 
-def pair_grads(half, dg, du, wg_t, wu_t, gg, pairs, after):
-    size = ROWS // 2
-    part = pl.BlockSpec((size, FF), lambda n: (half, 0))
+def pair_grads(dg, du, wg_t, wu_t, gg, after):
+    whole = pl.BlockSpec((ROWS, FF), lambda n: (0, 0))
     weight = pl.BlockSpec((1, FF, Q), lambda n: (n, 0, 0))
     return pl.pallas_call(
         pair_kernel,
         grid=(4,),
-        in_specs=[part, part, weight, weight, pl.BlockSpec((size, EXTRA), lambda n: (half, 0))] + [ANY] * 4,
-        out_specs=[
-            pl.BlockSpec((size, D + EXTRA), lambda n: (half, 0)),
-            pl.BlockSpec((16, 128), lambda n: (0, 0)),
-        ],
-        out_shape=[shape(ROWS, D + EXTRA), shape(16, 128)],
-        input_output_aliases={5: 0} if half else {},
+        in_specs=[whole, whole, weight, weight, pl.BlockSpec((ROWS, EXTRA), lambda n: (0, 0)), ANY],
+        out_specs=pl.BlockSpec((ROWS, D + EXTRA), lambda n: (0, 0)),
+        out_shape=shape(ROWS, D + EXTRA),
         compiler_params=params(MID),
-        cost_estimate=cost(2 * ROWS * D * FF, 9_000_000),
-    )(dg, du, wg_t, wu_t, gg, pairs, *after)
+        cost_estimate=cost(4 * ROWS * D * FF, 12_000_000),
+    )(dg, du, wg_t, wu_t, gg, after)
 
 
 def outer_kernel(at_ref, bt_ref, a_ref, b_ref, after_ref, out_ref, flag_ref):
@@ -398,7 +392,7 @@
 
 
 def swap_cores(a):
-    return lax.ppermute(a, "dp", [(i, i ^ 1) for i in range(2 * N_Z)])
+    return lax.ppermute(a, "core", [(0, 1), (1, 0)])
 
 
 def pick(a, index):
@@ -413,7 +407,7 @@
 def ring_step(g, held, z, sign, step, after=None):
     if step == 1:
         held = pick(g, (z - sign) & (N_Z - 1))
-    came = lax.ppermute(held, "dp", ROUTE)
+    came = lax.ppermute(held, ("z", "core"), ROUTE)
     if after is not None:
         came = hold(came, after)
     block = pick(g, (z - (step + 1) * sign) & (N_Z - 1))
@@ -421,8 +415,8 @@
 
 
 def body(tokens, out_grad, gates, expert_ids, w_gate, w_up, w_down):
-    dp = lax.axis_index("dp").astype(jnp.int32)
-    z, core = dp >> 1, dp & 1
+    z = lax.axis_index("z").astype(jnp.int32)
+    core = lax.axis_index("core").astype(jnp.int32)
     sign = 1 - 2 * core
     core_arg = core.reshape(1)
     me = lax.axis_index("expert").astype(jnp.int32).reshape(1)
@@ -447,37 +441,34 @@
     part_gate, flag = outer_sum(x_own, x_other, d_gate, d_gate_other, 0, FF, flag)
     part_up, flag = outer_sum(x_own, x_other, d_up, d_up_other, 0, FF, flag)
 
-    part_down = part_down.reshape(N_Z, FF // N_Z, H)
+    sum_down = lax.psum_scatter(part_down, "z", scatter_dimension=0, tiled=True)
     part_gate = part_gate.reshape(N_Z, D // (2 * N_Z), FF)
     part_up = part_up.reshape(N_Z, D // (2 * N_Z), FF)
-    sum_down = ring_step(part_down, None, z, sign, 1)
     sum_gate = ring_step(part_gate, None, z, sign, 1)
     sum_up = ring_step(part_up, None, z, sign, 1)
 
-    pairs, first_flag = pair_grads(0, d_gate, d_up, gate_t, up_t, prob, flag, (flag, flag, flag))
-    pairs, flag = pair_grads(1, d_gate, d_up, gate_t, up_t, prob, pairs, (sum_down, sum_gate, sum_up))
+    pairs = pair_grads(d_gate, d_up, gate_t, up_t, prob, flag)
+    pairs = hold(pairs, sum_gate[:16, :128], sum_up[:16, :128], mib=62)
     back_rows = exchange_experts(pairs)
     token_grad, gate_grad_t = combine(ids_t, gates_t, back_rows)
-
-    sum_down = hold(sum_down, first_flag)
-    for step in range(2, N_Z):
-        sum_down = ring_step(part_down, sum_down, z, sign, step)
-        sum_gate = ring_step(part_gate, sum_gate, z, sign, step)
-        sum_up = ring_step(part_up, sum_up, z, sign, step, gate_grad_t if step == 6 else None)
-
     halves = sum_down.reshape(2, FF // (2 * N_Z), H)
     mine = pick(halves, core)
     theirs = swap_cores(pick(halves, 1 - core))
     left = jnp.where(core == 0, mine, theirs)
     right = jnp.where(core == 0, theirs, mine)
     grad_down = jnp.concatenate([left, right], axis=1)
+    for step in range(2, N_Z):
+        sum_gate = ring_step(part_gate, sum_gate, z, sign, step, theirs if step == 7 else None)
+        sum_up = ring_step(part_up, sum_up, z, sign, step, gate_grad_t if step == 7 else None)
+
     return token_grad, gate_grad_t.T, sum_gate[None], sum_up[None], grad_down[None]
 
 
 def solution(mesh):
-    both = P(("dp", "expert"), None)
+    mesh = Mesh(mesh.devices.reshape(N_Z, 2, N_EXP), ("z", "core", "expert"))
+    both = P(("z", "core", "expert"), None)
     weight = P("expert", None, None)
-    grad = P("expert", "dp", None)
+    grad = P("expert", ("z", "core"), None)
     return jax.shard_map(
         body,
         mesh=mesh,

time: 203 us -> 211 us (1.039)
  between operations: 1.14 us -> 14.5 us
  starting transfers between devices: 43.7 us -> 31.7 us
  local copies, waits for them, and re-layouts: 7.89 us -> 14.7 us
  Pallas kernels: 62.4 us -> 59.8 us
  waiting for transfers between devices: 74.4 us -> 76.8 us
    ppermute x27 -> x20, starting transfers between devices: 17.9 us -> 6.19 us  [the longest x14 5.01 us: ring_step(): came = lax.ppermute(held, ('z', 'core'), ROUTE)]
    unnamed x46, local copies, waits for them, and re-layouts: 7.82 us -> 12.5 us
    ppermute x27 -> x20, waiting for transfers between devices: 41.3 us -> 45.7 us  [the longest x14 44.3 us: ring_step(): came = lax.ppermute(held, ('z', 'core'), ROUTE)]
    pallas_call x2 -> x1, Pallas kernels: 7.72 us -> 4.78 us  [pair_grads(): pl.pallas_call(pair_kernel, grid=(4,), in_specs=[whole, whole, weight, we...]
    convert_element_type x19 -> x12, other arithmetic: 8.82 us -> 6.9 us  [ring_step(): return (came.astype(F32) + block.astype(F32)).astype(BF16)]
  transfers between devices with their start and end apart: 30 -> 24, of which waited for: 19 -> 16; matrix products, arithmetic and copies ran while one was open for 5% -> 5% of each run, Pallas kernels for 25% -> 27%
where the time goes in v1:
time: 211 us; the launch traced here: 208 us
  waiting for transfers between devices  76.8 us (36%)
  Pallas kernels  59.8 us (28%)
  starting transfers between devices  31.7 us (15%)
  local copies, waits for them, and re-layouts  14.7 us (7%)
  between operations  14.5 us (7%)
  other arithmetic  10.9 us (5%)
    ppermute x14, waiting for transfers between devices, ring_step(): came = lax.ppermute(held, ('z', 'core'), ROUTE)  44.3 us
    all_to_all x3, waiting for transfers between devices, exchange_experts(): lax.all_to_all(rows.reshape(N_EXP, CAP, width), 'expert', split_axis=0, c...  31.1 us
    all_to_all x3, starting transfers between devices, exchange_experts(): lax.all_to_all(rows.reshape(N_EXP, CAP, width), 'expert', split_axis=0, c...  25.5 us
    pallas_call x3, Pallas kernels, outer_sum(): pl.pallas_call(outer_kernel, grid=(n // width,), in_specs=[left, left, pl...  15.6 us
    unnamed x46, local copies, waits for them, and re-layouts  12.5 us
    pallas_call x1, Pallas kernels, backward(): pl.pallas_call(backward_kernel, grid=(3,), in_specs=[SMEM, pl.BlockSpec((...  7.13 us
    pallas_call x1, Pallas kernels, forward(): pl.pallas_call(forward_kernel, grid=(3,), in_specs=[pl.BlockSpec((ROWS, D...  7.1 us
    convert_element_type x12, other arithmetic, ring_step(): return (came.astype(F32) + block.astype(F32)).astype(BF16)  6.9 us
  transfers between devices with their start and end apart: 24, of which 16 were waited for; matrix products, arithmetic and copies ran while one was open for 5% of the time, Pallas kernels for 27%

profile of v1, /device:TPU:2, one launch (start us, length us, event | category | flops | bytes accessed | tf_op | source)
XLA Modules:
  0.0 208.5 jit_solution(13016801187328697819)
XLA Ops:
  7.2 3.0 %shard_map.111 = bf16[640,2048]{1,0:T(8,128)(2,1)} custom-call(s32[1]{0:T(128)} %bitcast.3.core_ref, s32[4,128]{1,0:T(4,128)} %bitcast.89, bf16[128,2048]{1,0:T(8,128)(2,1)} %x_hbm.3), custom_call_target="tpu_custom_call" | custom-call | flops 335544320 | bytes 2621440 | tf_op jit(solution)/shard_map/pallas_call | solution.py:114
  10.2 7.5 %all-to-all-start = ((bf16[16,40,2048]{2,1,0:T(8,128)(2,1)}), bf16[16,40,2048]{2,1,0:T(8,128)(2,1)}, u32[]{:S(2)}, u32[]{:S(2)}) async-start(bf16[16,40,2048]{2,1,0:T(8,128)(2,1)} %bitcast.96), calls=%async_computation | async-start | bytes 5242880 | tf_op jit(solution)/shard_map/all_to_all | solution.py:372
  17.7 5.7 %shard_map.112.refs_2_.wd_ref = bf16[3,2048,256]{2,1,0:T(8,128)(2,1)} custom-call(s32[1]{0:T(128)} %bitcast.3.core_ref, bf16[1,768,2048]{2,1,0:T(8,128)(2,1)} %w_ref.1), custom_call_target="tpu_custom_call" | custom-call | bytes 6291456 | tf_op jit(solution)/shard_map/pallas_call | solution.py:138
  23.4 6.1 %shard_map.113 = (bf16[4,768,512]{2,1,0:T(8,128)(2,1)}, bf16[4,768,512]{2,1,0:T(8,128)(2,1)}) custom-call(bf16[1,2048,768]{2,1,0:T(8,128)(2,1)} %wg_ref.1, bf16[1,2048,768]{2,1,0:T(8,128)(2,1)} %wu_ref.1), custom_call_target="tpu_custom_call" | custom-call | bytes 12582912 | tf_op jit(solution)/shard_map/pallas_call | solution.py:161
  29.6 2.9 %shard_map.110.refs_0_ = bf16[640,2048]{1,0:T(8,128)(2,1)} custom-call(s32[1]{0:T(128)} %bitcast.3.core_ref, s32[4,128]{1,0:T(4,128)} %bitcast.90, bf16[4,128]{1,0:T(4,128)(2,1)} %bitcast.92, bf16[128,2048]{1,0:T(8,128)(2,1)} %x_hbm.2), custom_call_target="tpu_custom_call" | custom-call | flops 335544320 | bytes 2621440 | tf_op jit(solution)/shard_map/pallas_call | solution.py:114
  32.5 20.0 %all-to-all-done = bf16[16,40,2048]{2,1,0:T(8,128)(2,1)} async-done(((bf16[16,40,2048]{2,1,0:T(8,128)(2,1)}), bf16[16,40,2048]{2,1,0:T(8,128)(2,1)}, u32[]{:S(2)}, u32[]{:S(2)}) %all-to-all-start) | async-done | bytes 2621472 | tf_op jit(solution)/shard_map/all_to_all | solution.py:372
  52.5 9.4 %all-to-all-start.1 = ((bf16[16,40,2048]{2,1,0:T(8,128)(2,1)}), bf16[16,40,2048]{2,1,0:T(8,128)(2,1)}, u32[]{:S(2)}, u32[]{:S(2)}) async-start(bf16[16,40,2048]{2,1,0:T(8,128)(2,1)} %bitcast.95), calls=%async_computation.1 | async-start | bytes 5242880 | tf_op jit(solution)/shard_map/all_to_all | solution.py:372
  61.9 5.0 %shard_map.115 = (bf16[1024,640]{1,0:T(8,128)(2,1)S(1)}, bf16[1024,640]{1,0:T(8,128)(2,1)S(1)}) custom-call(s32[1]{0:T(128)} %bitcast.3.core_ref, bf16[640,2048]{1,0:T(8,128)(2,1)} %bitcast.5.refs_1_.mine_ref.theirs_ref.x_ref, bf16[640,2048]{1,0:T(8,128)(2,1)} %bitcast.5.refs_1_.mine_ref.theirs_ref.x_ref), custom_call_target="tpu_custom_call" | custom-call | bytes 5242880 | tf_op jit(solution)/shard_map/pallas_call | solution.py:206
  70.0 7.1 %shard_map.116 = (bf16[768,640]{1,0:T(8,128)(2,1)S(1)}, bf16[3,640,256]{2,1,0:T(8,128)(2,1)S(1)}, bf16[3,640,256]{2,1,0:T(8,128)(2,1)S(1)}, bf16[3,640,256]{2,1,0:T(8,128)(2,1)S(1)}) custom-call(bf16[640,2048]{1,0:T(8,128)(2,1)} %bitcast.5.refs_1_.mine_ref.theirs_ref.x_ref, bf16[1,2048,768]{2,1,0:T(8,128)(2,1)S(1)} %copy-done.2, ...), custom_call_target="tpu_custom_call" | custom-call | flops 4026531840 | bytes 13000000 | tf_op jit(solution)/shard_map/pallas_call | solution.py:188
  82.9 11.1 %all-to-all-done.1 = bf16[16,40,2048]{2,1,0:T(8,128)(2,1)} async-done(((bf16[16,40,2048]{2,1,0:T(8,128)(2,1)}), bf16[16,40,2048]{2,1,0:T(8,128)(2,1)}, u32[]{:S(2)}, u32[]{:S(2)}) %all-to-all-start.1) | async-done | bytes 2621472 | tf_op jit(solution)/shard_map/all_to_all | solution.py:372
  94.0 7.1 %shard_map.118 = (bf16[640,768]{1,0:T(8,128)(2,1)}, bf16[640,768]{1,0:T(8,128)(2,1)}, bf16[640,128]{1,0:T(8,128)(2,1)}) custom-call(s32[1]{0:T(128)} %bitcast.2.me_ref, bf16[640,2048]{1,0:T(8,128)(2,1)} %shard_map.117.dy_ref.a_ref, bf16[3,2048,256]{2,1,0:T(8,128)(2,1)} %shard_map.112.refs_2_.wd_ref, bf16[3,640,256]{2,1,0:T(8,128)(2,1)} %copy-done.7, ...), custom_call_target="tpu_custom_call" | custom-call | flops 2013265920 | bytes 11000000 | tf_op jit(solution)/shard_map/pallas_call | solution.py:252
  103.9 5.9 %shard_map.119 = (bf16[768,1024]{1,0:T(8,128)(2,1)}, bf16[16,128]{1,0:T(8,128)(2,1)S(1)}) custom-call(bf16[768,640]{1,0:T(8,128)(2,1)S(1)} %copy-done.19, bf16[768,640]{1,0:T(8,128)(2,1)} %collective-permute-done.1.refs_2_.bt_ref, bf16[640,2048]{1,0:T(8,128)(2,1)} %shard_map.117.dy_ref.a_ref, bf16[640,2048]{1,0:T(8,128)(2,1)} %collective-permute-done.4.b_ref, ...), custom_call_target="tpu_custom_call" | custom-call | flops 2013265920 | bytes 6160384 | tf_op jit(solution)/shard_map/pallas_call | solution.py:304
  111.1 4.6 %shard_map.120 = (bf16[1024,768]{1,0:T(8,128)(2,1)S(1)}, bf16[16,128]{1,0:T(8,128)(2,1)S(1)}) custom-call(bf16[1024,640]{1,0:T(8,128)(2,1)S(1)} %copy-done.15, bf16[1024,640]{1,0:T(8,128)(2,1)} %collective-permute-done.refs_1_.bt_ref, bf16[640,768]{1,0:T(8,128)(2,1)S(1)} %copy-done.16, bf16[640,768]{1,0:T(8,128)(2,1)} %collective-permute-done.3.b_ref, ...), custom_call_target="tpu_custom_call" | custom-call | flops 2013265920 | bytes 6160384 | tf_op jit(solution)/shard_map/pallas_call | solution.py:304
  115.8 5.1 %shard_map.121 = (bf16[1024,768]{1,0:T(8,128)(2,1)S(1)}, bf16[16,128]{1,0:T(8,128)(2,1)S(1)}) custom-call(bf16[1024,640]{1,0:T(8,128)(2,1)S(1)} %copy-done.15, bf16[1024,640]{1,0:T(8,128)(2,1)} %collective-permute-done.refs_1_.bt_ref, bf16[640,768]{1,0:T(8,128)(2,1)S(1)} %copy-done.17, bf16[640,768]{1,0:T(8,128)(2,1)S(1)} %collective-permute-done.2.b_ref, ...), custom_call_target="tpu_custom_call" | custom-call | flops 2013265920 | bytes 6160384 | tf_op jit(solution)/shard_map/pallas_call | solution.py:304
  125.1 4.8 %shard_map.122.refs_0_ = bf16[640,2176]{1,0:T(8,128)(2,1)S(1)} custom-call(bf16[640,768]{1,0:T(8,128)(2,1)S(1)} %copy-done.16, bf16[640,768]{1,0:T(8,128)(2,1)S(1)} %copy-done.17, bf16[4,768,512]{2,1,0:T(8,128)(2,1)S(1)} %copy-done.13, bf16[4,768,512]{2,1,0:T(8,128)(2,1)S(1)} %copy-done.1, bf16[640,128]{1,0:T(8,128)(2,1)S(1)} %copy-done.21, ...), custom_call_target="tpu_custom_call" | custom-call | flops 4026531840 | bytes 12000000 | tf_op jit(solution)/shard_map/pallas_call | solution.py:284
  131.4 2.5 %collective-permute-done.6 = bf16[128,768]{1,0:T(8,128)(2,1)S(1)} collective-permute-done((bf16[128,768]{1,0:T(8,128)(2,1)S(1)}, bf16[128,768]{1,0:T(8,128)(2,1)S(1)}, u32[]{:S(2)}, u32[]{:S(2)}) %collective-permute-start.6) | collective-permute-done | bytes 196640 | tf_op jit(solution)/shard_map/ppermute | solution.py:410
  134.5 3.7 %collective-permute-done.5 = bf16[128,768]{1,0:T(8,128)(2,1)S(1)} collective-permute-done((bf16[128,768]{1,0:T(8,128)(2,1)S(1)}, bf16[128,768]{1,0:T(8,128)(2,1)S(1)}, u32[]{:S(2)}, u32[]{:S(2)}) %collective-permute-start.5) | collective-permute-done | bytes 196640 | tf_op jit(solution)/shard_map/ppermute | solution.py:410
  138.9 8.6 %all-to-all-start.2 = ((bf16[16,40,2176]{2,1,0:T(8,128)(2,1)}), bf16[16,40,2176]{2,1,0:T(8,128)(2,1)S(1)}, u32[]{:S(2)}, u32[]{:S(2)}) async-start(bf16[16,40,2176]{2,1,0:T(8,128)(2,1)} %bitcast.72), calls=%async_computation.2 | async-start | bytes 5570560 | tf_op jit(solution)/shard_map/all_to_all | solution.py:372
  147.7 7.6 %collective-permute-done.14 = bf16[128,768]{1,0:T(8,128)(2,1)S(1)} collective-permute-done((bf16[128,768]{1,0:T(8,128)(2,1)S(1)}, bf16[128,768]{1,0:T(8,128)(2,1)S(1)}, u32[]{:S(2)}, u32[]{:S(2)}) %collective-permute-start.14) | collective-permute-done | bytes 196640 | tf_op jit(solution)/shard_map/ppermute | solution.py:410
  158.5 4.7 %collective-permute-done.15 = bf16[128,768]{1,0:T(8,128)(2,1)S(1)} collective-permute-done((bf16[128,768]{1,0:T(8,128)(2,1)S(1)}, bf16[128,768]{1,0:T(8,128)(2,1)S(1)}, u32[]{:S(2)}, u32[]{:S(2)}) %collective-permute-start.15) | collective-permute-done | bytes 196640 | tf_op jit(solution)/shard_map/ppermute | solution.py:410
  165.6 5.7 %collective-permute-done.16 = bf16[128,768]{1,0:T(8,128)(2,1)S(1)} collective-permute-done((bf16[128,768]{1,0:T(8,128)(2,1)S(1)}, bf16[128,768]{1,0:T(8,128)(2,1)S(1)}, u32[]{:S(2)}, u32[]{:S(2)}) %collective-permute-start.16) | collective-permute-done | bytes 196640 | tf_op jit(solution)/shard_map/ppermute | solution.py:410
  173.5 5.7 %collective-permute-done.17 = bf16[128,768]{1,0:T(8,128)(2,1)S(1)} collective-permute-done((bf16[128,768]{1,0:T(8,128)(2,1)S(1)}, bf16[128,768]{1,0:T(8,128)(2,1)S(1)}, u32[]{:S(2)}, u32[]{:S(2)}) %collective-permute-start.17) | collective-permute-done | bytes 196640 | tf_op jit(solution)/shard_map/ppermute | solution.py:410
  181.5 5.7 %collective-permute-done.18 = bf16[128,768]{1,0:T(8,128)(2,1)S(1)} collective-permute-done((bf16[128,768]{1,0:T(8,128)(2,1)S(1)}, bf16[128,768]{1,0:T(8,128)(2,1)S(1)}, u32[]{:S(2)}, u32[]{:S(2)}) %collective-permute-start.18) | collective-permute-done | bytes 196640 | tf_op jit(solution)/shard_map/ppermute | solution.py:410
  191.8 4.1 %collective-permute-done.19.refs_0_ = bf16[128,768]{1,0:T(8,128)(2,1)S(1)} collective-permute-done((bf16[128,768]{1,0:T(8,128)(2,1)}, bf16[128,768]{1,0:T(8,128)(2,1)S(1)}, u32[]{:S(2)}, u32[]{:S(2)}) %collective-permute-start.19) | collective-permute-done | bytes 196640 | tf_op jit(solution)/shard_map/ppermute | solution.py:410
  (109 shorter events, 40.2 us)
Async XLA Ops:
  10.2 42.3 %all-to-all-start = ((bf16[16,40,2048]{2,1,0:T(8,128)(2,1)}), bf16[16,40,2048]{2,1,0:T(8,128)(2,1)}, u32[]{:S(2)}, u32[]{:S(2)}) async-start(bf16[16,40,2048]{2,1,0:T(8,128)(2,1)} %bitcast.96), calls=%async_computation | async-start | bytes 5242880 | tf_op jit(solution)/shard_map/all_to_all | solution.py:372
  52.5 41.5 %all-to-all-start.1 = ((bf16[16,40,2048]{2,1,0:T(8,128)(2,1)}), bf16[16,40,2048]{2,1,0:T(8,128)(2,1)}, u32[]{:S(2)}, u32[]{:S(2)}) async-start(bf16[16,40,2048]{2,1,0:T(8,128)(2,1)} %bitcast.95), calls=%async_computation.1 | async-start | bytes 5242880 | tf_op jit(solution)/shard_map/all_to_all | solution.py:372
  61.9 134.7 %reduce-scatter.2.cloned.1.call-start = ((), (), s32[]{:S(2)}) async-start(), calls=%async_computation.4 | async-start | bytes 1769472 | tf_op jit(solution)/shard_map/reduce_scatter | solution.py:444
  68.1 14.7 %collective-permute-start = (bf16[1024,640]{1,0:T(8,128)(2,1)S(1)}, bf16[1024,640]{1,0:T(8,128)(2,1)}, u32[]{:S(2)}, u32[]{:S(2)}) collective-permute-start(bf16[1024,640]{1,0:T(8,128)(2,1)S(1)} %get-tuple-element.25), channel_id=1, source_target_pairs={{0,16},{16,0},{1,17},{17,1},{2,18},{18,2},{3,19},{19,3},{4,20},{20... | collective-permute-start | bytes 3932168 | tf_op jit(solution)/shard_map/ppermute | solution.py:395
  80.0 2.8 %collective-permute-start.1 = (bf16[768,640]{1,0:T(8,128)(2,1)S(1)}, bf16[768,640]{1,0:T(8,128)(2,1)}, u32[]{:S(2)}, u32[]{:S(2)}) collective-permute-start(bf16[768,640]{1,0:T(8,128)(2,1)S(1)} %get-tuple-element.26.at_ref), channel_id=1, source_target_pairs={{0,16},{16,0},{1,17},{17,1},{2,18},{18,2},{3,19},{19,3},{4,20},{20... | collective-permute-start | bytes 2949128 | tf_op jit(solution)/shard_map/ppermute | solution.py:395
  94.0 7.8 %collective-permute-start.4 = (bf16[640,2048]{1,0:T(8,128)(2,1)}, bf16[640,2048]{1,0:T(8,128)(2,1)}, u32[]{:S(2)}, u32[]{:S(2)}) collective-permute-start(bf16[640,2048]{1,0:T(8,128)(2,1)} %shard_map.117.dy_ref.a_ref), channel_id=1, source_target_pairs={{0,16},{16,0},{1,17},{17,1},{2,18},{18,2},{3,19},{19,3},{4,20},{20... | collective-permute-start | bytes 7864328 | tf_op jit(solution)/shard_map/ppermute | solution.py:395
  101.1 8.7 %collective-permute-start.3 = (bf16[640,768]{1,0:T(8,128)(2,1)}, bf16[640,768]{1,0:T(8,128)(2,1)}, u32[]{:S(2)}, u32[]{:S(2)}) collective-permute-start(bf16[640,768]{1,0:T(8,128)(2,1)} %get-tuple-element.30.a_ref.dg_ref), channel_id=1, source_target_pairs={{0,16},{16,0},{1,17},{17,1},{2,18},{18,2},{3,19},{19,3},{4,20},{20... | collective-permute-start | bytes 2949128 | tf_op jit(solution)/shard_map/ppermute | solution.py:395
  101.7 14.1 %collective-permute-start.2 = (bf16[640,768]{1,0:T(8,128)(2,1)}, bf16[640,768]{1,0:T(8,128)(2,1)S(1)}, u32[]{:S(2)}, u32[]{:S(2)}) collective-permute-start(bf16[640,768]{1,0:T(8,128)(2,1)} %get-tuple-element.31.a_ref.du_ref), channel_id=1, source_target_pairs={{0,16},{16,0},{1,17},{17,1},{2,18},{18,2},{3,19},{19,3},{4,20},{20... | collective-permute-start | bytes 2949128 | tf_op jit(solution)/shard_map/ppermute | solution.py:395
  120.9 13.0 %collective-permute-start.6 = (bf16[128,768]{1,0:T(8,128)(2,1)S(1)}, bf16[128,768]{1,0:T(8,128)(2,1)S(1)}, u32[]{:S(2)}, u32[]{:S(2)}) collective-permute-start(bf16[128,768]{1,0:T(8,128)(2,1)S(1)} %dynamic-slice_bitcast_fusion), channel_id=1, source_target_pairs={{0,32},{32,64},{64,96},{96,128},{128,160},{160,192},{192,224},{224... | collective-permute-start | bytes 589832 | tf_op jit(solution)/shard_map/ppermute | solution.py:410
  122.9 15.4 %collective-permute-start.5 = (bf16[128,768]{1,0:T(8,128)(2,1)S(1)}, bf16[128,768]{1,0:T(8,128)(2,1)S(1)}, u32[]{:S(2)}, u32[]{:S(2)}) collective-permute-start(bf16[128,768]{1,0:T(8,128)(2,1)S(1)} %dynamic-slice_bitcast_fusion.1), channel_id=1, source_target_pairs={{0,32},{32,64},{64,96},{96,128},{128,160},{160,192},{192,224},{224... | collective-permute-start | bytes 589832 | tf_op jit(solution)/shard_map/ppermute | solution.py:410
  138.9 50.5 %all-to-all-start.2 = ((bf16[16,40,2176]{2,1,0:T(8,128)(2,1)}), bf16[16,40,2176]{2,1,0:T(8,128)(2,1)S(1)}, u32[]{:S(2)}, u32[]{:S(2)}) async-start(bf16[16,40,2176]{2,1,0:T(8,128)(2,1)} %bitcast.72), calls=%async_computation.2 | async-start | bytes 5570560 | tf_op jit(solution)/shard_map/all_to_all | solution.py:372
  147.6 7.8 %collective-permute-start.14 = (bf16[128,768]{1,0:T(8,128)(2,1)S(1)}, bf16[128,768]{1,0:T(8,128)(2,1)S(1)}, u32[]{:S(2)}, u32[]{:S(2)}) collective-permute-start(bf16[128,768]{1,0:T(8,128)(2,1)S(1)} %fusion.12), channel_id=1, source_target_pairs={{0,32},{32,64},{64,96},{96,128},{128,160},{160,192},{192,224},{224... | collective-permute-start | bytes 589832 | tf_op jit(solution)/shard_map/ppermute | solution.py:410
  147.6 9.8 %collective-permute-start.7 = (bf16[128,768]{1,0:T(8,128)(2,1)S(1)}, bf16[128,768]{1,0:T(8,128)(2,1)S(1)}, u32[]{:S(2)}, u32[]{:S(2)}) collective-permute-start(bf16[128,768]{1,0:T(8,128)(2,1)S(1)} %fusion.13), channel_id=1, source_target_pairs={{0,32},{32,64},{64,96},{96,128},{128,160},{160,192},{192,224},{224... | collective-permute-start | bytes 589832 | tf_op jit(solution)/shard_map/ppermute | solution.py:410
  156.3 7.0 %collective-permute-start.15 = (bf16[128,768]{1,0:T(8,128)(2,1)S(1)}, bf16[128,768]{1,0:T(8,128)(2,1)S(1)}, u32[]{:S(2)}, u32[]{:S(2)}) collective-permute-start(bf16[128,768]{1,0:T(8,128)(2,1)S(1)} %fusion.5), channel_id=1, source_target_pairs={{0,32},{32,64},{64,96},{96,128},{128,160},{160,192},{192,224},{224... | collective-permute-start | bytes 589832 | tf_op jit(solution)/shard_map/ppermute | solution.py:410
  158.4 7.0 %collective-permute-start.8 = (bf16[128,768]{1,0:T(8,128)(2,1)S(1)}, bf16[128,768]{1,0:T(8,128)(2,1)S(1)}, u32[]{:S(2)}, u32[]{:S(2)}) collective-permute-start(bf16[128,768]{1,0:T(8,128)(2,1)S(1)} %fusion.11), channel_id=1, source_target_pairs={{0,32},{32,64},{64,96},{96,128},{128,160},{160,192},{192,224},{224... | collective-permute-start | bytes 589832 | tf_op jit(solution)/shard_map/ppermute | solution.py:410
  164.3 7.0 %collective-permute-start.16 = (bf16[128,768]{1,0:T(8,128)(2,1)S(1)}, bf16[128,768]{1,0:T(8,128)(2,1)S(1)}, u32[]{:S(2)}, u32[]{:S(2)}) collective-permute-start(bf16[128,768]{1,0:T(8,128)(2,1)S(1)} %fusion.4), channel_id=1, source_target_pairs={{0,32},{32,64},{64,96},{96,128},{128,160},{160,192},{192,224},{224... | collective-permute-start | bytes 589832 | tf_op jit(solution)/shard_map/ppermute | solution.py:410
  165.5 7.9 %collective-permute-start.9 = (bf16[128,768]{1,0:T(8,128)(2,1)S(1)}, bf16[128,768]{1,0:T(8,128)(2,1)S(1)}, u32[]{:S(2)}, u32[]{:S(2)}) collective-permute-start(bf16[128,768]{1,0:T(8,128)(2,1)S(1)} %fusion.10), channel_id=1, source_target_pairs={{0,32},{32,64},{64,96},{96,128},{128,160},{160,192},{192,224},{224... | collective-permute-start | bytes 589832 | tf_op jit(solution)/shard_map/ppermute | solution.py:410
  172.2 7.0 %collective-permute-start.17 = (bf16[128,768]{1,0:T(8,128)(2,1)S(1)}, bf16[128,768]{1,0:T(8,128)(2,1)S(1)}, u32[]{:S(2)}, u32[]{:S(2)}) collective-permute-start(bf16[128,768]{1,0:T(8,128)(2,1)S(1)} %fusion.3), channel_id=1, source_target_pairs={{0,32},{32,64},{64,96},{96,128},{128,160},{160,192},{192,224},{224... | collective-permute-start | bytes 589832 | tf_op jit(solution)/shard_map/ppermute | solution.py:410
  173.4 7.9 %collective-permute-start.10 = (bf16[128,768]{1,0:T(8,128)(2,1)S(1)}, bf16[128,768]{1,0:T(8,128)(2,1)S(1)}, u32[]{:S(2)}, u32[]{:S(2)}) collective-permute-start(bf16[128,768]{1,0:T(8,128)(2,1)S(1)} %fusion.9), channel_id=1, source_target_pairs={{0,32},{32,64},{64,96},{96,128},{128,160},{160,192},{192,224},{224... | collective-permute-start | bytes 589832 | tf_op jit(solution)/shard_map/ppermute | solution.py:410
  180.2 7.0 %collective-permute-start.18 = (bf16[128,768]{1,0:T(8,128)(2,1)S(1)}, bf16[128,768]{1,0:T(8,128)(2,1)S(1)}, u32[]{:S(2)}, u32[]{:S(2)}) collective-permute-start(bf16[128,768]{1,0:T(8,128)(2,1)S(1)} %fusion.2), channel_id=1, source_target_pairs={{0,32},{32,64},{64,96},{96,128},{128,160},{160,192},{192,224},{224... | collective-permute-start | bytes 589832 | tf_op jit(solution)/shard_map/ppermute | solution.py:410
  181.4 7.9 %collective-permute-start.11 = (bf16[128,768]{1,0:T(8,128)(2,1)S(1)}, bf16[128,768]{1,0:T(8,128)(2,1)S(1)}, u32[]{:S(2)}, u32[]{:S(2)}) collective-permute-start(bf16[128,768]{1,0:T(8,128)(2,1)S(1)} %fusion.8), channel_id=1, source_target_pairs={{0,32},{32,64},{64,96},{96,128},{128,160},{160,192},{192,224},{224... | collective-permute-start | bytes 589832 | tf_op jit(solution)/shard_map/ppermute | solution.py:410
  188.8 7.1 %collective-permute-start.19 = (bf16[128,768]{1,0:T(8,128)(2,1)}, bf16[128,768]{1,0:T(8,128)(2,1)S(1)}, u32[]{:S(2)}, u32[]{:S(2)}) collective-permute-start(bf16[128,768]{1,0:T(8,128)(2,1)} %fusion.1), channel_id=1, source_target_pairs={{0,32},{32,64},{64,96},{96,128},{128,160},{160,192},{192,224},{224... | collective-permute-start | bytes 589832 | tf_op jit(solution)/shard_map/ppermute | solution.py:410
  189.3 9.9 %collective-permute-start.12 = (bf16[128,768]{1,0:T(8,128)(2,1)S(1)}, bf16[128,768]{1,0:T(8,128)(2,1)S(1)}, u32[]{:S(2)}, u32[]{:S(2)}) collective-permute-start(bf16[128,768]{1,0:T(8,128)(2,1)S(1)} %fusion.7), channel_id=1, source_target_pairs={{0,32},{32,64},{64,96},{96,128},{128,160},{160,192},{192,224},{224... | collective-permute-start | bytes 589832 | tf_op jit(solution)/shard_map/ppermute | solution.py:410
  197.6 1.7 collective-permute-start.13
  (23 other events, 149.5 us)
Sparse Core Ops, SparseCore 0:
  109.9 45.4 reduce-scatter.1

commit v2 on v0

--- a/solution.py
+++ b/solution.py
@@ -17,7 +17,7 @@
 EXTRA = 128
 CHUNK = 160
 FULL = 64
-MID = 26
+MID = 28
 H = D // 2
 Q = D // 4
 
@@ -267,8 +267,7 @@
     )(me, dy, wd_t, h, f, a)
 
 
-def pair_kernel(*refs):
-    dg_ref, du_ref, wg_ref, wu_ref, gg_ref, _, _, _, _, out_ref, flag_ref = refs
+def pair_kernel(dg_ref, du_ref, wg_ref, wu_ref, gg_ref, after_ref, out_ref, flag_ref):
     n = pl.program_id(0)
     value = dot(dg_ref[...], wg_ref[0]) + dot(du_ref[...], wu_ref[0])
     out_ref[:, pl.ds(pl.multiple_of(n * Q, Q), Q)] = value.astype(BF16)
@@ -279,23 +278,21 @@
         out_ref[:, D:] = gg_ref[...]
 
 
-def pair_grads(half, dg, du, wg_t, wu_t, gg, pairs, after):
-    size = ROWS // 2
-    part = pl.BlockSpec((size, FF), lambda n: (half, 0))
+def pair_grads(dg, du, wg_t, wu_t, gg, after):
+    whole = pl.BlockSpec((ROWS, FF), lambda n: (0, 0))
     weight = pl.BlockSpec((1, FF, Q), lambda n: (n, 0, 0))
     return pl.pallas_call(
         pair_kernel,
         grid=(4,),
-        in_specs=[part, part, weight, weight, pl.BlockSpec((size, EXTRA), lambda n: (half, 0))] + [ANY] * 4,
+        in_specs=[whole, whole, weight, weight, pl.BlockSpec((ROWS, EXTRA), lambda n: (0, 0)), ANY],
         out_specs=[
-            pl.BlockSpec((size, D + EXTRA), lambda n: (half, 0)),
+            pl.BlockSpec((ROWS, D + EXTRA), lambda n: (0, 0)),
             pl.BlockSpec((16, 128), lambda n: (0, 0)),
         ],
         out_shape=[shape(ROWS, D + EXTRA), shape(16, 128)],
-        input_output_aliases={5: 0} if half else {},
         compiler_params=params(MID),
-        cost_estimate=cost(2 * ROWS * D * FF, 9_000_000),
-    )(dg, du, wg_t, wu_t, gg, pairs, *after)
+        cost_estimate=cost(4 * ROWS * D * FF, 12_000_000),
+    )(dg, du, wg_t, wu_t, gg, after)
 
 
 def outer_kernel(at_ref, bt_ref, a_ref, b_ref, after_ref, out_ref, flag_ref):
@@ -443,9 +440,10 @@
     dy_other = swap_cores(dy)
     d_gate, d_up, prob = backward(me, dy, down_t, hidden, factor, active)
     d_gate_other, d_up_other = swap_cores(d_gate), swap_cores(d_up)
-    part_down, flag = outer_sum(hidden_t, hidden_other_t, dy, dy_other, H, H, prob)
+    part_down, flag = outer_sum(hidden_t, hidden_other_t, dy, dy_other, H, H, me)
     part_gate, flag = outer_sum(x_own, x_other, d_gate, d_gate_other, 0, FF, flag)
     part_up, flag = outer_sum(x_own, x_other, d_up, d_up_other, 0, FF, flag)
+    pairs, flag = pair_grads(d_gate, d_up, gate_t, up_t, prob, flag)
 
     part_down = part_down.reshape(N_Z, FF // N_Z, H)
     part_gate = part_gate.reshape(N_Z, D // (2 * N_Z), FF)
@@ -453,17 +451,14 @@
     sum_down = ring_step(part_down, None, z, sign, 1)
     sum_gate = ring_step(part_gate, None, z, sign, 1)
     sum_up = ring_step(part_up, None, z, sign, 1)
-
-    pairs, first_flag = pair_grads(0, d_gate, d_up, gate_t, up_t, prob, flag, (flag, flag, flag))
-    pairs, flag = pair_grads(1, d_gate, d_up, gate_t, up_t, prob, pairs, (sum_down, sum_gate, sum_up))
+    pairs = hold(pairs, sum_down, sum_gate, sum_up, mib=1)
     back_rows = exchange_experts(pairs)
     token_grad, gate_grad_t = combine(ids_t, gates_t, back_rows)
-
-    sum_down = hold(sum_down, first_flag)
+    sum_down = hold(sum_down, flag)
     for step in range(2, N_Z):
         sum_down = ring_step(part_down, sum_down, z, sign, step)
         sum_gate = ring_step(part_gate, sum_gate, z, sign, step)
-        sum_up = ring_step(part_up, sum_up, z, sign, step, gate_grad_t if step == 6 else None)
+        sum_up = ring_step(part_up, sum_up, z, sign, step, gate_grad_t if step == 7 else None)
 
     halves = sum_down.reshape(2, FF // (2 * N_Z), H)
     mine = pick(halves, core)

time: 203 us -> 191 us (0.941)
  waiting for transfers between devices: 74.4 us -> 66.6 us
  Pallas kernels: 62.4 us -> 58.4 us
    ppermute x21, waiting for transfers between devices: 39.9 us -> 32 us  [ring_step(): came = lax.ppermute(held, 'dp', ROUTE)]
    pallas_call x2 -> x1, Pallas kernels: 7.72 us -> 4.78 us  [pair_grads(): pl.pallas_call(pair_kernel, grid=(4,), in_specs=[whole, whole, weight, we...]
  transfers between devices with their start and end apart: 30 -> 30, of which waited for: 19 -> 16; matrix products, arithmetic and copies ran while one was open for 5% -> 5% of each run, Pallas kernels for 25% -> 29%
where the time goes in v2:
time: 191 us; the launch traced here: 188 us
  waiting for transfers between devices  66.6 us (35%)
  Pallas kernels  58.4 us (31%)
  starting transfers between devices  42 us (22%)
  other arithmetic  11.7 us (6%)
  local copies, waits for them, and re-layouts  8.63 us (5%)
    all_to_all x3, waiting for transfers between devices, exchange_experts(): lax.all_to_all(rows.reshape(N_EXP, CAP, width), 'expert', split_axis=0, c...  33.2 us
    ppermute x21, waiting for transfers between devices, ring_step(): came = lax.ppermute(held, 'dp', ROUTE)  32 us
    all_to_all x3, starting transfers between devices, exchange_experts(): lax.all_to_all(rows.reshape(N_EXP, CAP, width), 'expert', split_axis=0, c...  25.8 us
    ppermute x21, starting transfers between devices, ring_step(): came = lax.ppermute(held, 'dp', ROUTE)  14.9 us
    pallas_call x3, Pallas kernels, outer_sum(): pl.pallas_call(outer_kernel, grid=(n // width,), in_specs=[left, left, pl...  14.2 us
    unnamed x46, local copies, waits for them, and re-layouts  8.54 us
    convert_element_type x19, other arithmetic, ring_step(): return (came.astype(F32) + block.astype(F32)).astype(BF16)  7.7 us
    pallas_call x1, Pallas kernels, backward(): pl.pallas_call(backward_kernel, grid=(3,), in_specs=[SMEM, pl.BlockSpec((...  7.13 us
  transfers between devices with their start and end apart: 30, of which 16 were waited for; matrix products, arithmetic and copies ran while one was open for 5% of the time, Pallas kernels for 29%

profile of v2, /device:TPU:2, one launch (start us, length us, event | category | flops | bytes accessed | tf_op | source)
XLA Modules:
  0.0 188.4 jit_solution(17347511101032974359)
XLA Ops:
  0.6 2.9 %shard_map.111 = bf16[640,2048]{1,0:T(8,128)(2,1)} custom-call(s32[1]{0:T(128)} %bitcast.3.core_ref, s32[4,128]{1,0:T(4,128)} %bitcast.121, bf16[128,2048]{1,0:T(8,128)(2,1)} %x_hbm.3), custom_call_target="tpu_custom_call" | custom-call | flops 335544320 | bytes 2621440 | tf_op jit(solution)/shard_map/pallas_call | solution.py:113
  3.6 7.5 %all-to-all-start = ((bf16[16,40,2048]{2,1,0:T(8,128)(2,1)}), bf16[16,40,2048]{2,1,0:T(8,128)(2,1)}, u32[]{:S(2)}, u32[]{:S(2)}) async-start(bf16[16,40,2048]{2,1,0:T(8,128)(2,1)} %bitcast.128), calls=%async_computation | async-start | bytes 5242880 | tf_op jit(solution)/shard_map/all_to_all | solution.py:375
  11.0 5.8 %shard_map.112.refs_2_.wd_ref = bf16[3,2048,256]{2,1,0:T(8,128)(2,1)} custom-call(s32[1]{0:T(128)} %bitcast.3.core_ref, bf16[1,768,2048]{2,1,0:T(8,128)(2,1)} %w_ref.1), custom_call_target="tpu_custom_call" | custom-call | bytes 6291456 | tf_op jit(solution)/shard_map/pallas_call | solution.py:137
  16.8 6.1 %shard_map.113 = (bf16[4,768,512]{2,1,0:T(8,128)(2,1)}, bf16[4,768,512]{2,1,0:T(8,128)(2,1)}) custom-call(bf16[1,2048,768]{2,1,0:T(8,128)(2,1)} %wg_ref.1, bf16[1,2048,768]{2,1,0:T(8,128)(2,1)} %wu_ref.1), custom_call_target="tpu_custom_call" | custom-call | bytes 12582912 | tf_op jit(solution)/shard_map/pallas_call | solution.py:160
  22.9 2.9 %shard_map.110.refs_0_ = bf16[640,2048]{1,0:T(8,128)(2,1)} custom-call(s32[1]{0:T(128)} %bitcast.3.core_ref, s32[4,128]{1,0:T(4,128)} %bitcast.122, bf16[4,128]{1,0:T(4,128)(2,1)} %bitcast.124, bf16[128,2048]{1,0:T(8,128)(2,1)} %x_hbm.2), custom_call_target="tpu_custom_call" | custom-call | flops 335544320 | bytes 2621440 | tf_op jit(solution)/shard_map/pallas_call | solution.py:113
  25.9 20.0 %all-to-all-done = bf16[16,40,2048]{2,1,0:T(8,128)(2,1)} async-done(((bf16[16,40,2048]{2,1,0:T(8,128)(2,1)}), bf16[16,40,2048]{2,1,0:T(8,128)(2,1)}, u32[]{:S(2)}, u32[]{:S(2)}) %all-to-all-start) | async-done | bytes 2621472 | tf_op jit(solution)/shard_map/all_to_all | solution.py:375
  45.9 9.6 %all-to-all-start.1 = ((bf16[16,40,2048]{2,1,0:T(8,128)(2,1)}), bf16[16,40,2048]{2,1,0:T(8,128)(2,1)}, u32[]{:S(2)}, u32[]{:S(2)}) async-start(bf16[16,40,2048]{2,1,0:T(8,128)(2,1)} %bitcast.127), calls=%async_computation.1 | async-start | bytes 5242880 | tf_op jit(solution)/shard_map/all_to_all | solution.py:375
  55.5 5.0 %shard_map.115 = (bf16[1024,640]{1,0:T(8,128)(2,1)S(1)}, bf16[1024,640]{1,0:T(8,128)(2,1)S(1)}) custom-call(s32[1]{0:T(128)} %bitcast.3.core_ref, bf16[640,2048]{1,0:T(8,128)(2,1)} %bitcast.5.refs_1_.mine_ref.theirs_ref.x_ref, bf16[640,2048]{1,0:T(8,128)(2,1)} %bitcast.5.refs_1_.mine_ref.theirs_ref.x_ref), custom_call_target="tpu_custom_call" | custom-call | bytes 5242880 | tf_op jit(solution)/shard_map/pallas_call | solution.py:205
  61.6 7.1 %shard_map.116 = (bf16[768,640]{1,0:T(8,128)(2,1)S(1)}, bf16[3,640,256]{2,1,0:T(8,128)(2,1)S(1)}, bf16[3,640,256]{2,1,0:T(8,128)(2,1)S(1)}, bf16[3,640,256]{2,1,0:T(8,128)(2,1)S(1)}) custom-call(bf16[640,2048]{1,0:T(8,128)(2,1)} %bitcast.5.refs_1_.mine_ref.theirs_ref.x_ref, bf16[1,2048,768]{2,1,0:T(8,128)(2,1)S(1)} %copy-done.2, ...), custom_call_target="tpu_custom_call" | custom-call | flops 4026531840 | bytes 13000000 | tf_op jit(solution)/shard_map/pallas_call | solution.py:187
  74.4 13.2 %all-to-all-done.1 = bf16[16,40,2048]{2,1,0:T(8,128)(2,1)} async-done(((bf16[16,40,2048]{2,1,0:T(8,128)(2,1)}), bf16[16,40,2048]{2,1,0:T(8,128)(2,1)}, u32[]{:S(2)}, u32[]{:S(2)}) %all-to-all-start.1) | async-done | bytes 2621472 | tf_op jit(solution)/shard_map/all_to_all | solution.py:375
  87.6 7.1 %shard_map.118 = (bf16[640,768]{1,0:T(8,128)(2,1)}, bf16[640,768]{1,0:T(8,128)(2,1)}, bf16[640,128]{1,0:T(8,128)(2,1)}) custom-call(s32[1]{0:T(128)} %bitcast.2.me_ref.after_ref, bf16[640,2048]{1,0:T(8,128)(2,1)} %shard_map.117.dy_ref.a_ref, bf16[3,2048,256]{2,1,0:T(8,128)(2,1)} %shard_map.112.refs_2_.wd_ref, bf16[3,640,256]{2,1,0:T(8,128)(2,1)} %copy-done.9, ...), custom_call_target="tpu_custom_call" | custom-call | flops 2013265920 | bytes 11000000 | tf_op jit(solution)/shard_map/pallas_call | solution.py:251
  96.8 5.0 %shard_map.119 = (bf16[768,1024]{1,0:T(8,128)(2,1)S(1)}, bf16[16,128]{1,0:T(8,128)(2,1)S(1)}) custom-call(bf16[768,640]{1,0:T(8,128)(2,1)S(1)} %copy-done.21, bf16[768,640]{1,0:T(8,128)(2,1)} %collective-permute-done.1.refs_2_.bt_ref, bf16[640,2048]{1,0:T(8,128)(2,1)} %shard_map.117.dy_ref.a_ref, bf16[640,2048]{1,0:T(8,128)(2,1)} %collective-permute-done.4.b_ref, ...), custom_call_target="tpu_custom_call" | custom-call | flops 2013265920 | bytes 6160384 | tf_op jit(solution)/shard_map/pallas_call | solution.py:307
  103.8 4.5 %shard_map.120 = (bf16[1024,768]{1,0:T(8,128)(2,1)S(1)}, bf16[16,128]{1,0:T(8,128)(2,1)S(1)}) custom-call(bf16[1024,640]{1,0:T(8,128)(2,1)S(1)} %copy-done.17, bf16[1024,640]{1,0:T(8,128)(2,1)} %collective-permute-done.refs_1_.bt_ref, bf16[640,768]{1,0:T(8,128)(2,1)S(1)} %copy-done.18, bf16[640,768]{1,0:T(8,128)(2,1)S(1)} %collective-permute-done.3.b_ref, ...), custom_call_target="tpu_custom_call" | custom-call | flops 2013265920 | bytes 6160384 | tf_op jit(solution)/shard_map/pallas_call | solution.py:307
  110.6 4.6 %shard_map.121 = (bf16[1024,768]{1,0:T(8,128)(2,1)S(1)}, bf16[16,128]{1,0:T(8,128)(2,1)S(1)}) custom-call(bf16[1024,640]{1,0:T(8,128)(2,1)S(1)} %copy-done.17, bf16[1024,640]{1,0:T(8,128)(2,1)} %collective-permute-done.refs_1_.bt_ref, bf16[640,768]{1,0:T(8,128)(2,1)S(1)} %copy-done.19, bf16[640,768]{1,0:T(8,128)(2,1)S(1)} %collective-permute-done.2.b_ref, ...), custom_call_target="tpu_custom_call" | custom-call | flops 2013265920 | bytes 6160384 | tf_op jit(solution)/shard_map/pallas_call | solution.py:307
  117.3 4.8 %shard_map.122 = (bf16[640,2176]{1,0:T(8,128)(2,1)S(1)}, bf16[16,128]{1,0:T(8,128)(2,1)S(1)}) custom-call(bf16[640,768]{1,0:T(8,128)(2,1)S(1)} %copy-done.18, bf16[640,768]{1,0:T(8,128)(2,1)S(1)} %copy-done.19, bf16[4,768,512]{2,1,0:T(8,128)(2,1)S(1)} %copy-done.15, bf16[4,768,512]{2,1,0:T(8,128)(2,1)S(1)} %copy-done.1, bf16[640,128]{1,0:T(8,128)(2,1)S(1)} %copy-done.22, ...), custom_call_target="tpu_custom_call" | custom-call | flops 4026531840 | bytes 12000000 | tf_op jit(solution)/shard_map/pallas_call | solution.py:284
  122.2 3.2 %collective-permute-start.8 = (bf16[128,768]{1,0:T(8,128)(2,1)S(1)}, bf16[128,768]{1,0:T(8,128)(2,1)}, u32[]{:S(2)}, u32[]{:S(2)}) collective-permute-start(bf16[128,768]{1,0:T(8,128)(2,1)S(1)} %fusion.19.refs_2_), channel_id=1, source_target_pairs={{0,32},{32,64},{64,96},{96,128},{128,160},{160,192},{192,224},{224... | collective-permute-start | bytes 589832 | tf_op jit(solution)/shard_map/ppermute | solution.py:413
  128.2 8.7 %all-to-all-start.2 = ((bf16[16,40,2176]{2,1,0:T(8,128)(2,1)}), bf16[16,40,2176]{2,1,0:T(8,128)(2,1)S(1)}, u32[]{:S(2)}, u32[]{:S(2)}) async-start(bf16[16,40,2176]{2,1,0:T(8,128)(2,1)} %bitcast.96), calls=%async_computation.2 | async-start | bytes 5570560 | tf_op jit(solution)/shard_map/all_to_all | solution.py:375
  148.4 3.5 %collective-permute-done.21 = bf16[96,1024]{1,0:T(8,128)(2,1)S(1)} collective-permute-done((bf16[96,1024]{1,0:T(8,128)(2,1)S(1)}, bf16[96,1024]{1,0:T(8,128)(2,1)S(1)}, u32[]{:S(2)}, u32[]{:S(2)}) %collective-permute-start.21) | collective-permute-done | bytes 196640 | tf_op jit(solution)/shard_map/ppermute | solution.py:413
  156.2 2.6 %collective-permute-done.22 = bf16[96,1024]{1,0:T(8,128)(2,1)S(1)} collective-permute-done((bf16[96,1024]{1,0:T(8,128)(2,1)S(1)}, bf16[96,1024]{1,0:T(8,128)(2,1)S(1)}, u32[]{:S(2)}, u32[]{:S(2)}) %collective-permute-start.22) | collective-permute-done | bytes 196640 | tf_op jit(solution)/shard_map/ppermute | solution.py:413
  159.2 2.7 %collective-permute-done.11 = bf16[128,768]{1,0:T(8,128)(2,1)S(1)} collective-permute-done((bf16[128,768]{1,0:T(8,128)(2,1)S(1)}, bf16[128,768]{1,0:T(8,128)(2,1)S(1)}, u32[]{:S(2)}, u32[]{:S(2)}) %collective-permute-start.11) | collective-permute-done | bytes 196640 | tf_op jit(solution)/shard_map/ppermute | solution.py:413
  166.3 3.6 %collective-permute-done.12 = bf16[128,768]{1,0:T(8,128)(2,1)S(1)} collective-permute-done((bf16[128,768]{1,0:T(8,128)(2,1)S(1)}, bf16[128,768]{1,0:T(8,128)(2,1)S(1)}, u32[]{:S(2)}, u32[]{:S(2)}) %collective-permute-start.12) | collective-permute-done | bytes 196640 | tf_op jit(solution)/shard_map/ppermute | solution.py:413
  171.0 3.1 %collective-permute-done.24 = bf16[96,1024]{1,0:T(8,128)(2,1)S(1)} collective-permute-done((bf16[96,1024]{1,0:T(8,128)(2,1)S(1)}, bf16[96,1024]{1,0:T(8,128)(2,1)S(1)}, u32[]{:S(2)}, u32[]{:S(2)}) %collective-permute-start.24) | collective-permute-done | bytes 196640 | tf_op jit(solution)/shard_map/ppermute | solution.py:413
  174.4 6.7 %collective-permute-done.25 = bf16[96,1024]{1,0:T(8,128)(2,1)S(1)} collective-permute-done((bf16[96,1024]{1,0:T(8,128)(2,1)S(1)}, bf16[96,1024]{1,0:T(8,128)(2,1)S(1)}, u32[]{:S(2)}, u32[]{:S(2)}) %collective-permute-start.25) | collective-permute-done | bytes 196640 | tf_op jit(solution)/shard_map/ppermute | solution.py:413
  183.7 2.4 %shard_map.124 = (bf16[128,2048]{1,0:T(8,128)(2,1)}, bf16[4,128]{1,0:T(4,128)(2,1)}) custom-call(s32[4,128]{1,0:T(4,128)S(1)} %bitcast.123, bf16[4,128]{1,0:T(4,128)(2,1)S(1)} %bitcast.125, bf16[640,2176]{1,0:T(8,128)(2,1)S(1)} %bitcast.95), custom_call_target="tpu_custom_call" | custom-call | flops 335544320 | bytes 2621440 | tf_op jit(solution)/shard_map/pallas_call | solution.py:353
  (126 shorter events, 44.5 us)
Async XLA Ops:
  3.6 42.3 %all-to-all-start = ((bf16[16,40,2048]{2,1,0:T(8,128)(2,1)}), bf16[16,40,2048]{2,1,0:T(8,128)(2,1)}, u32[]{:S(2)}, u32[]{:S(2)}) async-start(bf16[16,40,2048]{2,1,0:T(8,128)(2,1)} %bitcast.128), calls=%async_computation | async-start | bytes 5242880 | tf_op jit(solution)/shard_map/all_to_all | solution.py:375
  45.9 41.7 %all-to-all-start.1 = ((bf16[16,40,2048]{2,1,0:T(8,128)(2,1)}), bf16[16,40,2048]{2,1,0:T(8,128)(2,1)}, u32[]{:S(2)}, u32[]{:S(2)}) async-start(bf16[16,40,2048]{2,1,0:T(8,128)(2,1)} %bitcast.127), calls=%async_computation.1 | async-start | bytes 5242880 | tf_op jit(solution)/shard_map/all_to_all | solution.py:375
  61.6 12.8 %collective-permute-start = (bf16[1024,640]{1,0:T(8,128)(2,1)S(1)}, bf16[1024,640]{1,0:T(8,128)(2,1)}, u32[]{:S(2)}, u32[]{:S(2)}) collective-permute-start(bf16[1024,640]{1,0:T(8,128)(2,1)S(1)} %get-tuple-element.27), channel_id=1, source_target_pairs={{0,16},{16,0},{32,48},{48,32},{64,80},{80,64},{96,112},{112,96},{1... | collective-permute-start | bytes 3932168 | tf_op jit(solution)/shard_map/ppermute | solution.py:398
  87.6 7.8 %collective-permute-start.4 = (bf16[640,2048]{1,0:T(8,128)(2,1)}, bf16[640,2048]{1,0:T(8,128)(2,1)}, u32[]{:S(2)}, u32[]{:S(2)}) collective-permute-start(bf16[640,2048]{1,0:T(8,128)(2,1)} %shard_map.117.dy_ref.a_ref), channel_id=1, source_target_pairs={{0,16},{16,0},{32,48},{48,32},{64,80},{80,64},{96,112},{112,96},{1... | collective-permute-start | bytes 7864328 | tf_op jit(solution)/shard_map/ppermute | solution.py:398
  94.7 9.1 %collective-permute-start.3 = (bf16[640,768]{1,0:T(8,128)(2,1)}, bf16[640,768]{1,0:T(8,128)(2,1)S(1)}, u32[]{:S(2)}, u32[]{:S(2)}) collective-permute-start(bf16[640,768]{1,0:T(8,128)(2,1)} %get-tuple-element.32.a_ref.dg_ref), channel_id=1, source_target_pairs={{0,16},{16,0},{32,48},{48,32},{64,80},{80,64},{96,112},{112,96},{1... | collective-permute-start | bytes 2949128 | tf_op jit(solution)/shard_map/ppermute | solution.py:398
  95.3 15.3 %collective-permute-start.2 = (bf16[640,768]{1,0:T(8,128)(2,1)}, bf16[640,768]{1,0:T(8,128)(2,1)S(1)}, u32[]{:S(2)}, u32[]{:S(2)}) collective-permute-start(bf16[640,768]{1,0:T(8,128)(2,1)} %get-tuple-element.33.a_ref.du_ref), channel_id=1, source_target_pairs={{0,16},{16,0},{32,48},{48,32},{64,80},{80,64},{96,112},{112,96},{1... | collective-permute-start | bytes 2949128 | tf_op jit(solution)/shard_map/ppermute | solution.py:398
  101.8 24.7 %collective-permute-start.5 = (bf16[96,1024]{1,0:T(8,128)(2,1)S(1)}, bf16[96,1024]{1,0:T(8,128)(2,1)S(1)}, u32[]{:S(2)}, u32[]{:S(2)}) collective-permute-start(bf16[96,1024]{1,0:T(8,128)(2,1)S(1)} %dynamic-slice_bitcast_fusion.2), channel_id=1, source_target_pairs={{0,32},{32,64},{64,96},{96,128},{128,160},{160,192},{192,224},{224... | collective-permute-start | bytes 589832 | tf_op jit(solution)/shard_map/ppermute | solution.py:413
  108.4 13.7 %collective-permute-start.6 = (bf16[128,768]{1,0:T(8,128)(2,1)S(1)}, bf16[128,768]{1,0:T(8,128)(2,1)S(1)}, u32[]{:S(2)}, u32[]{:S(2)}) collective-permute-start(bf16[128,768]{1,0:T(8,128)(2,1)S(1)} %dynamic-slice_bitcast_fusion.1), channel_id=1, source_target_pairs={{0,32},{32,64},{64,96},{96,128},{128,160},{160,192},{192,224},{224... | collective-permute-start | bytes 589832 | tf_op jit(solution)/shard_map/ppermute | solution.py:413
  115.3 10.1 %collective-permute-start.7 = (bf16[128,768]{1,0:T(8,128)(2,1)S(1)}, bf16[128,768]{1,0:T(8,128)(2,1)S(1)}, u32[]{:S(2)}, u32[]{:S(2)}) collective-permute-start(bf16[128,768]{1,0:T(8,128)(2,1)S(1)} %dynamic-slice_bitcast_fusion), channel_id=1, source_target_pairs={{0,32},{32,64},{64,96},{96,128},{128,160},{160,192},{192,224},{224... | collective-permute-start | bytes 589832 | tf_op jit(solution)/shard_map/ppermute | solution.py:413
  122.2 15.8 %collective-permute-start.8 = (bf16[128,768]{1,0:T(8,128)(2,1)S(1)}, bf16[128,768]{1,0:T(8,128)(2,1)}, u32[]{:S(2)}, u32[]{:S(2)}) collective-permute-start(bf16[128,768]{1,0:T(8,128)(2,1)S(1)} %fusion.19.refs_2_), channel_id=1, source_target_pairs={{0,32},{32,64},{64,96},{96,128},{128,160},{160,192},{192,224},{224... | collective-permute-start | bytes 589832 | tf_op jit(solution)/shard_map/ppermute | solution.py:413
  125.4 14.8 %collective-permute-start.14 = (bf16[128,768]{1,0:T(8,128)(2,1)S(1)}, bf16[128,768]{1,0:T(8,128)(2,1)}, u32[]{:S(2)}, u32[]{:S(2)}) collective-permute-start(bf16[128,768]{1,0:T(8,128)(2,1)S(1)} %fusion.18.refs_3_), channel_id=1, source_target_pairs={{0,32},{32,64},{64,96},{96,128},{128,160},{160,192},{192,224},{224... | collective-permute-start | bytes 589832 | tf_op jit(solution)/shard_map/ppermute | solution.py:413
  128.2 55.6 %all-to-all-start.2 = ((bf16[16,40,2176]{2,1,0:T(8,128)(2,1)}), bf16[16,40,2176]{2,1,0:T(8,128)(2,1)S(1)}, u32[]{:S(2)}, u32[]{:S(2)}) async-start(bf16[16,40,2176]{2,1,0:T(8,128)(2,1)} %bitcast.96), calls=%async_computation.2 | async-start | bytes 5570560 | tf_op jit(solution)/shard_map/all_to_all | solution.py:375
  136.9 7.0 %collective-permute-start.20 = (bf16[96,1024]{1,0:T(8,128)(2,1)S(1)}, bf16[96,1024]{1,0:T(8,128)(2,1)S(1)}, u32[]{:S(2)}, u32[]{:S(2)}) collective-permute-start(bf16[96,1024]{1,0:T(8,128)(2,1)S(1)} %shard_map.126), channel_id=1, source_target_pairs={{0,32},{32,64},{64,96},{96,128},{128,160},{160,192},{192,224},{224... | collective-permute-start | bytes 589832 | tf_op jit(solution)/shard_map/ppermute | solution.py:413
  139.1 7.0 %collective-permute-start.9 = (bf16[128,768]{1,0:T(8,128)(2,1)S(1)}, bf16[128,768]{1,0:T(8,128)(2,1)S(1)}, u32[]{:S(2)}, u32[]{:S(2)}) collective-permute-start(bf16[128,768]{1,0:T(8,128)(2,1)S(1)} %fusion.17), channel_id=1, source_target_pairs={{0,32},{32,64},{64,96},{96,128},{128,160},{160,192},{192,224},{224... | collective-permute-start | bytes 589832 | tf_op jit(solution)/shard_map/ppermute | solution.py:413
  141.3 7.0 %collective-permute-start.15 = (bf16[128,768]{1,0:T(8,128)(2,1)S(1)}, bf16[128,768]{1,0:T(8,128)(2,1)S(1)}, u32[]{:S(2)}, u32[]{:S(2)}) collective-permute-start(bf16[128,768]{1,0:T(8,128)(2,1)S(1)} %fusion.11), channel_id=1, source_target_pairs={{0,32},{32,64},{64,96},{96,128},{128,160},{160,192},{192,224},{224... | collective-permute-start | bytes 589832 | tf_op jit(solution)/shard_map/ppermute | solution.py:413
  144.9 7.0 %collective-permute-start.21 = (bf16[96,1024]{1,0:T(8,128)(2,1)S(1)}, bf16[96,1024]{1,0:T(8,128)(2,1)S(1)}, u32[]{:S(2)}, u32[]{:S(2)}) collective-permute-start(bf16[96,1024]{1,0:T(8,128)(2,1)S(1)} %fusion.5), channel_id=1, source_target_pairs={{0,32},{32,64},{64,96},{96,128},{128,160},{160,192},{192,224},{224... | collective-permute-start | bytes 589832 | tf_op jit(solution)/shard_map/ppermute | solution.py:413
  147.0 7.0 %collective-permute-start.10 = (bf16[128,768]{1,0:T(8,128)(2,1)S(1)}, bf16[128,768]{1,0:T(8,128)(2,1)S(1)}, u32[]{:S(2)}, u32[]{:S(2)}) collective-permute-start(bf16[128,768]{1,0:T(8,128)(2,1)S(1)} %fusion.16), channel_id=1, source_target_pairs={{0,32},{32,64},{64,96},{96,128},{128,160},{160,192},{192,224},{224... | collective-permute-start | bytes 589832 | tf_op jit(solution)/shard_map/ppermute | solution.py:413
  148.3 7.8 %collective-permute-start.16 = (bf16[128,768]{1,0:T(8,128)(2,1)S(1)}, bf16[128,768]{1,0:T(8,128)(2,1)S(1)}, u32[]{:S(2)}, u32[]{:S(2)}) collective-permute-start(bf16[128,768]{1,0:T(8,128)(2,1)S(1)} %fusion.10), channel_id=1, source_target_pairs={{0,32},{32,64},{64,96},{96,128},{128,160},{160,192},{192,224},{224... | collective-permute-start | bytes 589832 | tf_op jit(solution)/shard_map/ppermute | solution.py:413
  156.2 7.9 %collective-permute-start.17 = (bf16[128,768]{1,0:T(8,128)(2,1)S(1)}, bf16[128,768]{1,0:T(8,128)(2,1)S(1)}, u32[]{:S(2)}, u32[]{:S(2)}) collective-permute-start(bf16[128,768]{1,0:T(8,128)(2,1)S(1)} %fusion.9), channel_id=1, source_target_pairs={{0,32},{32,64},{64,96},{96,128},{128,160},{160,192},{192,224},{224... | collective-permute-start | bytes 589832 | tf_op jit(solution)/shard_map/ppermute | solution.py:413
  158.9 7.3 %collective-permute-start.23 = (bf16[96,1024]{1,0:T(8,128)(2,1)S(1)}, bf16[96,1024]{1,0:T(8,128)(2,1)S(1)}, u32[]{:S(2)}, u32[]{:S(2)}) collective-permute-start(bf16[96,1024]{1,0:T(8,128)(2,1)S(1)} %fusion.3), channel_id=1, source_target_pairs={{0,32},{32,64},{64,96},{96,128},{128,160},{160,192},{192,224},{224... | collective-permute-start | bytes 589832 | tf_op jit(solution)/shard_map/ppermute | solution.py:413
  164.1 10.2 %collective-permute-start.18 = (bf16[128,768]{1,0:T(8,128)(2,1)S(1)}, bf16[128,768]{1,0:T(8,128)(2,1)S(1)}, u32[]{:S(2)}, u32[]{:S(2)}) collective-permute-start(bf16[128,768]{1,0:T(8,128)(2,1)S(1)} %fusion.8), channel_id=1, source_target_pairs={{0,32},{32,64},{64,96},{96,128},{128,160},{160,192},{192,224},{224... | collective-permute-start | bytes 589832 | tf_op jit(solution)/shard_map/ppermute | solution.py:413
  166.2 7.9 %collective-permute-start.24 = (bf16[96,1024]{1,0:T(8,128)(2,1)S(1)}, bf16[96,1024]{1,0:T(8,128)(2,1)S(1)}, u32[]{:S(2)}, u32[]{:S(2)}) collective-permute-start(bf16[96,1024]{1,0:T(8,128)(2,1)S(1)} %fusion.2), channel_id=1, source_target_pairs={{0,32},{32,64},{64,96},{96,128},{128,160},{160,192},{192,224},{224... | collective-permute-start | bytes 589832 | tf_op jit(solution)/shard_map/ppermute | solution.py:413
  170.9 10.4 %collective-permute-start.13 = (bf16[128,768]{1,0:T(8,128)(2,1)S(1)}, bf16[128,768]{1,0:T(8,128)(2,1)S(1)}, u32[]{:S(2)}, u32[]{:S(2)}) collective-permute-start(bf16[128,768]{1,0:T(8,128)(2,1)S(1)} %fusion.13), channel_id=1, source_target_pairs={{0,32},{32,64},{64,96},{96,128},{128,160},{160,192},{192,224},{224... | collective-permute-start | bytes 589832 | tf_op jit(solution)/shard_map/ppermute | solution.py:413
  174.3 11.8 %collective-permute-start.19 = (bf16[128,768]{1,0:T(8,128)(2,1)S(1)}, bf16[128,768]{1,0:T(8,128)(2,1)S(1)}, u32[]{:S(2)}, u32[]{:S(2)}) collective-permute-start(bf16[128,768]{1,0:T(8,128)(2,1)S(1)} %fusion.7), channel_id=1, source_target_pairs={{0,32},{32,64},{64,96},{96,128},{128,160},{160,192},{192,224},{224... | collective-permute-start | bytes 589832 | tf_op jit(solution)/shard_map/ppermute | solution.py:413
  (29 other events, 207.0 us)

commit v3 on v2

--- a/solution.py
+++ b/solution.py
@@ -324,7 +324,8 @@
     )(own_t, other_t, own, other, after)
 
 
-def combine_kernel(ids_hbm, gates_hbm, rows_hbm, tok_hbm, gate_hbm, ids, gates, rows, extra, tok, gate, sems, out_sems):
+def combine_kernel(ids_hbm, gates_hbm, rows_hbm, tok_hbm, gate_hbm, flag_ref, ids, gates, rows, extra, tok, gate, sems, out_sems):
+    flag_ref[...] = jnp.zeros_like(flag_ref)
     few = [start(sems, 0, ids_hbm, ids), start(sems, 1, gates_hbm, gates)]
     extra_load = start(sems, 2, rows_hbm.at[:, pl.ds(D, EXTRA)], extra)
     loads = [start(sems, 3 + n, rows_hbm.at[:, pl.ds(n * Q, Q)], rows.at[n]) for n in range(4)]
@@ -353,8 +354,8 @@
     return pl.pallas_call(
         combine_kernel,
         in_specs=[ANY] * 3,
-        out_specs=[ANY] * 2,
-        out_shape=[shape(N_TOK, D), shape(4, N_TOK)],
+        out_specs=[ANY, ANY, pl.BlockSpec(memory_space=pltpu.VMEM)],
+        out_shape=[shape(N_TOK, D), shape(4, N_TOK), shape(16, 128)],
         scratch_shapes=[
             vmem(4, N_TOK, dtype=jnp.int32),
             vmem(4, N_TOK),
@@ -443,7 +444,7 @@
     part_down, flag = outer_sum(hidden_t, hidden_other_t, dy, dy_other, H, H, me)
     part_gate, flag = outer_sum(x_own, x_other, d_gate, d_gate_other, 0, FF, flag)
     part_up, flag = outer_sum(x_own, x_other, d_up, d_up_other, 0, FF, flag)
-    pairs, flag = pair_grads(d_gate, d_up, gate_t, up_t, prob, flag)
+    pairs, _ = pair_grads(d_gate, d_up, gate_t, up_t, prob, flag)
 
     part_down = part_down.reshape(N_Z, FF // N_Z, H)
     part_gate = part_gate.reshape(N_Z, D // (2 * N_Z), FF)
@@ -453,12 +454,12 @@
     sum_up = ring_step(part_up, None, z, sign, 1)
     pairs = hold(pairs, sum_down, sum_gate, sum_up, mib=1)
     back_rows = exchange_experts(pairs)
-    token_grad, gate_grad_t = combine(ids_t, gates_t, back_rows)
-    sum_down = hold(sum_down, flag)
+    token_grad, gate_grad_t, flag = combine(ids_t, gates_t, back_rows)
     for step in range(2, N_Z):
         sum_down = ring_step(part_down, sum_down, z, sign, step)
-        sum_gate = ring_step(part_gate, sum_gate, z, sign, step)
-        sum_up = ring_step(part_up, sum_up, z, sign, step, gate_grad_t if step == 7 else None)
+        last = flag if step == 7 else None
+        sum_gate = ring_step(part_gate, sum_gate, z, sign, step, last)
+        sum_up = ring_step(part_up, sum_up, z, sign, step, last)
 
     halves = sum_down.reshape(2, FF // (2 * N_Z), H)
     mine = pick(halves, core)

time: 191 us -> 192 us (level); the launches traced: 188 us -> 192 us
    unnamed x46 -> x44, local copies, waits for them, and re-layouts: 8.54 us -> 7.89 us
  transfers between devices with their start and end apart: 30 -> 30, of which waited for: 16 -> 14; matrix products, arithmetic and copies ran while one was open for 5% -> 6% of each run, Pallas kernels for 29% -> 29%
where the time goes in v3:
time: 192 us
  waiting for transfers between devices  68.4 us (36%)
  Pallas kernels  58.9 us (31%)
  starting transfers between devices  41.6 us (22%)
  other arithmetic  13.5 us (7%)
  local copies, waits for them, and re-layouts  7.97 us (4%)
    ppermute x21, waiting for transfers between devices, ring_step(): came = lax.ppermute(held, 'dp', ROUTE)  33.8 us
    all_to_all x3, waiting for transfers between devices, exchange_experts(): lax.all_to_all(rows.reshape(N_EXP, CAP, width), 'expert', split_axis=0, c...  33.2 us
    all_to_all x3, starting transfers between devices, exchange_experts(): lax.all_to_all(rows.reshape(N_EXP, CAP, width), 'expert', split_axis=0, c...  25.8 us
    ppermute x21, starting transfers between devices, ring_step(): came = lax.ppermute(held, 'dp', ROUTE)  14.5 us
    pallas_call x3, Pallas kernels, outer_sum(): pl.pallas_call(outer_kernel, grid=(n // width,), in_specs=[left, left, pl...  14.2 us
    convert_element_type x19, other arithmetic, ring_step(): return (came.astype(F32) + block.astype(F32)).astype(BF16)  9.51 us
    unnamed x44, local copies, waits for them, and re-layouts  7.89 us
    pallas_call x1, Pallas kernels, forward(): pl.pallas_call(forward_kernel, grid=(3,), in_specs=[pl.BlockSpec((ROWS, D...  7.12 us
  transfers between devices with their start and end apart: 30, of which 14 were waited for; matrix products, arithmetic and copies ran while one was open for 6% of the time, Pallas kernels for 29%

profile of v3, /device:TPU:2, one launch (start us, length us, event | category | flops | bytes accessed | tf_op | source)
XLA Modules:
  0.0 191.6 jit_solution(5388347014966508081)
XLA Ops:
  0.6 2.9 %shard_map.111 = bf16[640,2048]{1,0:T(8,128)(2,1)} custom-call(s32[1]{0:T(128)} %bitcast.3.core_ref, s32[4,128]{1,0:T(4,128)} %bitcast.121, bf16[128,2048]{1,0:T(8,128)(2,1)} %x_hbm.3), custom_call_target="tpu_custom_call" | custom-call | flops 335544320 | bytes 2621440 | tf_op jit(solution)/shard_map/pallas_call | solution.py:113
  3.6 7.5 %all-to-all-start = ((bf16[16,40,2048]{2,1,0:T(8,128)(2,1)}), bf16[16,40,2048]{2,1,0:T(8,128)(2,1)}, u32[]{:S(2)}, u32[]{:S(2)}) async-start(bf16[16,40,2048]{2,1,0:T(8,128)(2,1)} %bitcast.127), calls=%async_computation | async-start | bytes 5242880 | tf_op jit(solution)/shard_map/all_to_all | solution.py:376
  11.1 5.8 %shard_map.112.refs_2_.wd_ref = bf16[3,2048,256]{2,1,0:T(8,128)(2,1)} custom-call(s32[1]{0:T(128)} %bitcast.3.core_ref, bf16[1,768,2048]{2,1,0:T(8,128)(2,1)} %w_ref.1), custom_call_target="tpu_custom_call" | custom-call | bytes 6291456 | tf_op jit(solution)/shard_map/pallas_call | solution.py:137
  16.8 6.1 %shard_map.113 = (bf16[4,768,512]{2,1,0:T(8,128)(2,1)}, bf16[4,768,512]{2,1,0:T(8,128)(2,1)}) custom-call(bf16[1,2048,768]{2,1,0:T(8,128)(2,1)} %wg_ref.1, bf16[1,2048,768]{2,1,0:T(8,128)(2,1)} %wu_ref.1), custom_call_target="tpu_custom_call" | custom-call | bytes 12582912 | tf_op jit(solution)/shard_map/pallas_call | solution.py:160
  22.9 2.9 %shard_map.110.refs_0_ = bf16[640,2048]{1,0:T(8,128)(2,1)} custom-call(s32[1]{0:T(128)} %bitcast.3.core_ref, s32[4,128]{1,0:T(4,128)} %bitcast.122, bf16[4,128]{1,0:T(4,128)(2,1)} %bitcast.124, bf16[128,2048]{1,0:T(8,128)(2,1)} %x_hbm.2), custom_call_target="tpu_custom_call" | custom-call | flops 335544320 | bytes 2621440 | tf_op jit(solution)/shard_map/pallas_call | solution.py:113
  25.9 20.0 %all-to-all-done = bf16[16,40,2048]{2,1,0:T(8,128)(2,1)} async-done(((bf16[16,40,2048]{2,1,0:T(8,128)(2,1)}), bf16[16,40,2048]{2,1,0:T(8,128)(2,1)}, u32[]{:S(2)}, u32[]{:S(2)}) %all-to-all-start) | async-done | bytes 2621472 | tf_op jit(solution)/shard_map/all_to_all | solution.py:376
  45.9 9.6 %all-to-all-start.1 = ((bf16[16,40,2048]{2,1,0:T(8,128)(2,1)}), bf16[16,40,2048]{2,1,0:T(8,128)(2,1)}, u32[]{:S(2)}, u32[]{:S(2)}) async-start(bf16[16,40,2048]{2,1,0:T(8,128)(2,1)} %bitcast.126), calls=%async_computation.1 | async-start | bytes 5242880 | tf_op jit(solution)/shard_map/all_to_all | solution.py:376
  55.5 5.0 %shard_map.115 = (bf16[1024,640]{1,0:T(8,128)(2,1)S(1)}, bf16[1024,640]{1,0:T(8,128)(2,1)S(1)}) custom-call(s32[1]{0:T(128)} %bitcast.3.core_ref, bf16[640,2048]{1,0:T(8,128)(2,1)} %bitcast.5.refs_1_.mine_ref.theirs_ref.x_ref, bf16[640,2048]{1,0:T(8,128)(2,1)} %bitcast.5.refs_1_.mine_ref.theirs_ref.x_ref), custom_call_target="tpu_custom_call" | custom-call | bytes 5242880 | tf_op jit(solution)/shard_map/pallas_call | solution.py:205
  61.6 7.1 %shard_map.116 = (bf16[768,640]{1,0:T(8,128)(2,1)S(1)}, bf16[3,640,256]{2,1,0:T(8,128)(2,1)S(1)}, bf16[3,640,256]{2,1,0:T(8,128)(2,1)S(1)}, bf16[3,640,256]{2,1,0:T(8,128)(2,1)S(1)}) custom-call(bf16[640,2048]{1,0:T(8,128)(2,1)} %bitcast.5.refs_1_.mine_ref.theirs_ref.x_ref, bf16[1,2048,768]{2,1,0:T(8,128)(2,1)S(1)} %copy-done.2, ...), custom_call_target="tpu_custom_call" | custom-call | flops 4026531840 | bytes 13000000 | tf_op jit(solution)/shard_map/pallas_call | solution.py:187
  74.5 13.2 %all-to-all-done.1 = bf16[16,40,2048]{2,1,0:T(8,128)(2,1)} async-done(((bf16[16,40,2048]{2,1,0:T(8,128)(2,1)}), bf16[16,40,2048]{2,1,0:T(8,128)(2,1)}, u32[]{:S(2)}, u32[]{:S(2)}) %all-to-all-start.1) | async-done | bytes 2621472 | tf_op jit(solution)/shard_map/all_to_all | solution.py:376
  87.6 7.1 %shard_map.118 = (bf16[640,768]{1,0:T(8,128)(2,1)}, bf16[640,768]{1,0:T(8,128)(2,1)}, bf16[640,128]{1,0:T(8,128)(2,1)}) custom-call(s32[1]{0:T(128)} %bitcast.2.me_ref.after_ref, bf16[640,2048]{1,0:T(8,128)(2,1)} %shard_map.117.dy_ref.a_ref, bf16[3,2048,256]{2,1,0:T(8,128)(2,1)} %shard_map.112.refs_2_.wd_ref, bf16[3,640,256]{2,1,0:T(8,128)(2,1)} %copy-done.9, ...), custom_call_target="tpu_custom_call" | custom-call | flops 2013265920 | bytes 11000000 | tf_op jit(solution)/shard_map/pallas_call | solution.py:251
  96.8 5.0 %shard_map.119 = (bf16[768,1024]{1,0:T(8,128)(2,1)S(1)}, bf16[16,128]{1,0:T(8,128)(2,1)S(1)}) custom-call(bf16[768,640]{1,0:T(8,128)(2,1)S(1)} %copy-done.20, bf16[768,640]{1,0:T(8,128)(2,1)} %collective-permute-done.1.refs_2_.bt_ref, bf16[640,2048]{1,0:T(8,128)(2,1)} %shard_map.117.dy_ref.a_ref, bf16[640,2048]{1,0:T(8,128)(2,1)} %collective-permute-done.4.b_ref, ...), custom_call_target="tpu_custom_call" | custom-call | flops 2013265920 | bytes 6160384 | tf_op jit(solution)/shard_map/pallas_call | solution.py:307
  103.8 4.5 %shard_map.120 = (bf16[1024,768]{1,0:T(8,128)(2,1)S(1)}, bf16[16,128]{1,0:T(8,128)(2,1)S(1)}) custom-call(bf16[1024,640]{1,0:T(8,128)(2,1)S(1)} %copy-done.16, bf16[1024,640]{1,0:T(8,128)(2,1)} %collective-permute-done.refs_1_.bt_ref, bf16[640,768]{1,0:T(8,128)(2,1)S(1)} %copy-done.17, bf16[640,768]{1,0:T(8,128)(2,1)S(1)} %collective-permute-done.3.b_ref, ...), custom_call_target="tpu_custom_call" | custom-call | flops 2013265920 | bytes 6160384 | tf_op jit(solution)/shard_map/pallas_call | solution.py:307
  110.6 4.6 %shard_map.121 = (bf16[1024,768]{1,0:T(8,128)(2,1)S(1)}, bf16[16,128]{1,0:T(8,128)(2,1)S(1)}) custom-call(bf16[1024,640]{1,0:T(8,128)(2,1)S(1)} %copy-done.16, bf16[1024,640]{1,0:T(8,128)(2,1)} %collective-permute-done.refs_1_.bt_ref, bf16[640,768]{1,0:T(8,128)(2,1)S(1)} %copy-done.18, bf16[640,768]{1,0:T(8,128)(2,1)S(1)} %collective-permute-done.2.b_ref, ...), custom_call_target="tpu_custom_call" | custom-call | flops 2013265920 | bytes 6160384 | tf_op jit(solution)/shard_map/pallas_call | solution.py:307
  117.3 5.4 %shard_map.122 = (bf16[640,2176]{1,0:T(8,128)(2,1)S(1)}, bf16[16,128]{1,0:T(8,128)(2,1)}) custom-call(bf16[640,768]{1,0:T(8,128)(2,1)S(1)} %copy-done.17, bf16[640,768]{1,0:T(8,128)(2,1)S(1)} %copy-done.18, bf16[4,768,512]{2,1,0:T(8,128)(2,1)S(1)} %copy-done.14, bf16[4,768,512]{2,1,0:T(8,128)(2,1)S(1)} %copy-done.1, bf16[640,128]{1,0:T(8,128)(2,1)S(1)} %copy-done.21, ...), custom_call_target="tpu_custom_call" | custom-call | flops 4026531840 | bytes 12000000 | tf_op jit(solution)/shard_map/pallas_call | solution.py:284
  122.7 3.2 %collective-permute-start.8 = (bf16[128,768]{1,0:T(8,128)(2,1)S(1)}, bf16[128,768]{1,0:T(8,128)(2,1)}, u32[]{:S(2)}, u32[]{:S(2)}) collective-permute-start(bf16[128,768]{1,0:T(8,128)(2,1)S(1)} %fusion.19.refs_2_), channel_id=1, source_target_pairs={{0,32},{32,64},{64,96},{96,128},{128,160},{160,192},{192,224},{224... | collective-permute-start | bytes 589832 | tf_op jit(solution)/shard_map/ppermute | solution.py:414
  129.8 8.7 %all-to-all-start.2 = ((bf16[16,40,2176]{2,1,0:T(8,128)(2,1)}), bf16[16,40,2176]{2,1,0:T(8,128)(2,1)S(1)}, u32[]{:S(2)}, u32[]{:S(2)}) async-start(bf16[16,40,2176]{2,1,0:T(8,128)(2,1)} %bitcast.96), calls=%async_computation.2 | async-start | bytes 5570560 | tf_op jit(solution)/shard_map/all_to_all | solution.py:376
  143.8 2.9 %collective-permute-done.9 = bf16[128,768]{1,0:T(8,128)(2,1)S(1)} collective-permute-done((bf16[128,768]{1,0:T(8,128)(2,1)S(1)}, bf16[128,768]{1,0:T(8,128)(2,1)S(1)}, u32[]{:S(2)}, u32[]{:S(2)}) %collective-permute-start.9) | collective-permute-done | bytes 196640 | tf_op jit(solution)/shard_map/ppermute | solution.py:414
  153.9 3.0 %collective-permute-done.16 = bf16[128,768]{1,0:T(8,128)(2,1)S(1)} collective-permute-done((bf16[128,768]{1,0:T(8,128)(2,1)S(1)}, bf16[128,768]{1,0:T(8,128)(2,1)S(1)}, u32[]{:S(2)}, u32[]{:S(2)}) %collective-permute-start.16) | collective-permute-done | bytes 196640 | tf_op jit(solution)/shard_map/ppermute | solution.py:414
  161.2 5.7 %collective-permute-done.23 = bf16[96,1024]{1,0:T(8,128)(2,1)S(1)} collective-permute-done((bf16[96,1024]{1,0:T(8,128)(2,1)S(1)}, bf16[96,1024]{1,0:T(8,128)(2,1)S(1)}, u32[]{:S(2)}, u32[]{:S(2)}) %collective-permute-start.23) | collective-permute-done | bytes 196640 | tf_op jit(solution)/shard_map/ppermute | solution.py:414
  168.2 5.8 %collective-permute-done.24 = bf16[96,1024]{1,0:T(8,128)(2,1)S(1)} collective-permute-done((bf16[96,1024]{1,0:T(8,128)(2,1)S(1)}, bf16[96,1024]{1,0:T(8,128)(2,1)S(1)}, u32[]{:S(2)}, u32[]{:S(2)}) %collective-permute-start.24) | collective-permute-done | bytes 196640 | tf_op jit(solution)/shard_map/ppermute | solution.py:414
  174.2 6.7 %collective-permute-done.25 = bf16[96,1024]{1,0:T(8,128)(2,1)S(1)} collective-permute-done((bf16[96,1024]{1,0:T(8,128)(2,1)S(1)}, bf16[96,1024]{1,0:T(8,128)(2,1)S(1)}, u32[]{:S(2)}, u32[]{:S(2)}) %collective-permute-start.25) | collective-permute-done | bytes 196640 | tf_op jit(solution)/shard_map/ppermute | solution.py:414
  183.5 2.4 %shard_map.124 = (bf16[128,2048]{1,0:T(8,128)(2,1)}, bf16[4,128]{1,0:T(4,128)(2,1)}, bf16[16,128]{1,0:T(8,128)(2,1)S(1)}) custom-call(s32[4,128]{1,0:T(4,128)S(1)} %bitcast.123, bf16[4,128]{1,0:T(4,128)(2,1)S(1)} %bitcast.125, bf16[640,2176]{1,0:T(8,128)(2,1)S(1)} %bitcast.95), custom_call_target="tpu_custom_call" | custom-call | flops 335544320 | bytes 2621440 | tf_op jit(solution)/shard_map/pallas_call | solution.py:354
  187.6 2.3 %collective-permute-done.19.refs_0_ = bf16[128,768]{1,0:T(8,128)(2,1)S(1)} collective-permute-done((bf16[128,768]{1,0:T(8,128)(2,1)}, bf16[128,768]{1,0:T(8,128)(2,1)S(1)}, u32[]{:S(2)}, u32[]{:S(2)}) %collective-permute-start.19) | collective-permute-done | bytes 196640 | tf_op jit(solution)/shard_map/ppermute | solution.py:414
  (124 shorter events, 42.9 us)
Async XLA Ops:
  3.6 42.3 %all-to-all-start = ((bf16[16,40,2048]{2,1,0:T(8,128)(2,1)}), bf16[16,40,2048]{2,1,0:T(8,128)(2,1)}, u32[]{:S(2)}, u32[]{:S(2)}) async-start(bf16[16,40,2048]{2,1,0:T(8,128)(2,1)} %bitcast.127), calls=%async_computation | async-start | bytes 5242880 | tf_op jit(solution)/shard_map/all_to_all | solution.py:376
  45.9 41.7 %all-to-all-start.1 = ((bf16[16,40,2048]{2,1,0:T(8,128)(2,1)}), bf16[16,40,2048]{2,1,0:T(8,128)(2,1)}, u32[]{:S(2)}, u32[]{:S(2)}) async-start(bf16[16,40,2048]{2,1,0:T(8,128)(2,1)} %bitcast.126), calls=%async_computation.1 | async-start | bytes 5242880 | tf_op jit(solution)/shard_map/all_to_all | solution.py:376
  61.6 12.8 %collective-permute-start = (bf16[1024,640]{1,0:T(8,128)(2,1)S(1)}, bf16[1024,640]{1,0:T(8,128)(2,1)}, u32[]{:S(2)}, u32[]{:S(2)}) collective-permute-start(bf16[1024,640]{1,0:T(8,128)(2,1)S(1)} %get-tuple-element.27), channel_id=1, source_target_pairs={{0,16},{16,0},{32,48},{48,32},{64,80},{80,64},{96,112},{112,96},{1... | collective-permute-start | bytes 3932168 | tf_op jit(solution)/shard_map/ppermute | solution.py:399
  87.6 7.8 %collective-permute-start.4 = (bf16[640,2048]{1,0:T(8,128)(2,1)}, bf16[640,2048]{1,0:T(8,128)(2,1)}, u32[]{:S(2)}, u32[]{:S(2)}) collective-permute-start(bf16[640,2048]{1,0:T(8,128)(2,1)} %shard_map.117.dy_ref.a_ref), channel_id=1, source_target_pairs={{0,16},{16,0},{32,48},{48,32},{64,80},{80,64},{96,112},{112,96},{1... | collective-permute-start | bytes 7864328 | tf_op jit(solution)/shard_map/ppermute | solution.py:399
  94.7 9.1 %collective-permute-start.3 = (bf16[640,768]{1,0:T(8,128)(2,1)}, bf16[640,768]{1,0:T(8,128)(2,1)S(1)}, u32[]{:S(2)}, u32[]{:S(2)}) collective-permute-start(bf16[640,768]{1,0:T(8,128)(2,1)} %get-tuple-element.32.a_ref.dg_ref), channel_id=1, source_target_pairs={{0,16},{16,0},{32,48},{48,32},{64,80},{80,64},{96,112},{112,96},{1... | collective-permute-start | bytes 2949128 | tf_op jit(solution)/shard_map/ppermute | solution.py:399
  95.3 15.3 %collective-permute-start.2 = (bf16[640,768]{1,0:T(8,128)(2,1)}, bf16[640,768]{1,0:T(8,128)(2,1)S(1)}, u32[]{:S(2)}, u32[]{:S(2)}) collective-permute-start(bf16[640,768]{1,0:T(8,128)(2,1)} %get-tuple-element.33.a_ref.du_ref), channel_id=1, source_target_pairs={{0,16},{16,0},{32,48},{48,32},{64,80},{80,64},{96,112},{112,96},{1... | collective-permute-start | bytes 2949128 | tf_op jit(solution)/shard_map/ppermute | solution.py:399
  101.8 25.3 %collective-permute-start.5 = (bf16[96,1024]{1,0:T(8,128)(2,1)S(1)}, bf16[96,1024]{1,0:T(8,128)(2,1)S(1)}, u32[]{:S(2)}, u32[]{:S(2)}) collective-permute-start(bf16[96,1024]{1,0:T(8,128)(2,1)S(1)} %dynamic-slice_bitcast_fusion.2), channel_id=1, source_target_pairs={{0,32},{32,64},{64,96},{96,128},{128,160},{160,192},{192,224},{224... | collective-permute-start | bytes 589832 | tf_op jit(solution)/shard_map/ppermute | solution.py:414
  108.4 14.3 %collective-permute-start.6 = (bf16[128,768]{1,0:T(8,128)(2,1)S(1)}, bf16[128,768]{1,0:T(8,128)(2,1)S(1)}, u32[]{:S(2)}, u32[]{:S(2)}) collective-permute-start(bf16[128,768]{1,0:T(8,128)(2,1)S(1)} %dynamic-slice_bitcast_fusion.1), channel_id=1, source_target_pairs={{0,32},{32,64},{64,96},{96,128},{128,160},{160,192},{192,224},{224... | collective-permute-start | bytes 589832 | tf_op jit(solution)/shard_map/ppermute | solution.py:414
  115.3 10.6 %collective-permute-start.7 = (bf16[128,768]{1,0:T(8,128)(2,1)S(1)}, bf16[128,768]{1,0:T(8,128)(2,1)S(1)}, u32[]{:S(2)}, u32[]{:S(2)}) collective-permute-start(bf16[128,768]{1,0:T(8,128)(2,1)S(1)} %dynamic-slice_bitcast_fusion), channel_id=1, source_target_pairs={{0,32},{32,64},{64,96},{96,128},{128,160},{160,192},{192,224},{224... | collective-permute-start | bytes 589832 | tf_op jit(solution)/shard_map/ppermute | solution.py:414
  122.7 15.8 %collective-permute-start.8 = (bf16[128,768]{1,0:T(8,128)(2,1)S(1)}, bf16[128,768]{1,0:T(8,128)(2,1)}, u32[]{:S(2)}, u32[]{:S(2)}) collective-permute-start(bf16[128,768]{1,0:T(8,128)(2,1)S(1)} %fusion.19.refs_2_), channel_id=1, source_target_pairs={{0,32},{32,64},{64,96},{96,128},{128,160},{160,192},{192,224},{224... | collective-permute-start | bytes 589832 | tf_op jit(solution)/shard_map/ppermute | solution.py:414
  126.0 14.9 %collective-permute-start.14 = (bf16[128,768]{1,0:T(8,128)(2,1)S(1)}, bf16[128,768]{1,0:T(8,128)(2,1)}, u32[]{:S(2)}, u32[]{:S(2)}) collective-permute-start(bf16[128,768]{1,0:T(8,128)(2,1)S(1)} %fusion.18.refs_3_), channel_id=1, source_target_pairs={{0,32},{32,64},{64,96},{96,128},{128,160},{160,192},{192,224},{224... | collective-permute-start | bytes 589832 | tf_op jit(solution)/shard_map/ppermute | solution.py:414
  127.2 15.3 %collective-permute-start.20 = (bf16[96,1024]{1,0:T(8,128)(2,1)S(1)}, bf16[96,1024]{1,0:T(8,128)(2,1)}, u32[]{:S(2)}, u32[]{:S(2)}) collective-permute-start(bf16[96,1024]{1,0:T(8,128)(2,1)S(1)} %fusion.20.refs_1_), channel_id=1, source_target_pairs={{0,32},{32,64},{64,96},{96,128},{128,160},{160,192},{192,224},{224... | collective-permute-start | bytes 589832 | tf_op jit(solution)/shard_map/ppermute | solution.py:414
  129.8 53.7 %all-to-all-start.2 = ((bf16[16,40,2176]{2,1,0:T(8,128)(2,1)}), bf16[16,40,2176]{2,1,0:T(8,128)(2,1)S(1)}, u32[]{:S(2)}, u32[]{:S(2)}) async-start(bf16[16,40,2176]{2,1,0:T(8,128)(2,1)} %bitcast.96), calls=%async_computation.2 | async-start | bytes 5570560 | tf_op jit(solution)/shard_map/all_to_all | solution.py:376
  139.7 7.0 %collective-permute-start.9 = (bf16[128,768]{1,0:T(8,128)(2,1)S(1)}, bf16[128,768]{1,0:T(8,128)(2,1)S(1)}, u32[]{:S(2)}, u32[]{:S(2)}) collective-permute-start(bf16[128,768]{1,0:T(8,128)(2,1)S(1)} %fusion.17), channel_id=1, source_target_pairs={{0,32},{32,64},{64,96},{96,128},{128,160},{160,192},{192,224},{224... | collective-permute-start | bytes 589832 | tf_op jit(solution)/shard_map/ppermute | solution.py:414
  141.9 7.0 %collective-permute-start.15 = (bf16[128,768]{1,0:T(8,128)(2,1)S(1)}, bf16[128,768]{1,0:T(8,128)(2,1)S(1)}, u32[]{:S(2)}, u32[]{:S(2)}) collective-permute-start(bf16[128,768]{1,0:T(8,128)(2,1)S(1)} %fusion.11), channel_id=1, source_target_pairs={{0,32},{32,64},{64,96},{96,128},{128,160},{160,192},{192,224},{224... | collective-permute-start | bytes 589832 | tf_op jit(solution)/shard_map/ppermute | solution.py:414
  143.5 7.5 %collective-permute-start.21 = (bf16[96,1024]{1,0:T(8,128)(2,1)S(1)}, bf16[96,1024]{1,0:T(8,128)(2,1)S(1)}, u32[]{:S(2)}, u32[]{:S(2)}) collective-permute-start(bf16[96,1024]{1,0:T(8,128)(2,1)S(1)} %fusion.5), channel_id=1, source_target_pairs={{0,32},{32,64},{64,96},{96,128},{128,160},{160,192},{192,224},{224... | collective-permute-start | bytes 589832 | tf_op jit(solution)/shard_map/ppermute | solution.py:414
  152.0 7.0 %collective-permute-start.22 = (bf16[96,1024]{1,0:T(8,128)(2,1)S(1)}, bf16[96,1024]{1,0:T(8,128)(2,1)S(1)}, u32[]{:S(2)}, u32[]{:S(2)}) collective-permute-start(bf16[96,1024]{1,0:T(8,128)(2,1)S(1)} %fusion.4), channel_id=1, source_target_pairs={{0,32},{32,64},{64,96},{96,128},{128,160},{160,192},{192,224},{224... | collective-permute-start | bytes 589832 | tf_op jit(solution)/shard_map/ppermute | solution.py:414
  153.8 7.3 %collective-permute-start.11 = (bf16[128,768]{1,0:T(8,128)(2,1)S(1)}, bf16[128,768]{1,0:T(8,128)(2,1)S(1)}, u32[]{:S(2)}, u32[]{:S(2)}) collective-permute-start(bf16[128,768]{1,0:T(8,128)(2,1)S(1)} %fusion.15), channel_id=1, source_target_pairs={{0,32},{32,64},{64,96},{96,128},{128,160},{160,192},{192,224},{224... | collective-permute-start | bytes 589832 | tf_op jit(solution)/shard_map/ppermute | solution.py:414
  157.8 9.2 %collective-permute-start.17 = (bf16[128,768]{1,0:T(8,128)(2,1)S(1)}, bf16[128,768]{1,0:T(8,128)(2,1)S(1)}, u32[]{:S(2)}, u32[]{:S(2)}) collective-permute-start(bf16[128,768]{1,0:T(8,128)(2,1)S(1)} %fusion.9), channel_id=1, source_target_pairs={{0,32},{32,64},{64,96},{96,128},{128,160},{160,192},{192,224},{224... | collective-permute-start | bytes 589832 | tf_op jit(solution)/shard_map/ppermute | solution.py:414
  159.0 7.9 %collective-permute-start.23 = (bf16[96,1024]{1,0:T(8,128)(2,1)S(1)}, bf16[96,1024]{1,0:T(8,128)(2,1)S(1)}, u32[]{:S(2)}, u32[]{:S(2)}) collective-permute-start(bf16[96,1024]{1,0:T(8,128)(2,1)S(1)} %fusion.3), channel_id=1, source_target_pairs={{0,32},{32,64},{64,96},{96,128},{128,160},{160,192},{192,224},{224... | collective-permute-start | bytes 589832 | tf_op jit(solution)/shard_map/ppermute | solution.py:414
  161.1 13.0 %collective-permute-start.12 = (bf16[128,768]{1,0:T(8,128)(2,1)S(1)}, bf16[128,768]{1,0:T(8,128)(2,1)S(1)}, u32[]{:S(2)}, u32[]{:S(2)}) collective-permute-start(bf16[128,768]{1,0:T(8,128)(2,1)S(1)} %fusion.14), channel_id=1, source_target_pairs={{0,32},{32,64},{64,96},{96,128},{128,160},{160,192},{192,224},{224... | collective-permute-start | bytes 589832 | tf_op jit(solution)/shard_map/ppermute | solution.py:414
  168.1 13.1 %collective-permute-start.18 = (bf16[128,768]{1,0:T(8,128)(2,1)S(1)}, bf16[128,768]{1,0:T(8,128)(2,1)S(1)}, u32[]{:S(2)}, u32[]{:S(2)}) collective-permute-start(bf16[128,768]{1,0:T(8,128)(2,1)S(1)} %fusion.8), channel_id=1, source_target_pairs={{0,32},{32,64},{64,96},{96,128},{128,160},{160,192},{192,224},{224... | collective-permute-start | bytes 589832 | tf_op jit(solution)/shard_map/ppermute | solution.py:414
  174.1 11.8 %collective-permute-start.13 = (bf16[128,768]{1,0:T(8,128)(2,1)S(1)}, bf16[128,768]{1,0:T(8,128)(2,1)S(1)}, u32[]{:S(2)}, u32[]{:S(2)}) collective-permute-start(bf16[128,768]{1,0:T(8,128)(2,1)S(1)} %fusion.13), channel_id=1, source_target_pairs={{0,32},{32,64},{64,96},{96,128},{128,160},{160,192},{192,224},{224... | collective-permute-start | bytes 589832 | tf_op jit(solution)/shard_map/ppermute | solution.py:414
  182.8 7.1 %collective-permute-start.19 = (bf16[128,768]{1,0:T(8,128)(2,1)}, bf16[128,768]{1,0:T(8,128)(2,1)S(1)}, u32[]{:S(2)}, u32[]{:S(2)}) collective-permute-start(bf16[128,768]{1,0:T(8,128)(2,1)} %fusion.7), channel_id=1, source_target_pairs={{0,32},{32,64},{64,96},{96,128},{128,160},{160,192},{192,224},{224... | collective-permute-start | bytes 589832 | tf_op jit(solution)/shard_map/ppermute | solution.py:414
  (28 other events, 210.6 us)

commit v4 on v3

--- a/solution.py
+++ b/solution.py
@@ -267,7 +267,8 @@
     )(me, dy, wd_t, h, f, a)
 
 
-def pair_kernel(dg_ref, du_ref, wg_ref, wu_ref, gg_ref, after_ref, out_ref, flag_ref):
+def pair_kernel(dg_ref, du_ref, wg_ref, wu_ref, gg_ref, *refs):
+    out_ref, flag_ref = refs[-2:]
     n = pl.program_id(0)
     value = dot(dg_ref[...], wg_ref[0]) + dot(du_ref[...], wu_ref[0])
     out_ref[:, pl.ds(pl.multiple_of(n * Q, Q), Q)] = value.astype(BF16)
@@ -278,13 +279,14 @@
         out_ref[:, D:] = gg_ref[...]
 
 
-def pair_grads(dg, du, wg_t, wu_t, gg, after):
+def pair_grads(dg, du, wg_t, wu_t, gg, *after):
     whole = pl.BlockSpec((ROWS, FF), lambda n: (0, 0))
     weight = pl.BlockSpec((1, FF, Q), lambda n: (n, 0, 0))
     return pl.pallas_call(
         pair_kernel,
         grid=(4,),
-        in_specs=[whole, whole, weight, weight, pl.BlockSpec((ROWS, EXTRA), lambda n: (0, 0)), ANY],
+        in_specs=[whole, whole, weight, weight, pl.BlockSpec((ROWS, EXTRA), lambda n: (0, 0))]
+        + [ANY] * len(after),
         out_specs=[
             pl.BlockSpec((ROWS, D + EXTRA), lambda n: (0, 0)),
             pl.BlockSpec((16, 128), lambda n: (0, 0)),
@@ -292,16 +294,17 @@
         out_shape=[shape(ROWS, D + EXTRA), shape(16, 128)],
         compiler_params=params(MID),
         cost_estimate=cost(4 * ROWS * D * FF, 12_000_000),
-    )(dg, du, wg_t, wu_t, gg, after)
-
-
-def outer_kernel(at_ref, bt_ref, a_ref, b_ref, after_ref, out_ref, flag_ref):
+    )(dg, du, wg_t, wu_t, gg, *after)
+
+
+def outer_kernel(at_ref, bt_ref, a_ref, b_ref, *refs):
+    out_ref, flag_ref = refs[-2:]
     value = dot(at_ref[...], a_ref[...]) + dot(bt_ref[...], b_ref[...])
     out_ref[...] = value.astype(BF16)
     flag_ref[...] = jnp.zeros_like(flag_ref)
 
 
-def outer_sum(own_t, other_t, own, other, other_at, n, after):
+def outer_sum(own_t, other_t, own, other, other_at, n, *after):
     m, width = own_t.shape[0], 256
     left = pl.BlockSpec((m, ROWS), lambda j: (0, 0))
     return pl.pallas_call(
@@ -312,8 +315,8 @@
             left,
             pl.BlockSpec((ROWS, width), lambda j: (0, j)),
             pl.BlockSpec((ROWS, width), lambda j: (0, j + other_at // width)),
-            ANY,
-        ],
+        ]
+        + [ANY] * len(after),
         out_specs=[
             pl.BlockSpec((m, width), lambda j: (0, j)),
             pl.BlockSpec((16, 128), lambda j: (0, 0)),
@@ -321,7 +324,7 @@
         out_shape=[shape(m, n), shape(16, 128)],
         compiler_params=params(MID),
         cost_estimate=cost(4 * ROWS * m * n, 2 * (m * n + 2 * ROWS * (m + n))),
-    )(own_t, other_t, own, other, after)
+    )(own_t, other_t, own, other, *after)
 
 
 def combine_kernel(ids_hbm, gates_hbm, rows_hbm, tok_hbm, gate_hbm, flag_ref, ids, gates, rows, extra, tok, gate, sems, out_sems):
@@ -442,24 +445,27 @@
     d_gate, d_up, prob = backward(me, dy, down_t, hidden, factor, active)
     d_gate_other, d_up_other = swap_cores(d_gate), swap_cores(d_up)
     part_down, flag = outer_sum(hidden_t, hidden_other_t, dy, dy_other, H, H, me)
+    part_down = part_down.reshape(N_Z, FF // N_Z, H)
+    sum_down = ring_step(part_down, None, z, sign, 1)
     part_gate, flag = outer_sum(x_own, x_other, d_gate, d_gate_other, 0, FF, flag)
-    part_up, flag = outer_sum(x_own, x_other, d_up, d_up_other, 0, FF, flag)
-    pairs, _ = pair_grads(d_gate, d_up, gate_t, up_t, prob, flag)
-
-    part_down = part_down.reshape(N_Z, FF // N_Z, H)
     part_gate = part_gate.reshape(N_Z, D // (2 * N_Z), FF)
+    sum_gate = ring_step(part_gate, None, z, sign, 1)
+    part_up, flag = outer_sum(x_own, x_other, d_up, d_up_other, 0, FF, flag, sum_down)
     part_up = part_up.reshape(N_Z, D // (2 * N_Z), FF)
-    sum_down = ring_step(part_down, None, z, sign, 1)
-    sum_gate = ring_step(part_gate, None, z, sign, 1)
     sum_up = ring_step(part_up, None, z, sign, 1)
-    pairs = hold(pairs, sum_down, sum_gate, sum_up, mib=1)
+    sum_down = ring_step(part_down, sum_down, z, sign, 2)
+    pairs, _ = pair_grads(d_gate, d_up, gate_t, up_t, prob, flag, sum_gate)
+    sum_down = ring_step(part_down, sum_down, z, sign, 3)
+    sum_gate = ring_step(part_gate, sum_gate, z, sign, 2)
+    pairs = hold(pairs, sum_up, mib=1)
     back_rows = exchange_experts(pairs)
     token_grad, gate_grad_t, flag = combine(ids_t, gates_t, back_rows)
+    for step in range(4, N_Z):
+        sum_down = ring_step(part_down, sum_down, z, sign, step)
+    for step in range(3, N_Z):
+        sum_gate = ring_step(part_gate, sum_gate, z, sign, step)
     for step in range(2, N_Z):
-        sum_down = ring_step(part_down, sum_down, z, sign, step)
-        last = flag if step == 7 else None
-        sum_gate = ring_step(part_gate, sum_gate, z, sign, step, last)
-        sum_up = ring_step(part_up, sum_up, z, sign, step, last)
+        sum_up = ring_step(part_up, sum_up, z, sign, step, flag if step == 7 else None)
 
     halves = sum_down.reshape(2, FF // (2 * N_Z), H)
     mine = pick(halves, core)

time: 192 us -> 192 us (level); the launches traced: 192 us -> 190 us
  transfers between devices with their start and end apart: 30 -> 30, of which waited for: 14 -> 16; matrix products, arithmetic and copies ran while one was open for 6% -> 6% of each run, Pallas kernels for 29% -> 30%
where the time goes in v4:
time: 192 us; the launch traced here: 190 us
  waiting for transfers between devices  67.2 us (35%)
  Pallas kernels  58.9 us (31%)
  starting transfers between devices  41.5 us (22%)
  other arithmetic  12.8 us (7%)
  local copies, waits for them, and re-layouts  7.97 us (4%)
    all_to_all x3, waiting for transfers between devices, exchange_experts(): lax.all_to_all(rows.reshape(N_EXP, CAP, width), 'expert', split_axis=0, c...  33.2 us
    ppermute x21, waiting for transfers between devices, ring_step(): came = lax.ppermute(held, 'dp', ROUTE)  32.7 us
    all_to_all x3, starting transfers between devices, exchange_experts(): lax.all_to_all(rows.reshape(N_EXP, CAP, width), 'expert', split_axis=0, c...  25.8 us
    ppermute x21, starting transfers between devices, ring_step(): came = lax.ppermute(held, 'dp', ROUTE)  14.4 us
    pallas_call x3, Pallas kernels, outer_sum(): pl.pallas_call(outer_kernel, grid=(n // width,), in_specs=[left, left, pl...  14.2 us
    convert_element_type x19, other arithmetic, ring_step(): return (came.astype(F32) + block.astype(F32)).astype(BF16)  8.75 us
    unnamed x44, local copies, waits for them, and re-layouts  7.89 us
    pallas_call x1, Pallas kernels, forward(): pl.pallas_call(forward_kernel, grid=(3,), in_specs=[pl.BlockSpec((ROWS, D...  7.12 us
  transfers between devices with their start and end apart: 30, of which 16 were waited for; matrix products, arithmetic and copies ran while one was open for 6% of the time, Pallas kernels for 30%

profile of v4, /device:TPU:2, one launch (start us, length us, event | category | flops | bytes accessed | tf_op | source)
XLA Modules:
  0.0 189.5 jit_solution(10720095798698238884)
XLA Ops:
  0.6 2.9 %shard_map.111 = bf16[640,2048]{1,0:T(8,128)(2,1)} custom-call(s32[1]{0:T(128)} %bitcast.3.core_ref, s32[4,128]{1,0:T(4,128)} %bitcast.121, bf16[128,2048]{1,0:T(8,128)(2,1)} %x_hbm.3), custom_call_target="tpu_custom_call" | custom-call | flops 335544320 | bytes 2621440 | tf_op jit(solution)/shard_map/pallas_call | solution.py:113
  3.6 7.5 %all-to-all-start = ((bf16[16,40,2048]{2,1,0:T(8,128)(2,1)}), bf16[16,40,2048]{2,1,0:T(8,128)(2,1)}, u32[]{:S(2)}, u32[]{:S(2)}) async-start(bf16[16,40,2048]{2,1,0:T(8,128)(2,1)} %bitcast.127), calls=%async_computation | async-start | bytes 5242880 | tf_op jit(solution)/shard_map/all_to_all | solution.py:379
  11.1 5.8 %shard_map.112.refs_2_.wd_ref = bf16[3,2048,256]{2,1,0:T(8,128)(2,1)} custom-call(s32[1]{0:T(128)} %bitcast.3.core_ref, bf16[1,768,2048]{2,1,0:T(8,128)(2,1)} %w_ref.1), custom_call_target="tpu_custom_call" | custom-call | bytes 6291456 | tf_op jit(solution)/shard_map/pallas_call | solution.py:137
  16.8 6.1 %shard_map.113 = (bf16[4,768,512]{2,1,0:T(8,128)(2,1)}, bf16[4,768,512]{2,1,0:T(8,128)(2,1)}) custom-call(bf16[1,2048,768]{2,1,0:T(8,128)(2,1)} %wg_ref.1, bf16[1,2048,768]{2,1,0:T(8,128)(2,1)} %wu_ref.1), custom_call_target="tpu_custom_call" | custom-call | bytes 12582912 | tf_op jit(solution)/shard_map/pallas_call | solution.py:160
  22.9 2.9 %shard_map.110.refs_0_ = bf16[640,2048]{1,0:T(8,128)(2,1)} custom-call(s32[1]{0:T(128)} %bitcast.3.core_ref, s32[4,128]{1,0:T(4,128)} %bitcast.122, bf16[4,128]{1,0:T(4,128)(2,1)} %bitcast.124, bf16[128,2048]{1,0:T(8,128)(2,1)} %x_hbm.2), custom_call_target="tpu_custom_call" | custom-call | flops 335544320 | bytes 2621440 | tf_op jit(solution)/shard_map/pallas_call | solution.py:113
  25.9 20.0 %all-to-all-done = bf16[16,40,2048]{2,1,0:T(8,128)(2,1)} async-done(((bf16[16,40,2048]{2,1,0:T(8,128)(2,1)}), bf16[16,40,2048]{2,1,0:T(8,128)(2,1)}, u32[]{:S(2)}, u32[]{:S(2)}) %all-to-all-start) | async-done | bytes 2621472 | tf_op jit(solution)/shard_map/all_to_all | solution.py:379
  45.9 9.6 %all-to-all-start.1 = ((bf16[16,40,2048]{2,1,0:T(8,128)(2,1)}), bf16[16,40,2048]{2,1,0:T(8,128)(2,1)}, u32[]{:S(2)}, u32[]{:S(2)}) async-start(bf16[16,40,2048]{2,1,0:T(8,128)(2,1)} %bitcast.126), calls=%async_computation.1 | async-start | bytes 5242880 | tf_op jit(solution)/shard_map/all_to_all | solution.py:379
  55.5 5.0 %shard_map.115 = (bf16[1024,640]{1,0:T(8,128)(2,1)S(1)}, bf16[1024,640]{1,0:T(8,128)(2,1)S(1)}) custom-call(s32[1]{0:T(128)} %bitcast.3.core_ref, bf16[640,2048]{1,0:T(8,128)(2,1)} %bitcast.5.refs_1_.mine_ref.theirs_ref.x_ref, bf16[640,2048]{1,0:T(8,128)(2,1)} %bitcast.5.refs_1_.mine_ref.theirs_ref.x_ref), custom_call_target="tpu_custom_call" | custom-call | bytes 5242880 | tf_op jit(solution)/shard_map/pallas_call | solution.py:205
  61.6 7.1 %shard_map.116 = (bf16[768,640]{1,0:T(8,128)(2,1)S(1)}, bf16[3,640,256]{2,1,0:T(8,128)(2,1)S(1)}, bf16[3,640,256]{2,1,0:T(8,128)(2,1)S(1)}, bf16[3,640,256]{2,1,0:T(8,128)(2,1)S(1)}) custom-call(bf16[640,2048]{1,0:T(8,128)(2,1)} %bitcast.5.refs_1_.mine_ref.theirs_ref.x_ref, bf16[1,2048,768]{2,1,0:T(8,128)(2,1)S(1)} %copy-done.2, ...), custom_call_target="tpu_custom_call" | custom-call | flops 4026531840 | bytes 13000000 | tf_op jit(solution)/shard_map/pallas_call | solution.py:187
  74.5 13.2 %all-to-all-done.1 = bf16[16,40,2048]{2,1,0:T(8,128)(2,1)} async-done(((bf16[16,40,2048]{2,1,0:T(8,128)(2,1)}), bf16[16,40,2048]{2,1,0:T(8,128)(2,1)}, u32[]{:S(2)}, u32[]{:S(2)}) %all-to-all-start.1) | async-done | bytes 2621472 | tf_op jit(solution)/shard_map/all_to_all | solution.py:379
  87.6 7.1 %shard_map.118 = (bf16[640,768]{1,0:T(8,128)(2,1)}, bf16[640,768]{1,0:T(8,128)(2,1)}, bf16[640,128]{1,0:T(8,128)(2,1)}) custom-call(s32[1]{0:T(128)} %bitcast.2.me_ref.refs_0_, bf16[640,2048]{1,0:T(8,128)(2,1)} %shard_map.117.dy_ref.a_ref, bf16[3,2048,256]{2,1,0:T(8,128)(2,1)} %shard_map.112.refs_2_.wd_ref, bf16[3,640,256]{2,1,0:T(8,128)(2,1)} %copy-done.9, ...), custom_call_target="tpu_custom_call" | custom-call | flops 2013265920 | bytes 11000000 | tf_op jit(solution)/shard_map/pallas_call | solution.py:251
  96.8 5.0 %shard_map.119 = (bf16[768,1024]{1,0:T(8,128)(2,1)S(1)}, bf16[16,128]{1,0:T(8,128)(2,1)S(1)}) custom-call(bf16[768,640]{1,0:T(8,128)(2,1)S(1)} %copy-done.20, bf16[768,640]{1,0:T(8,128)(2,1)} %collective-permute-done.1.refs_2_.bt_ref, bf16[640,2048]{1,0:T(8,128)(2,1)} %shard_map.117.dy_ref.a_ref, bf16[640,2048]{1,0:T(8,128)(2,1)} %collective-permute-done.4.b_ref, ...), custom_call_target="tpu_custom_call" | custom-call | flops 2013265920 | bytes 6160384 | tf_op jit(solution)/shard_map/pallas_call | solution.py:310
  103.8 4.5 %shard_map.120 = (bf16[1024,768]{1,0:T(8,128)(2,1)S(1)}, bf16[16,128]{1,0:T(8,128)(2,1)S(1)}) custom-call(bf16[1024,640]{1,0:T(8,128)(2,1)S(1)} %copy-done.16, bf16[1024,640]{1,0:T(8,128)(2,1)} %collective-permute-done.refs_1_.bt_ref, bf16[640,768]{1,0:T(8,128)(2,1)S(1)} %copy-done.17, bf16[640,768]{1,0:T(8,128)(2,1)S(1)} %collective-permute-done.3.b_ref, ...), custom_call_target="tpu_custom_call" | custom-call | flops 2013265920 | bytes 6160384 | tf_op jit(solution)/shard_map/pallas_call | solution.py:310
  108.4 2.0 %collective-permute-start.6 = (bf16[128,768]{1,0:T(8,128)(2,1)S(1)}, bf16[128,768]{1,0:T(8,128)(2,1)S(1)}, u32[]{:S(2)}, u32[]{:S(2)}) collective-permute-start(bf16[128,768]{1,0:T(8,128)(2,1)S(1)} %dynamic-slice_bitcast_fusion.1), channel_id=1, source_target_pairs={{0,32},{32,64},{64,96},{96,128},{128,160},{160,192},{192,224},{224... | collective-permute-start | bytes 589832 | tf_op jit(solution)/shard_map/ppermute | solution.py:417
  112.7 4.6 %shard_map.121 = (bf16[1024,768]{1,0:T(8,128)(2,1)S(1)}, bf16[16,128]{1,0:T(8,128)(2,1)S(1)}) custom-call(bf16[1024,640]{1,0:T(8,128)(2,1)S(1)} %copy-done.16, bf16[1024,640]{1,0:T(8,128)(2,1)} %collective-permute-done.refs_1_.bt_ref, bf16[640,768]{1,0:T(8,128)(2,1)S(1)} %copy-done.18, bf16[640,768]{1,0:T(8,128)(2,1)S(1)} %collective-permute-done.2.b_ref, ...), custom_call_target="tpu_custom_call" | custom-call | flops 2013265920 | bytes 6160384 | tf_op jit(solution)/shard_map/pallas_call | solution.py:310
  117.4 3.2 %collective-permute-start.7 = (bf16[128,768]{1,0:T(8,128)(2,1)S(1)}, bf16[128,768]{1,0:T(8,128)(2,1)S(1)}, u32[]{:S(2)}, u32[]{:S(2)}) collective-permute-start(bf16[128,768]{1,0:T(8,128)(2,1)S(1)} %dynamic-slice_bitcast_fusion), channel_id=1, source_target_pairs={{0,32},{32,64},{64,96},{96,128},{128,160},{160,192},{192,224},{224... | collective-permute-start | bytes 589832 | tf_op jit(solution)/shard_map/ppermute | solution.py:417
  121.8 5.4 %shard_map.122 = (bf16[640,2176]{1,0:T(8,128)(2,1)S(1)}, bf16[16,128]{1,0:T(8,128)(2,1)}) custom-call(bf16[640,768]{1,0:T(8,128)(2,1)S(1)} %copy-done.17, bf16[640,768]{1,0:T(8,128)(2,1)S(1)} %copy-done.18, bf16[4,768,512]{2,1,0:T(8,128)(2,1)S(1)} %copy-done.14, bf16[4,768,512]{2,1,0:T(8,128)(2,1)S(1)} %copy-done.1, bf16[640,128]{1,0:T(8,128)(2,1)S(1)} %copy-done.21, ...), custom_call_target="tpu_custom_call" | custom-call | flops 4026531840 | bytes 12000000 | tf_op jit(solution)/shard_map/pallas_call | solution.py:285
  129.9 8.7 %all-to-all-start.2 = ((bf16[16,40,2176]{2,1,0:T(8,128)(2,1)}), bf16[16,40,2176]{2,1,0:T(8,128)(2,1)S(1)}, u32[]{:S(2)}, u32[]{:S(2)}) async-start(bf16[16,40,2176]{2,1,0:T(8,128)(2,1)} %bitcast.96), calls=%async_computation.2 | async-start | bytes 5570560 | tf_op jit(solution)/shard_map/all_to_all | solution.py:379
  142.5 4.4 %collective-permute-done.9 = bf16[128,768]{1,0:T(8,128)(2,1)S(1)} collective-permute-done((bf16[128,768]{1,0:T(8,128)(2,1)S(1)}, bf16[128,768]{1,0:T(8,128)(2,1)S(1)}, u32[]{:S(2)}, u32[]{:S(2)}) %collective-permute-start.9) | collective-permute-done | bytes 196640 | tf_op jit(solution)/shard_map/ppermute | solution.py:417
  151.1 3.7 %collective-permute-done.10 = bf16[128,768]{1,0:T(8,128)(2,1)S(1)} collective-permute-done((bf16[128,768]{1,0:T(8,128)(2,1)S(1)}, bf16[128,768]{1,0:T(8,128)(2,1)S(1)}, u32[]{:S(2)}, u32[]{:S(2)}) %collective-permute-start.10) | collective-permute-done | bytes 196640 | tf_op jit(solution)/shard_map/ppermute | solution.py:417
  159.2 3.6 %collective-permute-done.11 = bf16[128,768]{1,0:T(8,128)(2,1)S(1)} collective-permute-done((bf16[128,768]{1,0:T(8,128)(2,1)S(1)}, bf16[128,768]{1,0:T(8,128)(2,1)S(1)}, u32[]{:S(2)}, u32[]{:S(2)}) %collective-permute-start.11) | collective-permute-done | bytes 196640 | tf_op jit(solution)/shard_map/ppermute | solution.py:417
  167.1 3.6 %collective-permute-done.12 = bf16[128,768]{1,0:T(8,128)(2,1)S(1)} collective-permute-done((bf16[128,768]{1,0:T(8,128)(2,1)S(1)}, bf16[128,768]{1,0:T(8,128)(2,1)S(1)}, u32[]{:S(2)}, u32[]{:S(2)}) %collective-permute-start.12) | collective-permute-done | bytes 196640 | tf_op jit(solution)/shard_map/ppermute | solution.py:417
  175.1 5.7 %collective-permute-done.18 = bf16[128,768]{1,0:T(8,128)(2,1)S(1)} collective-permute-done((bf16[128,768]{1,0:T(8,128)(2,1)S(1)}, bf16[128,768]{1,0:T(8,128)(2,1)S(1)}, u32[]{:S(2)}, u32[]{:S(2)}) %collective-permute-start.18) | collective-permute-done | bytes 196640 | tf_op jit(solution)/shard_map/ppermute | solution.py:417
  185.5 2.4 %shard_map.124 = (bf16[128,2048]{1,0:T(8,128)(2,1)}, bf16[4,128]{1,0:T(4,128)(2,1)}, bf16[16,128]{1,0:T(8,128)(2,1)S(1)}) custom-call(s32[4,128]{1,0:T(4,128)S(1)} %bitcast.123, bf16[4,128]{1,0:T(4,128)(2,1)S(1)} %bitcast.125, bf16[640,2176]{1,0:T(8,128)(2,1)S(1)} %bitcast.95), custom_call_target="tpu_custom_call" | custom-call | flops 335544320 | bytes 2621440 | tf_op jit(solution)/shard_map/pallas_call | solution.py:357
  (123 shorter events, 44.3 us)
Async XLA Ops:
  3.6 42.3 %all-to-all-start = ((bf16[16,40,2048]{2,1,0:T(8,128)(2,1)}), bf16[16,40,2048]{2,1,0:T(8,128)(2,1)}, u32[]{:S(2)}, u32[]{:S(2)}) async-start(bf16[16,40,2048]{2,1,0:T(8,128)(2,1)} %bitcast.127), calls=%async_computation | async-start | bytes 5242880 | tf_op jit(solution)/shard_map/all_to_all | solution.py:379
  45.9 41.7 %all-to-all-start.1 = ((bf16[16,40,2048]{2,1,0:T(8,128)(2,1)}), bf16[16,40,2048]{2,1,0:T(8,128)(2,1)}, u32[]{:S(2)}, u32[]{:S(2)}) async-start(bf16[16,40,2048]{2,1,0:T(8,128)(2,1)} %bitcast.126), calls=%async_computation.1 | async-start | bytes 5242880 | tf_op jit(solution)/shard_map/all_to_all | solution.py:379
  61.6 12.8 %collective-permute-start = (bf16[1024,640]{1,0:T(8,128)(2,1)S(1)}, bf16[1024,640]{1,0:T(8,128)(2,1)}, u32[]{:S(2)}, u32[]{:S(2)}) collective-permute-start(bf16[1024,640]{1,0:T(8,128)(2,1)S(1)} %get-tuple-element.27), channel_id=1, source_target_pairs={{0,16},{16,0},{32,48},{48,32},{64,80},{80,64},{96,112},{112,96},{1... | collective-permute-start | bytes 3932168 | tf_op jit(solution)/shard_map/ppermute | solution.py:402
  87.6 7.8 %collective-permute-start.4 = (bf16[640,2048]{1,0:T(8,128)(2,1)}, bf16[640,2048]{1,0:T(8,128)(2,1)}, u32[]{:S(2)}, u32[]{:S(2)}) collective-permute-start(bf16[640,2048]{1,0:T(8,128)(2,1)} %shard_map.117.dy_ref.a_ref), channel_id=1, source_target_pairs={{0,16},{16,0},{32,48},{48,32},{64,80},{80,64},{96,112},{112,96},{1... | collective-permute-start | bytes 7864328 | tf_op jit(solution)/shard_map/ppermute | solution.py:402
  94.7 9.1 %collective-permute-start.3 = (bf16[640,768]{1,0:T(8,128)(2,1)}, bf16[640,768]{1,0:T(8,128)(2,1)S(1)}, u32[]{:S(2)}, u32[]{:S(2)}) collective-permute-start(bf16[640,768]{1,0:T(8,128)(2,1)} %get-tuple-element.32.a_ref.dg_ref), channel_id=1, source_target_pairs={{0,16},{16,0},{32,48},{48,32},{64,80},{80,64},{96,112},{112,96},{1... | collective-permute-start | bytes 2949128 | tf_op jit(solution)/shard_map/ppermute | solution.py:402
  95.3 17.3 %collective-permute-start.2 = (bf16[640,768]{1,0:T(8,128)(2,1)}, bf16[640,768]{1,0:T(8,128)(2,1)S(1)}, u32[]{:S(2)}, u32[]{:S(2)}) collective-permute-start(bf16[640,768]{1,0:T(8,128)(2,1)} %get-tuple-element.33.a_ref.du_ref), channel_id=1, source_target_pairs={{0,16},{16,0},{32,48},{48,32},{64,80},{80,64},{96,112},{112,96},{1... | collective-permute-start | bytes 2949128 | tf_op jit(solution)/shard_map/ppermute | solution.py:402
  101.8 9.6 %collective-permute-start.5 = (bf16[96,1024]{1,0:T(8,128)(2,1)S(1)}, bf16[96,1024]{1,0:T(8,128)(2,1)S(1)}, u32[]{:S(2)}, u32[]{:S(2)}) collective-permute-start(bf16[96,1024]{1,0:T(8,128)(2,1)S(1)} %dynamic-slice_bitcast_fusion.2), channel_id=1, source_target_pairs={{0,32},{32,64},{64,96},{96,128},{128,160},{160,192},{192,224},{224... | collective-permute-start | bytes 589832 | tf_op jit(solution)/shard_map/ppermute | solution.py:417
  108.4 12.1 %collective-permute-start.6 = (bf16[128,768]{1,0:T(8,128)(2,1)S(1)}, bf16[128,768]{1,0:T(8,128)(2,1)S(1)}, u32[]{:S(2)}, u32[]{:S(2)}) collective-permute-start(bf16[128,768]{1,0:T(8,128)(2,1)S(1)} %dynamic-slice_bitcast_fusion.1), channel_id=1, source_target_pairs={{0,32},{32,64},{64,96},{96,128},{128,160},{160,192},{192,224},{224... | collective-permute-start | bytes 589832 | tf_op jit(solution)/shard_map/ppermute | solution.py:417
  111.5 29.4 %collective-permute-start.20 = (bf16[96,1024]{1,0:T(8,128)(2,1)S(1)}, bf16[96,1024]{1,0:T(8,128)(2,1)}, u32[]{:S(2)}, u32[]{:S(2)}) collective-permute-start(bf16[96,1024]{1,0:T(8,128)(2,1)S(1)} %fusion.20.refs_1_), channel_id=1, source_target_pairs={{0,32},{32,64},{64,96},{96,128},{128,160},{160,192},{192,224},{224... | collective-permute-start | bytes 589832 | tf_op jit(solution)/shard_map/ppermute | solution.py:417
  117.4 9.8 %collective-permute-start.7 = (bf16[128,768]{1,0:T(8,128)(2,1)S(1)}, bf16[128,768]{1,0:T(8,128)(2,1)S(1)}, u32[]{:S(2)}, u32[]{:S(2)}) collective-permute-start(bf16[128,768]{1,0:T(8,128)(2,1)S(1)} %dynamic-slice_bitcast_fusion), channel_id=1, source_target_pairs={{0,32},{32,64},{64,96},{96,128},{128,160},{160,192},{192,224},{224... | collective-permute-start | bytes 589832 | tf_op jit(solution)/shard_map/ppermute | solution.py:417
  120.6 18.1 %collective-permute-start.8 = (bf16[128,768]{1,0:T(8,128)(2,1)S(1)}, bf16[128,768]{1,0:T(8,128)(2,1)}, u32[]{:S(2)}, u32[]{:S(2)}) collective-permute-start(bf16[128,768]{1,0:T(8,128)(2,1)S(1)} %fusion.19.refs_1_), channel_id=1, source_target_pairs={{0,32},{32,64},{64,96},{96,128},{128,160},{160,192},{192,224},{224... | collective-permute-start | bytes 589832 | tf_op jit(solution)/shard_map/ppermute | solution.py:417
  127.2 20.8 %collective-permute-start.14 = (bf16[128,768]{1,0:T(8,128)(2,1)S(1)}, bf16[128,768]{1,0:T(8,128)(2,1)}, u32[]{:S(2)}, u32[]{:S(2)}) collective-permute-start(bf16[128,768]{1,0:T(8,128)(2,1)S(1)} %fusion.18.refs_1_), channel_id=1, source_target_pairs={{0,32},{32,64},{64,96},{96,128},{128,160},{160,192},{192,224},{224... | collective-permute-start | bytes 589832 | tf_op jit(solution)/shard_map/ppermute | solution.py:417
  129.9 55.5 %all-to-all-start.2 = ((bf16[16,40,2176]{2,1,0:T(8,128)(2,1)}), bf16[16,40,2176]{2,1,0:T(8,128)(2,1)S(1)}, u32[]{:S(2)}, u32[]{:S(2)}) async-start(bf16[16,40,2176]{2,1,0:T(8,128)(2,1)} %bitcast.96), calls=%async_computation.2 | async-start | bytes 5570560 | tf_op jit(solution)/shard_map/all_to_all | solution.py:379
  142.0 7.1 %collective-permute-start.21 = (bf16[96,1024]{1,0:T(8,128)(2,1)S(1)}, bf16[96,1024]{1,0:T(8,128)(2,1)S(1)}, u32[]{:S(2)}, u32[]{:S(2)}) collective-permute-start(bf16[96,1024]{1,0:T(8,128)(2,1)S(1)} %fusion.5), channel_id=1, source_target_pairs={{0,32},{32,64},{64,96},{96,128},{128,160},{160,192},{192,224},{224... | collective-permute-start | bytes 589832 | tf_op jit(solution)/shard_map/ppermute | solution.py:417
  149.0 8.0 %collective-permute-start.15 = (bf16[128,768]{1,0:T(8,128)(2,1)S(1)}, bf16[128,768]{1,0:T(8,128)(2,1)S(1)}, u32[]{:S(2)}, u32[]{:S(2)}) collective-permute-start(bf16[128,768]{1,0:T(8,128)(2,1)S(1)} %fusion.11), channel_id=1, source_target_pairs={{0,32},{32,64},{64,96},{96,128},{128,160},{160,192},{192,224},{224... | collective-permute-start | bytes 589832 | tf_op jit(solution)/shard_map/ppermute | solution.py:417
  150.1 8.9 %collective-permute-start.22 = (bf16[96,1024]{1,0:T(8,128)(2,1)S(1)}, bf16[96,1024]{1,0:T(8,128)(2,1)S(1)}, u32[]{:S(2)}, u32[]{:S(2)}) collective-permute-start(bf16[96,1024]{1,0:T(8,128)(2,1)S(1)} %fusion.4), channel_id=1, source_target_pairs={{0,32},{32,64},{64,96},{96,128},{128,160},{160,192},{192,224},{224... | collective-permute-start | bytes 589832 | tf_op jit(solution)/shard_map/ppermute | solution.py:417
  157.0 7.9 %collective-permute-start.16 = (bf16[128,768]{1,0:T(8,128)(2,1)S(1)}, bf16[128,768]{1,0:T(8,128)(2,1)S(1)}, u32[]{:S(2)}, u32[]{:S(2)}) collective-permute-start(bf16[128,768]{1,0:T(8,128)(2,1)S(1)} %fusion.10), channel_id=1, source_target_pairs={{0,32},{32,64},{64,96},{96,128},{128,160},{160,192},{192,224},{224... | collective-permute-start | bytes 589832 | tf_op jit(solution)/shard_map/ppermute | solution.py:417
  159.1 7.9 %collective-permute-start.23 = (bf16[96,1024]{1,0:T(8,128)(2,1)S(1)}, bf16[96,1024]{1,0:T(8,128)(2,1)S(1)}, u32[]{:S(2)}, u32[]{:S(2)}) collective-permute-start(bf16[96,1024]{1,0:T(8,128)(2,1)S(1)} %fusion.3), channel_id=1, source_target_pairs={{0,32},{32,64},{64,96},{96,128},{128,160},{160,192},{192,224},{224... | collective-permute-start | bytes 589832 | tf_op jit(solution)/shard_map/ppermute | solution.py:417
  164.9 7.9 %collective-permute-start.17 = (bf16[128,768]{1,0:T(8,128)(2,1)S(1)}, bf16[128,768]{1,0:T(8,128)(2,1)S(1)}, u32[]{:S(2)}, u32[]{:S(2)}) collective-permute-start(bf16[128,768]{1,0:T(8,128)(2,1)S(1)} %fusion.9), channel_id=1, source_target_pairs={{0,32},{32,64},{64,96},{96,128},{128,160},{160,192},{192,224},{224... | collective-permute-start | bytes 589832 | tf_op jit(solution)/shard_map/ppermute | solution.py:417
  167.0 7.9 %collective-permute-start.24 = (bf16[96,1024]{1,0:T(8,128)(2,1)S(1)}, bf16[96,1024]{1,0:T(8,128)(2,1)S(1)}, u32[]{:S(2)}, u32[]{:S(2)}) collective-permute-start(bf16[96,1024]{1,0:T(8,128)(2,1)S(1)} %fusion.2), channel_id=1, source_target_pairs={{0,32},{32,64},{64,96},{96,128},{128,160},{160,192},{192,224},{224... | collective-permute-start | bytes 589832 | tf_op jit(solution)/shard_map/ppermute | solution.py:417
  171.7 11.4 %collective-permute-start.13 = (bf16[128,768]{1,0:T(8,128)(2,1)S(1)}, bf16[128,768]{1,0:T(8,128)(2,1)S(1)}, u32[]{:S(2)}, u32[]{:S(2)}) collective-permute-start(bf16[128,768]{1,0:T(8,128)(2,1)S(1)} %fusion.13), channel_id=1, source_target_pairs={{0,32},{32,64},{64,96},{96,128},{128,160},{160,192},{192,224},{224... | collective-permute-start | bytes 589832 | tf_op jit(solution)/shard_map/ppermute | solution.py:417
  172.9 7.9 %collective-permute-start.18 = (bf16[128,768]{1,0:T(8,128)(2,1)S(1)}, bf16[128,768]{1,0:T(8,128)(2,1)S(1)}, u32[]{:S(2)}, u32[]{:S(2)}) collective-permute-start(bf16[128,768]{1,0:T(8,128)(2,1)S(1)} %fusion.8), channel_id=1, source_target_pairs={{0,32},{32,64},{64,96},{96,128},{128,160},{160,192},{192,224},{224... | collective-permute-start | bytes 589832 | tf_op jit(solution)/shard_map/ppermute | solution.py:417
  175.0 7.9 %collective-permute-start.25 = (bf16[96,1024]{1,0:T(8,128)(2,1)S(1)}, bf16[96,1024]{1,0:T(8,128)(2,1)S(1)}, u32[]{:S(2)}, u32[]{:S(2)}) collective-permute-start(bf16[96,1024]{1,0:T(8,128)(2,1)S(1)} %fusion.1), channel_id=1, source_target_pairs={{0,32},{32,64},{64,96},{96,128},{128,160},{160,192},{192,224},{224... | collective-permute-start | bytes 589832 | tf_op jit(solution)/shard_map/ppermute | solution.py:417
  180.8 7.0 %collective-permute-start.19 = (bf16[128,768]{1,0:T(8,128)(2,1)S(1)}, bf16[128,768]{1,0:T(8,128)(2,1)S(1)}, u32[]{:S(2)}, u32[]{:S(2)}) collective-permute-start(bf16[128,768]{1,0:T(8,128)(2,1)S(1)} %fusion.7), channel_id=1, source_target_pairs={{0,32},{32,64},{64,96},{96,128},{128,160},{160,192},{192,224},{224... | collective-permute-start | bytes 589832 | tf_op jit(solution)/shard_map/ppermute | solution.py:417
  (28 other events, 198.2 us)

commit v5 on v4

--- a/solution.py
+++ b/solution.py
@@ -461,11 +461,11 @@
     back_rows = exchange_experts(pairs)
     token_grad, gate_grad_t, flag = combine(ids_t, gates_t, back_rows)
     for step in range(4, N_Z):
-        sum_down = ring_step(part_down, sum_down, z, sign, step)
+        sum_down = ring_step(part_down, sum_down, z, sign, step, flag if step == 7 else None)
     for step in range(3, N_Z):
         sum_gate = ring_step(part_gate, sum_gate, z, sign, step)
     for step in range(2, N_Z):
-        sum_up = ring_step(part_up, sum_up, z, sign, step, flag if step == 7 else None)
+        sum_up = ring_step(part_up, sum_up, z, sign, step)
 
     halves = sum_down.reshape(2, FF // (2 * N_Z), H)
     mine = pick(halves, core)

time: 192 us -> 191 us (level)
  transfers between devices with their start and end apart: 30 -> 30, of which waited for: 16 -> 16; matrix products, arithmetic and copies ran while one was open for 6% -> 7% of each run, Pallas kernels for 30% -> 29%
where the time goes in v5:
time: 191 us; the launch traced here: 190 us
  waiting for transfers between devices  67.1 us (35%)
  Pallas kernels  59 us (31%)
  starting transfers between devices  41.5 us (22%)
  other arithmetic  13.6 us (7%)
  local copies, waits for them, and re-layouts  7.97 us (4%)
    all_to_all x3, waiting for transfers between devices, exchange_experts(): lax.all_to_all(rows.reshape(N_EXP, CAP, width), 'expert', split_axis=0, c...  33.2 us
    ppermute x21, waiting for transfers between devices, ring_step(): came = lax.ppermute(held, 'dp', ROUTE)  32.6 us
    all_to_all x3, starting transfers between devices, exchange_experts(): lax.all_to_all(rows.reshape(N_EXP, CAP, width), 'expert', split_axis=0, c...  25.8 us
    ppermute x21, starting transfers between devices, ring_step(): came = lax.ppermute(held, 'dp', ROUTE)  14.4 us
    pallas_call x3, Pallas kernels, outer_sum(): pl.pallas_call(outer_kernel, grid=(n // width,), in_specs=[left, left, pl...  14.2 us
    convert_element_type x19, other arithmetic, ring_step(): return (came.astype(F32) + block.astype(F32)).astype(BF16)  9.52 us
    unnamed x44, local copies, waits for them, and re-layouts  7.89 us
    pallas_call x1, Pallas kernels, forward(): pl.pallas_call(forward_kernel, grid=(3,), in_specs=[pl.BlockSpec((ROWS, D...  7.12 us
  transfers between devices with their start and end apart: 30, of which 16 were waited for; matrix products, arithmetic and copies ran while one was open for 7% of the time, Pallas kernels for 29%

profile of v5, /device:TPU:2, one launch (start us, length us, event | category | flops | bytes accessed | tf_op | source)
XLA Modules:
  0.0 190.2 jit_solution(13567436850879442388)
XLA Ops:
  0.6 2.9 %shard_map.111 = bf16[640,2048]{1,0:T(8,128)(2,1)} custom-call(s32[1]{0:T(128)} %bitcast.3.core_ref, s32[4,128]{1,0:T(4,128)} %bitcast.121, bf16[128,2048]{1,0:T(8,128)(2,1)} %x_hbm.3), custom_call_target="tpu_custom_call" | custom-call | flops 335544320 | bytes 2621440 | tf_op jit(solution)/shard_map/pallas_call | solution.py:113
  3.6 7.5 %all-to-all-start = ((bf16[16,40,2048]{2,1,0:T(8,128)(2,1)}), bf16[16,40,2048]{2,1,0:T(8,128)(2,1)}, u32[]{:S(2)}, u32[]{:S(2)}) async-start(bf16[16,40,2048]{2,1,0:T(8,128)(2,1)} %bitcast.127), calls=%async_computation | async-start | bytes 5242880 | tf_op jit(solution)/shard_map/all_to_all | solution.py:379
  11.1 5.8 %shard_map.112.refs_2_.wd_ref = bf16[3,2048,256]{2,1,0:T(8,128)(2,1)} custom-call(s32[1]{0:T(128)} %bitcast.3.core_ref, bf16[1,768,2048]{2,1,0:T(8,128)(2,1)} %w_ref.1), custom_call_target="tpu_custom_call" | custom-call | bytes 6291456 | tf_op jit(solution)/shard_map/pallas_call | solution.py:137
  16.8 6.1 %shard_map.113 = (bf16[4,768,512]{2,1,0:T(8,128)(2,1)}, bf16[4,768,512]{2,1,0:T(8,128)(2,1)}) custom-call(bf16[1,2048,768]{2,1,0:T(8,128)(2,1)} %wg_ref.1, bf16[1,2048,768]{2,1,0:T(8,128)(2,1)} %wu_ref.1), custom_call_target="tpu_custom_call" | custom-call | bytes 12582912 | tf_op jit(solution)/shard_map/pallas_call | solution.py:160
  22.9 2.9 %shard_map.110.refs_0_ = bf16[640,2048]{1,0:T(8,128)(2,1)} custom-call(s32[1]{0:T(128)} %bitcast.3.core_ref, s32[4,128]{1,0:T(4,128)} %bitcast.122, bf16[4,128]{1,0:T(4,128)(2,1)} %bitcast.124, bf16[128,2048]{1,0:T(8,128)(2,1)} %x_hbm.2), custom_call_target="tpu_custom_call" | custom-call | flops 335544320 | bytes 2621440 | tf_op jit(solution)/shard_map/pallas_call | solution.py:113
  25.9 20.0 %all-to-all-done = bf16[16,40,2048]{2,1,0:T(8,128)(2,1)} async-done(((bf16[16,40,2048]{2,1,0:T(8,128)(2,1)}), bf16[16,40,2048]{2,1,0:T(8,128)(2,1)}, u32[]{:S(2)}, u32[]{:S(2)}) %all-to-all-start) | async-done | bytes 2621472 | tf_op jit(solution)/shard_map/all_to_all | solution.py:379
  45.9 9.6 %all-to-all-start.1 = ((bf16[16,40,2048]{2,1,0:T(8,128)(2,1)}), bf16[16,40,2048]{2,1,0:T(8,128)(2,1)}, u32[]{:S(2)}, u32[]{:S(2)}) async-start(bf16[16,40,2048]{2,1,0:T(8,128)(2,1)} %bitcast.126), calls=%async_computation.1 | async-start | bytes 5242880 | tf_op jit(solution)/shard_map/all_to_all | solution.py:379
  55.5 5.0 %shard_map.115 = (bf16[1024,640]{1,0:T(8,128)(2,1)S(1)}, bf16[1024,640]{1,0:T(8,128)(2,1)S(1)}) custom-call(s32[1]{0:T(128)} %bitcast.3.core_ref, bf16[640,2048]{1,0:T(8,128)(2,1)} %bitcast.5.refs_1_.mine_ref.theirs_ref.x_ref, bf16[640,2048]{1,0:T(8,128)(2,1)} %bitcast.5.refs_1_.mine_ref.theirs_ref.x_ref), custom_call_target="tpu_custom_call" | custom-call | bytes 5242880 | tf_op jit(solution)/shard_map/pallas_call | solution.py:205
  61.6 7.1 %shard_map.116 = (bf16[768,640]{1,0:T(8,128)(2,1)S(1)}, bf16[3,640,256]{2,1,0:T(8,128)(2,1)S(1)}, bf16[3,640,256]{2,1,0:T(8,128)(2,1)S(1)}, bf16[3,640,256]{2,1,0:T(8,128)(2,1)S(1)}) custom-call(bf16[640,2048]{1,0:T(8,128)(2,1)} %bitcast.5.refs_1_.mine_ref.theirs_ref.x_ref, bf16[1,2048,768]{2,1,0:T(8,128)(2,1)S(1)} %copy-done.2, ...), custom_call_target="tpu_custom_call" | custom-call | flops 4026531840 | bytes 13000000 | tf_op jit(solution)/shard_map/pallas_call | solution.py:187
  74.5 13.2 %all-to-all-done.1 = bf16[16,40,2048]{2,1,0:T(8,128)(2,1)} async-done(((bf16[16,40,2048]{2,1,0:T(8,128)(2,1)}), bf16[16,40,2048]{2,1,0:T(8,128)(2,1)}, u32[]{:S(2)}, u32[]{:S(2)}) %all-to-all-start.1) | async-done | bytes 2621472 | tf_op jit(solution)/shard_map/all_to_all | solution.py:379
  87.6 7.1 %shard_map.118 = (bf16[640,768]{1,0:T(8,128)(2,1)}, bf16[640,768]{1,0:T(8,128)(2,1)}, bf16[640,128]{1,0:T(8,128)(2,1)}) custom-call(s32[1]{0:T(128)} %bitcast.2.me_ref.refs_0_, bf16[640,2048]{1,0:T(8,128)(2,1)} %shard_map.117.dy_ref.a_ref, bf16[3,2048,256]{2,1,0:T(8,128)(2,1)} %shard_map.112.refs_2_.wd_ref, bf16[3,640,256]{2,1,0:T(8,128)(2,1)} %copy-done.9, ...), custom_call_target="tpu_custom_call" | custom-call | flops 2013265920 | bytes 11000000 | tf_op jit(solution)/shard_map/pallas_call | solution.py:251
  96.8 5.0 %shard_map.119 = (bf16[768,1024]{1,0:T(8,128)(2,1)S(1)}, bf16[16,128]{1,0:T(8,128)(2,1)S(1)}) custom-call(bf16[768,640]{1,0:T(8,128)(2,1)S(1)} %copy-done.20, bf16[768,640]{1,0:T(8,128)(2,1)} %collective-permute-done.1.refs_2_.bt_ref, bf16[640,2048]{1,0:T(8,128)(2,1)} %shard_map.117.dy_ref.a_ref, bf16[640,2048]{1,0:T(8,128)(2,1)} %collective-permute-done.4.b_ref, ...), custom_call_target="tpu_custom_call" | custom-call | flops 2013265920 | bytes 6160384 | tf_op jit(solution)/shard_map/pallas_call | solution.py:310
  103.8 4.6 %shard_map.120 = (bf16[1024,768]{1,0:T(8,128)(2,1)S(1)}, bf16[16,128]{1,0:T(8,128)(2,1)S(1)}) custom-call(bf16[1024,640]{1,0:T(8,128)(2,1)S(1)} %copy-done.16, bf16[1024,640]{1,0:T(8,128)(2,1)} %collective-permute-done.refs_1_.bt_ref, bf16[640,768]{1,0:T(8,128)(2,1)S(1)} %copy-done.17, bf16[640,768]{1,0:T(8,128)(2,1)S(1)} %collective-permute-done.3.b_ref, ...), custom_call_target="tpu_custom_call" | custom-call | flops 2013265920 | bytes 6160384 | tf_op jit(solution)/shard_map/pallas_call | solution.py:310
  108.4 2.0 %collective-permute-start.6 = (bf16[128,768]{1,0:T(8,128)(2,1)S(1)}, bf16[128,768]{1,0:T(8,128)(2,1)S(1)}, u32[]{:S(2)}, u32[]{:S(2)}) collective-permute-start(bf16[128,768]{1,0:T(8,128)(2,1)S(1)} %dynamic-slice_bitcast_fusion.1), channel_id=1, source_target_pairs={{0,32},{32,64},{64,96},{96,128},{128,160},{160,192},{192,224},{224... | collective-permute-start | bytes 589832 | tf_op jit(solution)/shard_map/ppermute | solution.py:417
  112.7 4.6 %shard_map.121 = (bf16[1024,768]{1,0:T(8,128)(2,1)S(1)}, bf16[16,128]{1,0:T(8,128)(2,1)S(1)}) custom-call(bf16[1024,640]{1,0:T(8,128)(2,1)S(1)} %copy-done.16, bf16[1024,640]{1,0:T(8,128)(2,1)} %collective-permute-done.refs_1_.bt_ref, bf16[640,768]{1,0:T(8,128)(2,1)S(1)} %copy-done.18, bf16[640,768]{1,0:T(8,128)(2,1)S(1)} %collective-permute-done.2.b_ref, ...), custom_call_target="tpu_custom_call" | custom-call | flops 2013265920 | bytes 6160384 | tf_op jit(solution)/shard_map/pallas_call | solution.py:310
  117.4 3.2 %collective-permute-start.7 = (bf16[128,768]{1,0:T(8,128)(2,1)S(1)}, bf16[128,768]{1,0:T(8,128)(2,1)S(1)}, u32[]{:S(2)}, u32[]{:S(2)}) collective-permute-start(bf16[128,768]{1,0:T(8,128)(2,1)S(1)} %dynamic-slice_bitcast_fusion), channel_id=1, source_target_pairs={{0,32},{32,64},{64,96},{96,128},{128,160},{160,192},{192,224},{224... | collective-permute-start | bytes 589832 | tf_op jit(solution)/shard_map/ppermute | solution.py:417
  121.8 5.4 %shard_map.122 = (bf16[640,2176]{1,0:T(8,128)(2,1)S(1)}, bf16[16,128]{1,0:T(8,128)(2,1)}) custom-call(bf16[640,768]{1,0:T(8,128)(2,1)S(1)} %copy-done.17, bf16[640,768]{1,0:T(8,128)(2,1)S(1)} %copy-done.18, bf16[4,768,512]{2,1,0:T(8,128)(2,1)S(1)} %copy-done.14, bf16[4,768,512]{2,1,0:T(8,128)(2,1)S(1)} %copy-done.1, bf16[640,128]{1,0:T(8,128)(2,1)S(1)} %copy-done.21, ...), custom_call_target="tpu_custom_call" | custom-call | flops 4026531840 | bytes 12000000 | tf_op jit(solution)/shard_map/pallas_call | solution.py:285
  130.0 8.7 %all-to-all-start.2 = ((bf16[16,40,2176]{2,1,0:T(8,128)(2,1)}), bf16[16,40,2176]{2,1,0:T(8,128)(2,1)S(1)}, u32[]{:S(2)}, u32[]{:S(2)}) async-start(bf16[16,40,2176]{2,1,0:T(8,128)(2,1)} %bitcast.96), calls=%async_computation.2 | async-start | bytes 5570560 | tf_op jit(solution)/shard_map/all_to_all | solution.py:379
  142.5 4.4 %collective-permute-done.9 = bf16[128,768]{1,0:T(8,128)(2,1)S(1)} collective-permute-done((bf16[128,768]{1,0:T(8,128)(2,1)S(1)}, bf16[128,768]{1,0:T(8,128)(2,1)S(1)}, u32[]{:S(2)}, u32[]{:S(2)}) %collective-permute-start.9) | collective-permute-done | bytes 196640 | tf_op jit(solution)/shard_map/ppermute | solution.py:417
  150.3 4.5 %collective-permute-done.10 = bf16[128,768]{1,0:T(8,128)(2,1)S(1)} collective-permute-done((bf16[128,768]{1,0:T(8,128)(2,1)S(1)}, bf16[128,768]{1,0:T(8,128)(2,1)S(1)}, u32[]{:S(2)}, u32[]{:S(2)}) %collective-permute-start.10) | collective-permute-done | bytes 196640 | tf_op jit(solution)/shard_map/ppermute | solution.py:417
  159.2 3.6 %collective-permute-done.11 = bf16[128,768]{1,0:T(8,128)(2,1)S(1)} collective-permute-done((bf16[128,768]{1,0:T(8,128)(2,1)S(1)}, bf16[128,768]{1,0:T(8,128)(2,1)S(1)}, u32[]{:S(2)}, u32[]{:S(2)}) %collective-permute-start.11) | collective-permute-done | bytes 196640 | tf_op jit(solution)/shard_map/ppermute | solution.py:417
  167.2 3.6 %collective-permute-done.12 = bf16[128,768]{1,0:T(8,128)(2,1)S(1)} collective-permute-done((bf16[128,768]{1,0:T(8,128)(2,1)S(1)}, bf16[128,768]{1,0:T(8,128)(2,1)S(1)}, u32[]{:S(2)}, u32[]{:S(2)}) %collective-permute-start.12) | collective-permute-done | bytes 196640 | tf_op jit(solution)/shard_map/ppermute | solution.py:417
  175.7 5.1 %collective-permute-done.18 = bf16[128,768]{1,0:T(8,128)(2,1)S(1)} collective-permute-done((bf16[128,768]{1,0:T(8,128)(2,1)S(1)}, bf16[128,768]{1,0:T(8,128)(2,1)S(1)}, u32[]{:S(2)}, u32[]{:S(2)}) %collective-permute-start.18) | collective-permute-done | bytes 196640 | tf_op jit(solution)/shard_map/ppermute | solution.py:417
  182.6 2.4 %shard_map.124 = (bf16[128,2048]{1,0:T(8,128)(2,1)}, bf16[4,128]{1,0:T(4,128)(2,1)}, bf16[16,128]{1,0:T(8,128)(2,1)S(1)}) custom-call(s32[4,128]{1,0:T(4,128)S(1)} %bitcast.123, bf16[4,128]{1,0:T(4,128)(2,1)S(1)} %bitcast.125, bf16[640,2176]{1,0:T(8,128)(2,1)S(1)} %bitcast.95), custom_call_target="tpu_custom_call" | custom-call | flops 335544320 | bytes 2621440 | tf_op jit(solution)/shard_map/pallas_call | solution.py:357
  (123 shorter events, 44.7 us)
Async XLA Ops:
  3.6 42.3 %all-to-all-start = ((bf16[16,40,2048]{2,1,0:T(8,128)(2,1)}), bf16[16,40,2048]{2,1,0:T(8,128)(2,1)}, u32[]{:S(2)}, u32[]{:S(2)}) async-start(bf16[16,40,2048]{2,1,0:T(8,128)(2,1)} %bitcast.127), calls=%async_computation | async-start | bytes 5242880 | tf_op jit(solution)/shard_map/all_to_all | solution.py:379
  45.9 41.7 %all-to-all-start.1 = ((bf16[16,40,2048]{2,1,0:T(8,128)(2,1)}), bf16[16,40,2048]{2,1,0:T(8,128)(2,1)}, u32[]{:S(2)}, u32[]{:S(2)}) async-start(bf16[16,40,2048]{2,1,0:T(8,128)(2,1)} %bitcast.126), calls=%async_computation.1 | async-start | bytes 5242880 | tf_op jit(solution)/shard_map/all_to_all | solution.py:379
  61.6 12.8 %collective-permute-start = (bf16[1024,640]{1,0:T(8,128)(2,1)S(1)}, bf16[1024,640]{1,0:T(8,128)(2,1)}, u32[]{:S(2)}, u32[]{:S(2)}) collective-permute-start(bf16[1024,640]{1,0:T(8,128)(2,1)S(1)} %get-tuple-element.27), channel_id=1, source_target_pairs={{0,16},{16,0},{32,48},{48,32},{64,80},{80,64},{96,112},{112,96},{1... | collective-permute-start | bytes 3932168 | tf_op jit(solution)/shard_map/ppermute | solution.py:402
  87.6 7.8 %collective-permute-start.4 = (bf16[640,2048]{1,0:T(8,128)(2,1)}, bf16[640,2048]{1,0:T(8,128)(2,1)}, u32[]{:S(2)}, u32[]{:S(2)}) collective-permute-start(bf16[640,2048]{1,0:T(8,128)(2,1)} %shard_map.117.dy_ref.a_ref), channel_id=1, source_target_pairs={{0,16},{16,0},{32,48},{48,32},{64,80},{80,64},{96,112},{112,96},{1... | collective-permute-start | bytes 7864328 | tf_op jit(solution)/shard_map/ppermute | solution.py:402
  94.7 9.1 %collective-permute-start.3 = (bf16[640,768]{1,0:T(8,128)(2,1)}, bf16[640,768]{1,0:T(8,128)(2,1)S(1)}, u32[]{:S(2)}, u32[]{:S(2)}) collective-permute-start(bf16[640,768]{1,0:T(8,128)(2,1)} %get-tuple-element.32.a_ref.dg_ref), channel_id=1, source_target_pairs={{0,16},{16,0},{32,48},{48,32},{64,80},{80,64},{96,112},{112,96},{1... | collective-permute-start | bytes 2949128 | tf_op jit(solution)/shard_map/ppermute | solution.py:402
  95.3 17.4 %collective-permute-start.2 = (bf16[640,768]{1,0:T(8,128)(2,1)}, bf16[640,768]{1,0:T(8,128)(2,1)S(1)}, u32[]{:S(2)}, u32[]{:S(2)}) collective-permute-start(bf16[640,768]{1,0:T(8,128)(2,1)} %get-tuple-element.33.a_ref.du_ref), channel_id=1, source_target_pairs={{0,16},{16,0},{32,48},{48,32},{64,80},{80,64},{96,112},{112,96},{1... | collective-permute-start | bytes 2949128 | tf_op jit(solution)/shard_map/ppermute | solution.py:402
  101.8 9.6 %collective-permute-start.5 = (bf16[96,1024]{1,0:T(8,128)(2,1)S(1)}, bf16[96,1024]{1,0:T(8,128)(2,1)S(1)}, u32[]{:S(2)}, u32[]{:S(2)}) collective-permute-start(bf16[96,1024]{1,0:T(8,128)(2,1)S(1)} %dynamic-slice_bitcast_fusion.2), channel_id=1, source_target_pairs={{0,32},{32,64},{64,96},{96,128},{128,160},{160,192},{192,224},{224... | collective-permute-start | bytes 589832 | tf_op jit(solution)/shard_map/ppermute | solution.py:417
  108.4 12.2 %collective-permute-start.6 = (bf16[128,768]{1,0:T(8,128)(2,1)S(1)}, bf16[128,768]{1,0:T(8,128)(2,1)S(1)}, u32[]{:S(2)}, u32[]{:S(2)}) collective-permute-start(bf16[128,768]{1,0:T(8,128)(2,1)S(1)} %dynamic-slice_bitcast_fusion.1), channel_id=1, source_target_pairs={{0,32},{32,64},{64,96},{96,128},{128,160},{160,192},{192,224},{224... | collective-permute-start | bytes 589832 | tf_op jit(solution)/shard_map/ppermute | solution.py:417
  111.5 29.4 %collective-permute-start.20 = (bf16[96,1024]{1,0:T(8,128)(2,1)S(1)}, bf16[96,1024]{1,0:T(8,128)(2,1)}, u32[]{:S(2)}, u32[]{:S(2)}) collective-permute-start(bf16[96,1024]{1,0:T(8,128)(2,1)S(1)} %fusion.20.refs_1_), channel_id=1, source_target_pairs={{0,32},{32,64},{64,96},{96,128},{128,160},{160,192},{192,224},{224... | collective-permute-start | bytes 589832 | tf_op jit(solution)/shard_map/ppermute | solution.py:417
  117.4 9.8 %collective-permute-start.7 = (bf16[128,768]{1,0:T(8,128)(2,1)S(1)}, bf16[128,768]{1,0:T(8,128)(2,1)S(1)}, u32[]{:S(2)}, u32[]{:S(2)}) collective-permute-start(bf16[128,768]{1,0:T(8,128)(2,1)S(1)} %dynamic-slice_bitcast_fusion), channel_id=1, source_target_pairs={{0,32},{32,64},{64,96},{96,128},{128,160},{160,192},{192,224},{224... | collective-permute-start | bytes 589832 | tf_op jit(solution)/shard_map/ppermute | solution.py:417
  120.7 18.1 %collective-permute-start.8 = (bf16[128,768]{1,0:T(8,128)(2,1)S(1)}, bf16[128,768]{1,0:T(8,128)(2,1)}, u32[]{:S(2)}, u32[]{:S(2)}) collective-permute-start(bf16[128,768]{1,0:T(8,128)(2,1)S(1)} %fusion.19.refs_1_), channel_id=1, source_target_pairs={{0,32},{32,64},{64,96},{96,128},{128,160},{160,192},{192,224},{224... | collective-permute-start | bytes 589832 | tf_op jit(solution)/shard_map/ppermute | solution.py:417
  127.2 20.7 %collective-permute-start.14 = (bf16[128,768]{1,0:T(8,128)(2,1)S(1)}, bf16[128,768]{1,0:T(8,128)(2,1)}, u32[]{:S(2)}, u32[]{:S(2)}) collective-permute-start(bf16[128,768]{1,0:T(8,128)(2,1)S(1)} %fusion.18.refs_1_), channel_id=1, source_target_pairs={{0,32},{32,64},{64,96},{96,128},{128,160},{160,192},{192,224},{224... | collective-permute-start | bytes 589832 | tf_op jit(solution)/shard_map/ppermute | solution.py:417
  130.0 52.7 %all-to-all-start.2 = ((bf16[16,40,2176]{2,1,0:T(8,128)(2,1)}), bf16[16,40,2176]{2,1,0:T(8,128)(2,1)S(1)}, u32[]{:S(2)}, u32[]{:S(2)}) async-start(bf16[16,40,2176]{2,1,0:T(8,128)(2,1)} %bitcast.96), calls=%async_computation.2 | async-start | bytes 5570560 | tf_op jit(solution)/shard_map/all_to_all | solution.py:379
  139.9 7.0 %collective-permute-start.9 = (bf16[128,768]{1,0:T(8,128)(2,1)S(1)}, bf16[128,768]{1,0:T(8,128)(2,1)S(1)}, u32[]{:S(2)}, u32[]{:S(2)}) collective-permute-start(bf16[128,768]{1,0:T(8,128)(2,1)S(1)} %fusion.17), channel_id=1, source_target_pairs={{0,32},{32,64},{64,96},{96,128},{128,160},{160,192},{192,224},{224... | collective-permute-start | bytes 589832 | tf_op jit(solution)/shard_map/ppermute | solution.py:417
  142.0 7.2 %collective-permute-start.21 = (bf16[96,1024]{1,0:T(8,128)(2,1)S(1)}, bf16[96,1024]{1,0:T(8,128)(2,1)S(1)}, u32[]{:S(2)}, u32[]{:S(2)}) collective-permute-start(bf16[96,1024]{1,0:T(8,128)(2,1)S(1)} %fusion.5), channel_id=1, source_target_pairs={{0,32},{32,64},{64,96},{96,128},{128,160},{160,192},{192,224},{224... | collective-permute-start | bytes 589832 | tf_op jit(solution)/shard_map/ppermute | solution.py:417
  149.1 7.9 %collective-permute-start.15 = (bf16[128,768]{1,0:T(8,128)(2,1)S(1)}, bf16[128,768]{1,0:T(8,128)(2,1)S(1)}, u32[]{:S(2)}, u32[]{:S(2)}) collective-permute-start(bf16[128,768]{1,0:T(8,128)(2,1)S(1)} %fusion.11), channel_id=1, source_target_pairs={{0,32},{32,64},{64,96},{96,128},{128,160},{160,192},{192,224},{224... | collective-permute-start | bytes 589832 | tf_op jit(solution)/shard_map/ppermute | solution.py:417
  149.3 9.8 %collective-permute-start.22 = (bf16[96,1024]{1,0:T(8,128)(2,1)S(1)}, bf16[96,1024]{1,0:T(8,128)(2,1)S(1)}, u32[]{:S(2)}, u32[]{:S(2)}) collective-permute-start(bf16[96,1024]{1,0:T(8,128)(2,1)S(1)} %fusion.4), channel_id=1, source_target_pairs={{0,32},{32,64},{64,96},{96,128},{128,160},{160,192},{192,224},{224... | collective-permute-start | bytes 589832 | tf_op jit(solution)/shard_map/ppermute | solution.py:417
  157.0 7.9 %collective-permute-start.16 = (bf16[128,768]{1,0:T(8,128)(2,1)S(1)}, bf16[128,768]{1,0:T(8,128)(2,1)S(1)}, u32[]{:S(2)}, u32[]{:S(2)}) collective-permute-start(bf16[128,768]{1,0:T(8,128)(2,1)S(1)} %fusion.10), channel_id=1, source_target_pairs={{0,32},{32,64},{64,96},{96,128},{128,160},{160,192},{192,224},{224... | collective-permute-start | bytes 589832 | tf_op jit(solution)/shard_map/ppermute | solution.py:417
  159.1 7.9 %collective-permute-start.23 = (bf16[96,1024]{1,0:T(8,128)(2,1)S(1)}, bf16[96,1024]{1,0:T(8,128)(2,1)S(1)}, u32[]{:S(2)}, u32[]{:S(2)}) collective-permute-start(bf16[96,1024]{1,0:T(8,128)(2,1)S(1)} %fusion.3), channel_id=1, source_target_pairs={{0,32},{32,64},{64,96},{96,128},{128,160},{160,192},{192,224},{224... | collective-permute-start | bytes 589832 | tf_op jit(solution)/shard_map/ppermute | solution.py:417
  165.0 7.9 %collective-permute-start.17 = (bf16[128,768]{1,0:T(8,128)(2,1)S(1)}, bf16[128,768]{1,0:T(8,128)(2,1)S(1)}, u32[]{:S(2)}, u32[]{:S(2)}) collective-permute-start(bf16[128,768]{1,0:T(8,128)(2,1)S(1)} %fusion.9), channel_id=1, source_target_pairs={{0,32},{32,64},{64,96},{96,128},{128,160},{160,192},{192,224},{224... | collective-permute-start | bytes 589832 | tf_op jit(solution)/shard_map/ppermute | solution.py:417
  167.1 7.9 %collective-permute-start.24 = (bf16[96,1024]{1,0:T(8,128)(2,1)S(1)}, bf16[96,1024]{1,0:T(8,128)(2,1)S(1)}, u32[]{:S(2)}, u32[]{:S(2)}) collective-permute-start(bf16[96,1024]{1,0:T(8,128)(2,1)S(1)} %fusion.2), channel_id=1, source_target_pairs={{0,32},{32,64},{64,96},{96,128},{128,160},{160,192},{192,224},{224... | collective-permute-start | bytes 589832 | tf_op jit(solution)/shard_map/ppermute | solution.py:417
  171.7 9.2 %collective-permute-start.13 = (bf16[128,768]{1,0:T(8,128)(2,1)S(1)}, bf16[128,768]{1,0:T(8,128)(2,1)S(1)}, u32[]{:S(2)}, u32[]{:S(2)}) collective-permute-start(bf16[128,768]{1,0:T(8,128)(2,1)S(1)} %fusion.13), channel_id=1, source_target_pairs={{0,32},{32,64},{64,96},{96,128},{128,160},{160,192},{192,224},{224... | collective-permute-start | bytes 589832 | tf_op jit(solution)/shard_map/ppermute | solution.py:417
  172.9 7.9 %collective-permute-start.18 = (bf16[128,768]{1,0:T(8,128)(2,1)S(1)}, bf16[128,768]{1,0:T(8,128)(2,1)S(1)}, u32[]{:S(2)}, u32[]{:S(2)}) collective-permute-start(bf16[128,768]{1,0:T(8,128)(2,1)S(1)} %fusion.8), channel_id=1, source_target_pairs={{0,32},{32,64},{64,96},{96,128},{128,160},{160,192},{192,224},{224... | collective-permute-start | bytes 589832 | tf_op jit(solution)/shard_map/ppermute | solution.py:417
  175.7 9.3 %collective-permute-start.25 = (bf16[96,1024]{1,0:T(8,128)(2,1)}, bf16[96,1024]{1,0:T(8,128)(2,1)S(1)}, u32[]{:S(2)}, u32[]{:S(2)}) collective-permute-start(bf16[96,1024]{1,0:T(8,128)(2,1)} %fusion.1), channel_id=1, source_target_pairs={{0,32},{32,64},{64,96},{96,128},{128,160},{160,192},{192,224},{224... | collective-permute-start | bytes 589832 | tf_op jit(solution)/shard_map/ppermute | solution.py:417
  (28 other events, 207.1 us)

commit v6 on v5

--- a/solution.py
+++ b/solution.py
@@ -457,7 +457,7 @@
     pairs, _ = pair_grads(d_gate, d_up, gate_t, up_t, prob, flag, sum_gate)
     sum_down = ring_step(part_down, sum_down, z, sign, 3)
     sum_gate = ring_step(part_gate, sum_gate, z, sign, 2)
-    pairs = hold(pairs, sum_up, mib=1)
+    pairs = hold(pairs, sum_up[:16, :128], mib=62)
     back_rows = exchange_experts(pairs)
     token_grad, gate_grad_t, flag = combine(ids_t, gates_t, back_rows)
     for step in range(4, N_Z):

time: 191 us -> 192 us (level)
  no operation moved by 1% of the time
where the time goes in v6:
time: 192 us; the launch traced here: 191 us
  waiting for transfers between devices  67.5 us (35%)
  Pallas kernels  59 us (31%)
  starting transfers between devices  41 us (21%)
  other arithmetic  13.5 us (7%)
  local copies, waits for them, and re-layouts  8.57 us (4%)
    all_to_all x3, waiting for transfers between devices, exchange_experts(): lax.all_to_all(rows.reshape(N_EXP, CAP, width), 'expert', split_axis=0, c...  33.2 us
    ppermute x21, waiting for transfers between devices, ring_step(): came = lax.ppermute(held, 'dp', ROUTE)  33 us
    all_to_all x3, starting transfers between devices, exchange_experts(): lax.all_to_all(rows.reshape(N_EXP, CAP, width), 'expert', split_axis=0, c...  25.8 us
    pallas_call x3, Pallas kernels, outer_sum(): pl.pallas_call(outer_kernel, grid=(n // width,), in_specs=[left, left, pl...  14.2 us
    ppermute x21, starting transfers between devices, ring_step(): came = lax.ppermute(held, 'dp', ROUTE)  13.9 us
    convert_element_type x19, other arithmetic, ring_step(): return (came.astype(F32) + block.astype(F32)).astype(BF16)  9.5 us
    unnamed x44, local copies, waits for them, and re-layouts  7.89 us
    pallas_call x1, Pallas kernels, forward(): pl.pallas_call(forward_kernel, grid=(3,), in_specs=[pl.BlockSpec((ROWS, D...  7.12 us
  transfers between devices with their start and end apart: 30, of which 16 were waited for; matrix products, arithmetic and copies ran while one was open for 7% of the time, Pallas kernels for 29%

profile of v6, /device:TPU:2, one launch (start us, length us, event | category | flops | bytes accessed | tf_op | source)
XLA Modules:
  0.0 190.7 jit_solution(6579787676365857896)
XLA Ops:
  0.6 2.9 %shard_map.111 = bf16[640,2048]{1,0:T(8,128)(2,1)} custom-call(s32[1]{0:T(128)} %bitcast.3.core_ref, s32[4,128]{1,0:T(4,128)} %bitcast.121, bf16[128,2048]{1,0:T(8,128)(2,1)} %x_hbm.3), custom_call_target="tpu_custom_call" | custom-call | flops 335544320 | bytes 2621440 | tf_op jit(solution)/shard_map/pallas_call | solution.py:113
  3.6 7.5 %all-to-all-start = ((bf16[16,40,2048]{2,1,0:T(8,128)(2,1)}), bf16[16,40,2048]{2,1,0:T(8,128)(2,1)}, u32[]{:S(2)}, u32[]{:S(2)}) async-start(bf16[16,40,2048]{2,1,0:T(8,128)(2,1)} %bitcast.127), calls=%async_computation | async-start | bytes 5242880 | tf_op jit(solution)/shard_map/all_to_all | solution.py:379
  11.1 5.8 %shard_map.112.refs_2_.wd_ref = bf16[3,2048,256]{2,1,0:T(8,128)(2,1)} custom-call(s32[1]{0:T(128)} %bitcast.3.core_ref, bf16[1,768,2048]{2,1,0:T(8,128)(2,1)} %w_ref.1), custom_call_target="tpu_custom_call" | custom-call | bytes 6291456 | tf_op jit(solution)/shard_map/pallas_call | solution.py:137
  16.8 6.1 %shard_map.113 = (bf16[4,768,512]{2,1,0:T(8,128)(2,1)}, bf16[4,768,512]{2,1,0:T(8,128)(2,1)}) custom-call(bf16[1,2048,768]{2,1,0:T(8,128)(2,1)} %wg_ref.1, bf16[1,2048,768]{2,1,0:T(8,128)(2,1)} %wu_ref.1), custom_call_target="tpu_custom_call" | custom-call | bytes 12582912 | tf_op jit(solution)/shard_map/pallas_call | solution.py:160
  22.9 2.9 %shard_map.110.refs_0_ = bf16[640,2048]{1,0:T(8,128)(2,1)} custom-call(s32[1]{0:T(128)} %bitcast.3.core_ref, s32[4,128]{1,0:T(4,128)} %bitcast.122, bf16[4,128]{1,0:T(4,128)(2,1)} %bitcast.124, bf16[128,2048]{1,0:T(8,128)(2,1)} %x_hbm.2), custom_call_target="tpu_custom_call" | custom-call | flops 335544320 | bytes 2621440 | tf_op jit(solution)/shard_map/pallas_call | solution.py:113
  25.9 20.0 %all-to-all-done = bf16[16,40,2048]{2,1,0:T(8,128)(2,1)} async-done(((bf16[16,40,2048]{2,1,0:T(8,128)(2,1)}), bf16[16,40,2048]{2,1,0:T(8,128)(2,1)}, u32[]{:S(2)}, u32[]{:S(2)}) %all-to-all-start) | async-done | bytes 2621472 | tf_op jit(solution)/shard_map/all_to_all | solution.py:379
  45.9 9.6 %all-to-all-start.1 = ((bf16[16,40,2048]{2,1,0:T(8,128)(2,1)}), bf16[16,40,2048]{2,1,0:T(8,128)(2,1)}, u32[]{:S(2)}, u32[]{:S(2)}) async-start(bf16[16,40,2048]{2,1,0:T(8,128)(2,1)} %bitcast.126), calls=%async_computation.1 | async-start | bytes 5242880 | tf_op jit(solution)/shard_map/all_to_all | solution.py:379
  55.5 5.0 %shard_map.115 = (bf16[1024,640]{1,0:T(8,128)(2,1)S(1)}, bf16[1024,640]{1,0:T(8,128)(2,1)S(1)}) custom-call(s32[1]{0:T(128)} %bitcast.3.core_ref, bf16[640,2048]{1,0:T(8,128)(2,1)} %bitcast.5.refs_1_.mine_ref.theirs_ref.x_ref, bf16[640,2048]{1,0:T(8,128)(2,1)} %bitcast.5.refs_1_.mine_ref.theirs_ref.x_ref), custom_call_target="tpu_custom_call" | custom-call | bytes 5242880 | tf_op jit(solution)/shard_map/pallas_call | solution.py:205
  61.6 7.1 %shard_map.116 = (bf16[768,640]{1,0:T(8,128)(2,1)S(1)}, bf16[3,640,256]{2,1,0:T(8,128)(2,1)S(1)}, bf16[3,640,256]{2,1,0:T(8,128)(2,1)S(1)}, bf16[3,640,256]{2,1,0:T(8,128)(2,1)S(1)}) custom-call(bf16[640,2048]{1,0:T(8,128)(2,1)} %bitcast.5.refs_1_.mine_ref.theirs_ref.x_ref, bf16[1,2048,768]{2,1,0:T(8,128)(2,1)S(1)} %copy-done.2, ...), custom_call_target="tpu_custom_call" | custom-call | flops 4026531840 | bytes 13000000 | tf_op jit(solution)/shard_map/pallas_call | solution.py:187
  74.5 13.2 %all-to-all-done.1 = bf16[16,40,2048]{2,1,0:T(8,128)(2,1)} async-done(((bf16[16,40,2048]{2,1,0:T(8,128)(2,1)}), bf16[16,40,2048]{2,1,0:T(8,128)(2,1)}, u32[]{:S(2)}, u32[]{:S(2)}) %all-to-all-start.1) | async-done | bytes 2621472 | tf_op jit(solution)/shard_map/all_to_all | solution.py:379
  87.6 7.1 %shard_map.118 = (bf16[640,768]{1,0:T(8,128)(2,1)}, bf16[640,768]{1,0:T(8,128)(2,1)}, bf16[640,128]{1,0:T(8,128)(2,1)}) custom-call(s32[1]{0:T(128)} %bitcast.2.me_ref.refs_0_, bf16[640,2048]{1,0:T(8,128)(2,1)} %shard_map.117.dy_ref.a_ref, bf16[3,2048,256]{2,1,0:T(8,128)(2,1)} %shard_map.112.refs_2_.wd_ref, bf16[3,640,256]{2,1,0:T(8,128)(2,1)} %copy-done.9, ...), custom_call_target="tpu_custom_call" | custom-call | flops 2013265920 | bytes 11000000 | tf_op jit(solution)/shard_map/pallas_call | solution.py:251
  96.8 5.0 %shard_map.119 = (bf16[768,1024]{1,0:T(8,128)(2,1)S(1)}, bf16[16,128]{1,0:T(8,128)(2,1)S(1)}) custom-call(bf16[768,640]{1,0:T(8,128)(2,1)S(1)} %copy-done.20, bf16[768,640]{1,0:T(8,128)(2,1)} %collective-permute-done.1.refs_2_.bt_ref, bf16[640,2048]{1,0:T(8,128)(2,1)} %shard_map.117.dy_ref.a_ref, bf16[640,2048]{1,0:T(8,128)(2,1)} %collective-permute-done.4.b_ref, ...), custom_call_target="tpu_custom_call" | custom-call | flops 2013265920 | bytes 6160384 | tf_op jit(solution)/shard_map/pallas_call | solution.py:310
  103.8 4.6 %shard_map.120 = (bf16[1024,768]{1,0:T(8,128)(2,1)S(1)}, bf16[16,128]{1,0:T(8,128)(2,1)S(1)}) custom-call(bf16[1024,640]{1,0:T(8,128)(2,1)S(1)} %copy-done.16, bf16[1024,640]{1,0:T(8,128)(2,1)} %collective-permute-done.refs_1_.bt_ref, bf16[640,768]{1,0:T(8,128)(2,1)S(1)} %copy-done.17, bf16[640,768]{1,0:T(8,128)(2,1)S(1)} %collective-permute-done.3.b_ref, ...), custom_call_target="tpu_custom_call" | custom-call | flops 2013265920 | bytes 6160384 | tf_op jit(solution)/shard_map/pallas_call | solution.py:310
  108.4 2.0 %collective-permute-start.6 = (bf16[128,768]{1,0:T(8,128)(2,1)S(1)}, bf16[128,768]{1,0:T(8,128)(2,1)S(1)}, u32[]{:S(2)}, u32[]{:S(2)}) collective-permute-start(bf16[128,768]{1,0:T(8,128)(2,1)S(1)} %dynamic-slice_bitcast_fusion.1), channel_id=1, source_target_pairs={{0,32},{32,64},{64,96},{96,128},{128,160},{160,192},{192,224},{224... | collective-permute-start | bytes 589832 | tf_op jit(solution)/shard_map/ppermute | solution.py:417
  112.7 4.6 %shard_map.121 = (bf16[1024,768]{1,0:T(8,128)(2,1)S(1)}, bf16[16,128]{1,0:T(8,128)(2,1)S(1)}) custom-call(bf16[1024,640]{1,0:T(8,128)(2,1)S(1)} %copy-done.16, bf16[1024,640]{1,0:T(8,128)(2,1)} %collective-permute-done.refs_1_.bt_ref, bf16[640,768]{1,0:T(8,128)(2,1)S(1)} %copy-done.18, bf16[640,768]{1,0:T(8,128)(2,1)S(1)} %collective-permute-done.2.b_ref, ...), custom_call_target="tpu_custom_call" | custom-call | flops 2013265920 | bytes 6160384 | tf_op jit(solution)/shard_map/pallas_call | solution.py:310
  117.4 3.2 %collective-permute-start.7 = (bf16[128,768]{1,0:T(8,128)(2,1)S(1)}, bf16[128,768]{1,0:T(8,128)(2,1)S(1)}, u32[]{:S(2)}, u32[]{:S(2)}) collective-permute-start(bf16[128,768]{1,0:T(8,128)(2,1)S(1)} %dynamic-slice_bitcast_fusion), channel_id=1, source_target_pairs={{0,32},{32,64},{64,96},{96,128},{128,160},{160,192},{192,224},{224... | collective-permute-start | bytes 589832 | tf_op jit(solution)/shard_map/ppermute | solution.py:417
  121.8 5.4 %shard_map.122 = (bf16[640,2176]{1,0:T(8,128)(2,1)S(1)}, bf16[16,128]{1,0:T(8,128)(2,1)}) custom-call(bf16[640,768]{1,0:T(8,128)(2,1)S(1)} %copy-done.17, bf16[640,768]{1,0:T(8,128)(2,1)S(1)} %copy-done.18, bf16[4,768,512]{2,1,0:T(8,128)(2,1)S(1)} %copy-done.14, bf16[4,768,512]{2,1,0:T(8,128)(2,1)S(1)} %copy-done.1, bf16[640,128]{1,0:T(8,128)(2,1)S(1)} %copy-done.21, ...), custom_call_target="tpu_custom_call" | custom-call | flops 4026531840 | bytes 12000000 | tf_op jit(solution)/shard_map/pallas_call | solution.py:285
  130.5 8.7 %all-to-all-start.2 = ((bf16[16,40,2176]{2,1,0:T(8,128)(2,1)}), bf16[16,40,2176]{2,1,0:T(8,128)(2,1)S(1)}, u32[]{:S(2)}, u32[]{:S(2)}) async-start(bf16[16,40,2176]{2,1,0:T(8,128)(2,1)} %bitcast.95), calls=%async_computation.2 | async-start | bytes 5570560 | tf_op jit(solution)/shard_map/all_to_all | solution.py:379
  143.0 4.4 %collective-permute-done.9 = bf16[128,768]{1,0:T(8,128)(2,1)S(1)} collective-permute-done((bf16[128,768]{1,0:T(8,128)(2,1)S(1)}, bf16[128,768]{1,0:T(8,128)(2,1)S(1)}, u32[]{:S(2)}, u32[]{:S(2)}) %collective-permute-start.9) | collective-permute-done | bytes 196640 | tf_op jit(solution)/shard_map/ppermute | solution.py:417
  150.4 4.9 %collective-permute-done.10 = bf16[128,768]{1,0:T(8,128)(2,1)S(1)} collective-permute-done((bf16[128,768]{1,0:T(8,128)(2,1)S(1)}, bf16[128,768]{1,0:T(8,128)(2,1)S(1)}, u32[]{:S(2)}, u32[]{:S(2)}) %collective-permute-start.10) | collective-permute-done | bytes 196640 | tf_op jit(solution)/shard_map/ppermute | solution.py:417
  159.7 3.6 %collective-permute-done.11 = bf16[128,768]{1,0:T(8,128)(2,1)S(1)} collective-permute-done((bf16[128,768]{1,0:T(8,128)(2,1)S(1)}, bf16[128,768]{1,0:T(8,128)(2,1)S(1)}, u32[]{:S(2)}, u32[]{:S(2)}) %collective-permute-start.11) | collective-permute-done | bytes 196640 | tf_op jit(solution)/shard_map/ppermute | solution.py:417
  167.7 3.6 %collective-permute-done.12 = bf16[128,768]{1,0:T(8,128)(2,1)S(1)} collective-permute-done((bf16[128,768]{1,0:T(8,128)(2,1)S(1)}, bf16[128,768]{1,0:T(8,128)(2,1)S(1)}, u32[]{:S(2)}, u32[]{:S(2)}) %collective-permute-start.12) | collective-permute-done | bytes 196640 | tf_op jit(solution)/shard_map/ppermute | solution.py:417
  176.2 5.1 %collective-permute-done.18 = bf16[128,768]{1,0:T(8,128)(2,1)S(1)} collective-permute-done((bf16[128,768]{1,0:T(8,128)(2,1)S(1)}, bf16[128,768]{1,0:T(8,128)(2,1)S(1)}, u32[]{:S(2)}, u32[]{:S(2)}) %collective-permute-start.18) | collective-permute-done | bytes 196640 | tf_op jit(solution)/shard_map/ppermute | solution.py:417
  183.1 2.4 %shard_map.124 = (bf16[128,2048]{1,0:T(8,128)(2,1)}, bf16[4,128]{1,0:T(4,128)(2,1)}, bf16[16,128]{1,0:T(8,128)(2,1)S(1)}) custom-call(s32[4,128]{1,0:T(4,128)S(1)} %bitcast.123, bf16[4,128]{1,0:T(4,128)(2,1)S(1)} %bitcast.125, bf16[640,2176]{1,0:T(8,128)(2,1)S(1)} %bitcast.96), custom_call_target="tpu_custom_call" | custom-call | flops 335544320 | bytes 2621440 | tf_op jit(solution)/shard_map/pallas_call | solution.py:357
  (124 shorter events, 44.8 us)
Async XLA Ops:
  3.6 42.3 %all-to-all-start = ((bf16[16,40,2048]{2,1,0:T(8,128)(2,1)}), bf16[16,40,2048]{2,1,0:T(8,128)(2,1)}, u32[]{:S(2)}, u32[]{:S(2)}) async-start(bf16[16,40,2048]{2,1,0:T(8,128)(2,1)} %bitcast.127), calls=%async_computation | async-start | bytes 5242880 | tf_op jit(solution)/shard_map/all_to_all | solution.py:379
  45.9 41.7 %all-to-all-start.1 = ((bf16[16,40,2048]{2,1,0:T(8,128)(2,1)}), bf16[16,40,2048]{2,1,0:T(8,128)(2,1)}, u32[]{:S(2)}, u32[]{:S(2)}) async-start(bf16[16,40,2048]{2,1,0:T(8,128)(2,1)} %bitcast.126), calls=%async_computation.1 | async-start | bytes 5242880 | tf_op jit(solution)/shard_map/all_to_all | solution.py:379
  61.6 12.8 %collective-permute-start = (bf16[1024,640]{1,0:T(8,128)(2,1)S(1)}, bf16[1024,640]{1,0:T(8,128)(2,1)}, u32[]{:S(2)}, u32[]{:S(2)}) collective-permute-start(bf16[1024,640]{1,0:T(8,128)(2,1)S(1)} %get-tuple-element.27), channel_id=1, source_target_pairs={{0,16},{16,0},{32,48},{48,32},{64,80},{80,64},{96,112},{112,96},{1... | collective-permute-start | bytes 3932168 | tf_op jit(solution)/shard_map/ppermute | solution.py:402
  87.6 7.8 %collective-permute-start.4 = (bf16[640,2048]{1,0:T(8,128)(2,1)}, bf16[640,2048]{1,0:T(8,128)(2,1)}, u32[]{:S(2)}, u32[]{:S(2)}) collective-permute-start(bf16[640,2048]{1,0:T(8,128)(2,1)} %shard_map.117.dy_ref.a_ref), channel_id=1, source_target_pairs={{0,16},{16,0},{32,48},{48,32},{64,80},{80,64},{96,112},{112,96},{1... | collective-permute-start | bytes 7864328 | tf_op jit(solution)/shard_map/ppermute | solution.py:402
  94.7 9.1 %collective-permute-start.3 = (bf16[640,768]{1,0:T(8,128)(2,1)}, bf16[640,768]{1,0:T(8,128)(2,1)S(1)}, u32[]{:S(2)}, u32[]{:S(2)}) collective-permute-start(bf16[640,768]{1,0:T(8,128)(2,1)} %get-tuple-element.32.a_ref.dg_ref), channel_id=1, source_target_pairs={{0,16},{16,0},{32,48},{48,32},{64,80},{80,64},{96,112},{112,96},{1... | collective-permute-start | bytes 2949128 | tf_op jit(solution)/shard_map/ppermute | solution.py:402
  95.3 17.4 %collective-permute-start.2 = (bf16[640,768]{1,0:T(8,128)(2,1)}, bf16[640,768]{1,0:T(8,128)(2,1)S(1)}, u32[]{:S(2)}, u32[]{:S(2)}) collective-permute-start(bf16[640,768]{1,0:T(8,128)(2,1)} %get-tuple-element.33.a_ref.du_ref), channel_id=1, source_target_pairs={{0,16},{16,0},{32,48},{48,32},{64,80},{80,64},{96,112},{112,96},{1... | collective-permute-start | bytes 2949128 | tf_op jit(solution)/shard_map/ppermute | solution.py:402
  101.8 9.6 %collective-permute-start.5 = (bf16[96,1024]{1,0:T(8,128)(2,1)S(1)}, bf16[96,1024]{1,0:T(8,128)(2,1)S(1)}, u32[]{:S(2)}, u32[]{:S(2)}) collective-permute-start(bf16[96,1024]{1,0:T(8,128)(2,1)S(1)} %dynamic-slice_bitcast_fusion.2), channel_id=1, source_target_pairs={{0,32},{32,64},{64,96},{96,128},{128,160},{160,192},{192,224},{224... | collective-permute-start | bytes 589832 | tf_op jit(solution)/shard_map/ppermute | solution.py:417
  108.4 12.2 %collective-permute-start.6 = (bf16[128,768]{1,0:T(8,128)(2,1)S(1)}, bf16[128,768]{1,0:T(8,128)(2,1)S(1)}, u32[]{:S(2)}, u32[]{:S(2)}) collective-permute-start(bf16[128,768]{1,0:T(8,128)(2,1)S(1)} %dynamic-slice_bitcast_fusion.1), channel_id=1, source_target_pairs={{0,32},{32,64},{64,96},{96,128},{128,160},{160,192},{192,224},{224... | collective-permute-start | bytes 589832 | tf_op jit(solution)/shard_map/ppermute | solution.py:417
  111.5 30.0 %collective-permute-start.20 = (bf16[96,1024]{1,0:T(8,128)(2,1)S(1)}, bf16[96,1024]{1,0:T(8,128)(2,1)}, u32[]{:S(2)}, u32[]{:S(2)}) collective-permute-start(bf16[96,1024]{1,0:T(8,128)(2,1)S(1)} %fusion.20.refs_1_), channel_id=1, source_target_pairs={{0,32},{32,64},{64,96},{96,128},{128,160},{160,192},{192,224},{224... | collective-permute-start | bytes 589832 | tf_op jit(solution)/shard_map/ppermute | solution.py:417
  117.4 11.3 %collective-permute-start.7 = (bf16[128,768]{1,0:T(8,128)(2,1)S(1)}, bf16[128,768]{1,0:T(8,128)(2,1)S(1)}, u32[]{:S(2)}, u32[]{:S(2)}) collective-permute-start(bf16[128,768]{1,0:T(8,128)(2,1)S(1)} %dynamic-slice_bitcast_fusion), channel_id=1, source_target_pairs={{0,32},{32,64},{64,96},{96,128},{128,160},{160,192},{192,224},{224... | collective-permute-start | bytes 589832 | tf_op jit(solution)/shard_map/ppermute | solution.py:417
  120.7 18.6 %collective-permute-start.8 = (bf16[128,768]{1,0:T(8,128)(2,1)S(1)}, bf16[128,768]{1,0:T(8,128)(2,1)}, u32[]{:S(2)}, u32[]{:S(2)}) collective-permute-start(bf16[128,768]{1,0:T(8,128)(2,1)S(1)} %fusion.19.refs_1_), channel_id=1, source_target_pairs={{0,32},{32,64},{64,96},{96,128},{128,160},{160,192},{192,224},{224... | collective-permute-start | bytes 589832 | tf_op jit(solution)/shard_map/ppermute | solution.py:417
  129.4 19.1 %collective-permute-start.14 = (bf16[128,768]{1,0:T(8,128)(2,1)S(1)}, bf16[128,768]{1,0:T(8,128)(2,1)}, u32[]{:S(2)}, u32[]{:S(2)}) collective-permute-start(bf16[128,768]{1,0:T(8,128)(2,1)S(1)} %fusion.18), channel_id=1, source_target_pairs={{0,32},{32,64},{64,96},{96,128},{128,160},{160,192},{192,224},{224... | collective-permute-start | bytes 589832 | tf_op jit(solution)/shard_map/ppermute | solution.py:417
  130.5 52.7 %all-to-all-start.2 = ((bf16[16,40,2176]{2,1,0:T(8,128)(2,1)}), bf16[16,40,2176]{2,1,0:T(8,128)(2,1)S(1)}, u32[]{:S(2)}, u32[]{:S(2)}) async-start(bf16[16,40,2176]{2,1,0:T(8,128)(2,1)} %bitcast.95), calls=%async_computation.2 | async-start | bytes 5570560 | tf_op jit(solution)/shard_map/all_to_all | solution.py:379
  140.4 7.0 %collective-permute-start.9 = (bf16[128,768]{1,0:T(8,128)(2,1)S(1)}, bf16[128,768]{1,0:T(8,128)(2,1)S(1)}, u32[]{:S(2)}, u32[]{:S(2)}) collective-permute-start(bf16[128,768]{1,0:T(8,128)(2,1)S(1)} %fusion.17), channel_id=1, source_target_pairs={{0,32},{32,64},{64,96},{96,128},{128,160},{160,192},{192,224},{224... | collective-permute-start | bytes 589832 | tf_op jit(solution)/shard_map/ppermute | solution.py:417
  142.5 7.2 %collective-permute-start.21 = (bf16[96,1024]{1,0:T(8,128)(2,1)S(1)}, bf16[96,1024]{1,0:T(8,128)(2,1)S(1)}, u32[]{:S(2)}, u32[]{:S(2)}) collective-permute-start(bf16[96,1024]{1,0:T(8,128)(2,1)S(1)} %fusion.5), channel_id=1, source_target_pairs={{0,32},{32,64},{64,96},{96,128},{128,160},{160,192},{192,224},{224... | collective-permute-start | bytes 589832 | tf_op jit(solution)/shard_map/ppermute | solution.py:417
  149.6 7.9 %collective-permute-start.15 = (bf16[128,768]{1,0:T(8,128)(2,1)S(1)}, bf16[128,768]{1,0:T(8,128)(2,1)S(1)}, u32[]{:S(2)}, u32[]{:S(2)}) collective-permute-start(bf16[128,768]{1,0:T(8,128)(2,1)S(1)} %fusion.11), channel_id=1, source_target_pairs={{0,32},{32,64},{64,96},{96,128},{128,160},{160,192},{192,224},{224... | collective-permute-start | bytes 589832 | tf_op jit(solution)/shard_map/ppermute | solution.py:417
  149.8 9.8 %collective-permute-start.22 = (bf16[96,1024]{1,0:T(8,128)(2,1)S(1)}, bf16[96,1024]{1,0:T(8,128)(2,1)S(1)}, u32[]{:S(2)}, u32[]{:S(2)}) collective-permute-start(bf16[96,1024]{1,0:T(8,128)(2,1)S(1)} %fusion.4), channel_id=1, source_target_pairs={{0,32},{32,64},{64,96},{96,128},{128,160},{160,192},{192,224},{224... | collective-permute-start | bytes 589832 | tf_op jit(solution)/shard_map/ppermute | solution.py:417
  157.5 7.9 %collective-permute-start.16 = (bf16[128,768]{1,0:T(8,128)(2,1)S(1)}, bf16[128,768]{1,0:T(8,128)(2,1)S(1)}, u32[]{:S(2)}, u32[]{:S(2)}) collective-permute-start(bf16[128,768]{1,0:T(8,128)(2,1)S(1)} %fusion.10), channel_id=1, source_target_pairs={{0,32},{32,64},{64,96},{96,128},{128,160},{160,192},{192,224},{224... | collective-permute-start | bytes 589832 | tf_op jit(solution)/shard_map/ppermute | solution.py:417
  159.6 7.9 %collective-permute-start.23 = (bf16[96,1024]{1,0:T(8,128)(2,1)S(1)}, bf16[96,1024]{1,0:T(8,128)(2,1)S(1)}, u32[]{:S(2)}, u32[]{:S(2)}) collective-permute-start(bf16[96,1024]{1,0:T(8,128)(2,1)S(1)} %fusion.3), channel_id=1, source_target_pairs={{0,32},{32,64},{64,96},{96,128},{128,160},{160,192},{192,224},{224... | collective-permute-start | bytes 589832 | tf_op jit(solution)/shard_map/ppermute | solution.py:417
  165.5 7.9 %collective-permute-start.17 = (bf16[128,768]{1,0:T(8,128)(2,1)S(1)}, bf16[128,768]{1,0:T(8,128)(2,1)S(1)}, u32[]{:S(2)}, u32[]{:S(2)}) collective-permute-start(bf16[128,768]{1,0:T(8,128)(2,1)S(1)} %fusion.9), channel_id=1, source_target_pairs={{0,32},{32,64},{64,96},{96,128},{128,160},{160,192},{192,224},{224... | collective-permute-start | bytes 589832 | tf_op jit(solution)/shard_map/ppermute | solution.py:417
  167.6 7.9 %collective-permute-start.24 = (bf16[96,1024]{1,0:T(8,128)(2,1)S(1)}, bf16[96,1024]{1,0:T(8,128)(2,1)S(1)}, u32[]{:S(2)}, u32[]{:S(2)}) collective-permute-start(bf16[96,1024]{1,0:T(8,128)(2,1)S(1)} %fusion.2), channel_id=1, source_target_pairs={{0,32},{32,64},{64,96},{96,128},{128,160},{160,192},{192,224},{224... | collective-permute-start | bytes 589832 | tf_op jit(solution)/shard_map/ppermute | solution.py:417
  172.2 9.2 %collective-permute-start.13 = (bf16[128,768]{1,0:T(8,128)(2,1)S(1)}, bf16[128,768]{1,0:T(8,128)(2,1)S(1)}, u32[]{:S(2)}, u32[]{:S(2)}) collective-permute-start(bf16[128,768]{1,0:T(8,128)(2,1)S(1)} %fusion.13), channel_id=1, source_target_pairs={{0,32},{32,64},{64,96},{96,128},{128,160},{160,192},{192,224},{224... | collective-permute-start | bytes 589832 | tf_op jit(solution)/shard_map/ppermute | solution.py:417
  173.4 7.9 %collective-permute-start.18 = (bf16[128,768]{1,0:T(8,128)(2,1)S(1)}, bf16[128,768]{1,0:T(8,128)(2,1)S(1)}, u32[]{:S(2)}, u32[]{:S(2)}) collective-permute-start(bf16[128,768]{1,0:T(8,128)(2,1)S(1)} %fusion.8), channel_id=1, source_target_pairs={{0,32},{32,64},{64,96},{96,128},{128,160},{160,192},{192,224},{224... | collective-permute-start | bytes 589832 | tf_op jit(solution)/shard_map/ppermute | solution.py:417
  176.2 9.3 %collective-permute-start.25 = (bf16[96,1024]{1,0:T(8,128)(2,1)}, bf16[96,1024]{1,0:T(8,128)(2,1)S(1)}, u32[]{:S(2)}, u32[]{:S(2)}) collective-permute-start(bf16[96,1024]{1,0:T(8,128)(2,1)} %fusion.1), channel_id=1, source_target_pairs={{0,32},{32,64},{64,96},{96,128},{128,160},{160,192},{192,224},{224... | collective-permute-start | bytes 589832 | tf_op jit(solution)/shard_map/ppermute | solution.py:417
  (28 other events, 208.6 us)
